TPU v7x, 32 devices: a whole 2x2x4 slice. The times are simulated.
32 devices in a mesh: group: 2 (over y), expert: 4 (over z), dp: 4 (over x, core).
Axes of the slice: x: 2, y: 2, z: 4, core: 2. Of those that a mesh axis runs over, the one named last changes fastest.
Arguments:
- tokens: bfloat16 [128, 4096], P(('group', 'expert', 'dp')), parts along dimension 0, may hold values from -6 to 6
- expert_ids: int32 [128, 8], P(('group', 'expert', 'dp')), parts along dimension 0, may hold values from 0 to 15, all different within a row; in each aligned block of 4 rows (0 to 3, 4 to 7, ...) at most 3 rows name the same one
- route_weight: float32 [128, 8], P(('group', 'expert', 'dp')), parts along dimension 0, may hold values from 0.1 to 1
- tenant_ids: int32 [128], P(('group', 'expert', 'dp')), parts along dimension 0, may hold values from 0 to 7
- gate_weight: bfloat16 [16, 4096, 1536], P('expert', None, 'dp'), may hold values from -0.09375 to 0.09375
- up_weight: bfloat16 [16, 4096, 1536], P('expert', None, 'dp'), may hold values from -0.09375 to 0.09375
- down_weight: bfloat16 [16, 1536, 4096], P('expert', None, 'dp'), may hold values from -0.15625 to 0.15625
- pool_shrink: bfloat16 [16, 8, 16, 1536], P('expert', 'dp'), may hold values from -0.15625 to 0.15625
- adapter_pool_expand: bfloat16 [16, 8, 16, 4096], P('expert', 'dp'), may hold values from -1.5 to 1.5
- page_owner: int32 [8, 16], replicated, may hold values from 0 to 3, as said below
- page_slot: int32 [8, 16], replicated, may hold values from 0 to 1, as said below
Outputs:
- mixed_out: bfloat16 [128, 4096], P(('group', 'expert', 'dp')), parts along dimension 0
There are 2 independent parts, one for each index of `group`. A program takes and returns all parts, laid end to end along the dimension named above; an argument that names none is the same for every part. Nothing has to cross between parts.
Inputs may be any that keep to these rules, and one draw needn't show every extreme that they name: `expert_ids`: each row names 8 different experts; in the rows of one device no expert is named more than 3 times, a bound that some block reaches. For each expert, the pairs (page_owner, page_slot) of all tenants are all different. `page_slot`: see page_owner.
All inputs are finite; a program needn't handle non-finite values.
Results may differ from a plain program's by a relative error of at most 0.0062.
Values may be sent and summed in bfloat16 or wider, within the bound.
No kernel may reach another device: no remote copies, remote signals or barrier semaphores. Data moves between devices by JAX's collectives and lax.ppermute only.
A program may use at most 128 MiB of HBM per device.

v0:
```python
import jax
import jax.numpy as jnp
from jax import lax
from jax.sharding import PartitionSpec as P

TOP = 8
EXPERTS = 16
SLOTS = 2
CAP = 3


def slot_targets(route_ids, local_count, expert_count, capacity):
    source_count = route_ids.shape[0]
    one_hot = (route_ids[:, :, None] == jnp.arange(EXPERTS, dtype=jnp.int32)).astype(jnp.int32)
    earlier = jnp.sum((jnp.cumsum(one_hot, axis=1) - one_hot) * one_hot, axis=2)
    destination = route_ids // local_count
    lane_index = route_ids % local_count
    source_index = jnp.arange(source_count, dtype=jnp.int32)[:, None]
    targets = (
        (lane_index * expert_count + destination) * source_count + source_index
    ) * capacity + earlier
    return targets.reshape(-1)


def build_outgoing(rows_all, tenants_all, route_ids, local_count, expert_count, capacity):
    source_count = route_ids.shape[0]
    targets = slot_targets(route_ids, local_count, expert_count, capacity)
    slot_count = local_count * expert_count * source_count * capacity
    assignee = (
        jnp.full((slot_count,), -1, jnp.int32)
        .at[targets]
        .set(jnp.arange(targets.shape[0], dtype=jnp.int32))
    )
    occupied = assignee >= 0
    row_index = jnp.maximum(assignee, 0) // TOP
    outgoing = jnp.where(occupied[:, None], rows_all[row_index], jnp.zeros((), rows_all.dtype))
    tenants = jnp.where(occupied, tenants_all[row_index], -1)
    model_width = rows_all.shape[1]
    return (
        outgoing.reshape(local_count, expert_count, source_count, capacity, model_width),
        tenants.reshape(local_count, expert_count, source_count, capacity),
    )


def shards(
    tokens,
    expert_ids,
    route_weight,
    tenant_ids,
    gate_weight,
    up_weight,
    down_weight,
    pool_shrink,
    adapter_pool_expand,
    page_owner,
    page_slot,
):
    expert_count = lax.axis_size("expert")
    member_count = lax.axis_size("dp")
    local_count = gate_weight.shape[0]
    capacity = CAP
    model_width = tokens.shape[1]
    part_cols = down_weight.shape[2]
    outgoing, out_tenants = build_outgoing(
        tokens, tenant_ids, expert_ids.reshape(1, -1), local_count, expert_count, capacity
    )
    moved_rows, moved_tenants = (
        lax.all_to_all(outgoing, "expert", split_axis=1, concat_axis=1, tiled=True),
        lax.all_to_all(out_tenants, "expert", split_axis=1, concat_axis=1, tiled=True),
    )
    arrived, arrived_tenants = (
        lax.all_gather(moved_rows, "dp", axis=2, tiled=True),
        lax.all_gather(moved_tenants, "dp", axis=2, tiled=True),
    )
    expert_rows = arrived.reshape(local_count, -1, model_width)
    row_tenants = arrived_tenants.reshape(local_count, -1)
    gate_proj = jnp.einsum(
        "lrd,ldf->lrf", expert_rows, gate_weight, preferred_element_type=jnp.float32
    )
    up_proj = jnp.einsum("lrd,ldf->lrf", expert_rows, up_weight, preferred_element_type=jnp.float32)
    hidden = (jax.nn.silu(gate_proj) * up_proj).astype(jnp.bfloat16)
    shrink_source, expand_panels = (
        lax.all_gather(pool_shrink, "dp", axis=1, tiled=True),
        lax.all_gather(adapter_pool_expand, "dp", axis=1, tiled=True),
    )
    expand_cols = lax.dynamic_slice_in_dim(
        expand_panels, lax.axis_index("dp") * part_cols, part_cols, 3
    )
    tenant_total = pool_shrink.shape[1] * member_count
    first_expert = lax.axis_index("expert") * local_count
    owner_cols = lax.dynamic_slice_in_dim(page_owner, first_expert, local_count, 1)
    slot_cols = lax.dynamic_slice_in_dim(page_slot, first_expert, local_count, 1)
    global_slot = jnp.transpose(owner_cols * SLOTS + slot_cols)
    tenant_hot = (row_tenants[:, :, None] == jnp.arange(tenant_total, dtype=jnp.int32)).astype(
        jnp.int32
    )
    row_slot = jnp.sum(tenant_hot * global_slot[:, None, :], axis=2)
    row_slot = jnp.where(row_tenants >= 0, row_slot, -1)
    selector = (row_slot[:, :, None] == jnp.arange(tenant_total, dtype=jnp.int32)).astype(
        jnp.bfloat16
    )
    shard_piece = lax.all_gather(hidden, "dp", axis=2, tiled=True)
    base_portion = jnp.einsum(
        "lrf,lfd->lrd", shard_piece, down_weight, preferred_element_type=jnp.float32
    )
    shrink_part = jnp.einsum(
        "lrf,ltkf->lrtk", shard_piece, shrink_source, preferred_element_type=jnp.float32
    )
    shrink = shrink_part.astype(jnp.bfloat16)
    masked_rows = shrink * selector[:, :, :, None]
    adapter_update = jnp.einsum(
        "lrtk,ltkd->lrd", masked_rows, expand_cols, preferred_element_type=jnp.float32
    )
    final_output = (
        (base_portion + adapter_update)
        .astype(jnp.bfloat16)
        .reshape(local_count, expert_count, -1, capacity, part_cols)
    )
    returned = lax.all_to_all(
        lax.all_to_all(final_output, "expert", split_axis=1, concat_axis=1, tiled=True),
        "dp",
        split_axis=2,
        concat_axis=4,
        tiled=True,
    )
    returned_flat = returned.reshape(-1, model_width)
    own_targets = slot_targets(expert_ids.reshape(1, -1), local_count, expert_count, capacity)
    picked = (
        returned_flat[own_targets].astype(jnp.float32).reshape(tokens.shape[0], TOP, model_width)
    )
    mixed_out = jnp.sum(route_weight[:, :, None] * picked, axis=1)
    return mixed_out.astype(jnp.bfloat16)


def solution(mesh):
    in_specs = (
        P(("group", "expert", "dp"), None),
        P(("group", "expert", "dp"), None),
        P(("group", "expert", "dp"), None),
        P(("group", "expert", "dp")),
        P("expert", None, "dp"),
        P("expert", None, "dp"),
        P("expert", None, "dp"),
        P("expert", "dp", None, None),
        P("expert", "dp", None, None),
        P(),
        P(),
    )
    out_specs = P(("group", "expert", "dp"), None)
    return jax.shard_map(shards, mesh=mesh, in_specs=in_specs, out_specs=out_specs, check_vma=False)
```

profile of v0, /device:TPU:0, one launch (start us, length us, event | category | flops | bytes accessed | tf_op | source)
XLA Modules:
  0.0 156.7 jit_solution(629823180752504041)
XLA Ops:
  6.5 0.8 eq.67
  7.3 0.8 reshape.334
  8.4 1.5 fusion.26
  10.6 2.5 %fusion.20 = (s32[48]{0:T(128)S(1)}, s32[48]{0:T(128)S(1)}) fusion(s32[]{:T(128)} %bitcast.5, s32[]{:T(128)} %bitcast.6, s32[]{:T(128)} %bitcast.7, s32[]{:T(128)} %bitcast.8, s32[48]{0:T(128)S(1)} %scatter_custom_fusion), kind=kLoop, calls=%fused_computation.43 | loop fusion | flops 960 | bytes 592 | tf_op jit(solution)/shard_map/jit(_where)/select_n | solution.py:37
  13.1 0.8 gather_fusion
  14.9 17.8 %all_to_all.30 = bf16[4,4,1,3,4096]{4,0,3,2,1:T(4,128)(2,1)S(1)} all-to-all(bf16[4,4,1,3,4096]{4,0,3,2,1:T(4,128)(2,1)S(1)} %copy.34), channel_id=1, replica_groups=mesh['group'=2,'expert'=4,'dp'=4] {'expert'}, dimensions={1} | all-to-all | bytes 786432 | tf_op jit(solution)/shard_map/all_to_all | solution.py:68
  32.7 1.0 copy.35
  35.4 0.7 copy.39
  36.1 3.2 %all-to-all-start.1 = ((s32[4,4,1,3]{0,2,3,1:T(1,128)}), s32[4,4,1,3]{0,2,3,1:T(1,128)S(1)}, u32[]{:S(2)}, u32[]{:S(2)}) async-start(s32[4,4,1,3]{0,2,3,1:T(1,128)} %copy.39), calls=%async_computation.1 | async-start | bytes 12288 | tf_op jit(solution)/shard_map/all_to_all | solution.py:69
  39.5 5.4 %all-to-all-done.1 = s32[4,4,1,3]{0,2,3,1:T(1,128)S(1)} async-done(((s32[4,4,1,3]{0,2,3,1:T(1,128)}), s32[4,4,1,3]{0,2,3,1:T(1,128)S(1)}, u32[]{:S(2)}, u32[]{:S(2)}) %all-to-all-start.1) | async-done | bytes 224 | tf_op jit(solution)/shard_map/all_to_all | solution.py:69
  45.0 5.3 %all_gather.18 = s32[4,4,4,3]{1,0,3,2:T(4,128)S(1)} all-gather(s32[4,4,1,3]{1,0,3,2:T(4,128)S(1)} %copy.40), channel_id=1, replica_groups=mesh['group'=2,'expert'=4,'dp'=4] {'dp'}, dimensions={2}, use_global_device_ids=true | all-gather | bytes 960 | tf_op jit(solution)/shard_map/all_gather | solution.py:73
  50.7 2.2 %all-gather.4.cloned.1.call-done = bf16[4,4,4,3,4096]{4,1,3,0,2:T(4,128)(2,1)} async-done(((bf16[4,4,1,3,4096]{4,1,3,0,2:T(4,128)(2,1)}), bf16[4,4,4,3,4096]{4,1,3,0,2:T(4,128)(2,1)}) %all-gather.4.cloned.1.call-update) | async-done | bytes 1572880 | tf_op jit(solution)/shard_map/all_gather | solution.py:72
  52.8 2.6 %copy.36 = bf16[4,4,4,3,4096]{4,0,3,2,1:T(4,128)(2,1)S(1)} copy(bf16[4,4,4,3,4096]{4,1,3,0,2:T(4,128)(2,1)} %all-gather.4.cloned.1.call-done) | data formatting | bytes 3145728 | tf_op jit(solution)/shard_map/all_gather | solution.py:72
  55.5 7.7 %fusion.2 = f32[4,48,384]{2,1,0:T(8,128)S(1)} fusion(bf16[4,4096,384]{2,1,0:T(8,128)(2,1)} %param.15, bf16[4,48,4096]{2,0,1:T(4,128)(2,1)S(1)} %bitcast.39), kind=kOutput, calls=%fused_computation.5 | convolution fusion | flops 603979776 | bytes 14450688 | tf_op jit(solution)/shard_map/lrd,ldf->lrf/dot_general | solution.py:77
  63.2 7.8 %fusion.8 = bf16[4,48,384]{2,1,0:T(8,128)(2,1)S(1)} fusion(bf16[4,4096,384]{2,1,0:T(8,128)(2,1)} %param.16, bf16[4,48,4096]{2,0,1:T(4,128)(2,1)S(1)} %bitcast.40, f32[4,48,384]{2,1,0:T(8,128)S(1)} %fusion.2), kind=kOutput, calls=%fused_computation.11 | convolution fusion | flops 604422144 | bytes 14598144 | tf_op jit(solution)/shard_map/lrd,ldf->lrf/dot_general | solution.py:80
  70.9 7.7 %all_gather.16 = bf16[4,48,1536]{2,1,0:T(8,128)(2,1)S(1)} all-gather(bf16[4,48,384]{2,1,0:T(8,128)(2,1)S(1)} %fusion.8), channel_id=1, replica_groups=mesh['group'=2,'expert'=4,'dp'=4] {'dp'}, dimensions={2}, use_global_device_ids=true | all-gather | bytes 737280 | tf_op jit(solution)/shard_map/all_gather | solution.py:102
  78.7 31.5 %all-gather.8.cloned.1.call-done = bf16[4,8,16,4096]{3,2,1,0:T(8,128)(2,1)} async-done(((bf16[4,2,16,4096]{3,2,1,0:T(8,128)(2,1)}), bf16[4,8,16,4096]{3,2,1,0:T(8,128)(2,1)}) %all-gather.8.cloned.1.call-update) | async-done | bytes 4194320 | tf_op jit(solution)/shard_map/all_gather | solution.py:84
  110.2 2.5 %convolution_bitcast_fusion = f32[4,48,1024]{2,1,0:T(8,128)S(1)} fusion(bf16[4,8,16,1536]{3,2,1,0:T(8,128)(2,1)} %all-gather.6.cloned.1.call-done, bf16[4,8,16,4096]{3,2,1,0:T(8,128)(2,1)} %all-gather.8.cloned.1.call-done, s32[]{:T(128)S(6)} %select_n.94, bf16[4,48,1536]{2,1,0:T(8,128)(2,1)S(1)} %all_gather.16, bf16[4,48,8]{1,2,0:T(8,128)(2,1)S(1)} %fusion.18), kind=kOutput, calls=%fused_computation.7 | convolution fusion | flops 125878272 | bytes 4000772 | tf_op jit(solution)/shard_map/lrtk,ltkd->lrd/dot_general | solution.py:111
  112.7 6.9 %fusion.4 = bf16[4,48,1024]{2,1,0:T(8,128)(2,1)S(1)} fusion(f32[4,48,1024]{2,1,0:T(8,128)S(1)} %convolution_bitcast_fusion, bf16[4,48,1536]{2,1,0:T(8,128)(2,1)S(1)} %all_gather.16, bf16[4,1536,1024]{2,1,0:T(8,128)(2,1)} %param.17), kind=kOutput, calls=%fused_computation.9 | convolution fusion | flops 604372992 | bytes 14352384 | tf_op jit(solution)/shard_map/lrf,lfd->lrd/dot_general | solution.py:103
  119.9 16.5 %all_to_all.31 = bf16[4,4,4,3,1024]{4,0,3,2,1:T(4,128)(2,1)S(1)} all-to-all(bf16[4,4,4,3,1024]{4,0,3,2,1:T(4,128)(2,1)S(1)} %bitcast.42), channel_id=1, replica_groups=mesh['group'=2,'expert'=4,'dp'=4] {'expert'}, dimensions={1} | all-to-all | bytes 786432 | tf_op jit(solution)/shard_map/all_to_all | solution.py:120
  136.4 0.9 copy.44
  137.3 3.5 %all-to-all-start.3 = ((bf16[4,4,4,3,1024]{4,0,3,1,2:T(4,128)(2,1)}), bf16[4,4,4,3,1024]{4,0,3,1,2:T(4,128)(2,1)S(1)}, u32[]{:S(2)}, u32[]{:S(2)}) async-start(bf16[4,4,4,3,1024]{4,0,3,1,2:T(4,128)(2,1)} %copy.44), calls=%async_computation.3 | async-start | bytes 786432 | tf_op jit(solution)/shard_map/all_to_all | solution.py:119
  140.7 7.4 %all-to-all-done.3 = bf16[4,4,4,3,1024]{4,0,3,1,2:T(4,128)(2,1)S(1)} async-done(((bf16[4,4,4,3,1024]{4,0,3,1,2:T(4,128)(2,1)}), bf16[4,4,4,3,1024]{4,0,3,1,2:T(4,128)(2,1)S(1)}, u32[]{:S(2)}, u32[]{:S(2)}) %all-to-all-start.3) | async-done | bytes 393248 | tf_op jit(solution)/shard_map/all_to_all | solution.py:119
  149.3 0.9 fusion.15
  (41 shorter events, 5.7 us)
Async XLA Ops:
  6.5 6.5 %copy-start = (bf16[4,4096]{1,0:T(4,128)(2,1)S(1)}, bf16[4,4096]{1,0:T(4,128)(2,1)}, u32[]{:S(2)}) copy-start(bf16[4,4096]{1,0:T(4,128)(2,1)} %param.11) | copy-start | bytes 98308
  6.5 46.3 %all-gather.4.cloned.1.call-start = ((), (), s32[]{:S(2)}) async-start(), calls=%async_computation.4 | async-start | bytes 1966080 | tf_op jit(solution)/shard_map/all_gather | solution.py:72
  13.1 26.3 %copy-start.1 = (s32[8,16]{1,0:T(8,128)S(1)}, s32[8,16]{1,0:T(8,128)}, u32[]{:S(2)}) copy-start(s32[8,16]{1,0:T(8,128)} %param.21) | copy-start | bytes 1540
  13.1 26.3 %copy-start.2 = (s32[8,16]{1,0:T(8,128)S(1)}, s32[8,16]{1,0:T(8,128)}, u32[]{:S(2)}) copy-start(s32[8,16]{1,0:T(8,128)} %param.20) | copy-start | bytes 1540
  33.8 44.9 %all-gather.6.cloned.1.call-start = ((), (), s32[]{:S(2)}) async-start(), calls=%async_computation.5 | async-start | bytes 1966080 | tf_op jit(solution)/shard_map/all_gather | solution.py:83
  34.5 75.6 %all-gather.8.cloned.1.call-start = ((), (), s32[]{:S(2)}) async-start(), calls=%async_computation.6 | async-start | bytes 5242880 | tf_op jit(solution)/shard_map/all_gather | solution.py:84
  36.1 8.8 %all-to-all-start.1 = ((s32[4,4,1,3]{0,2,3,1:T(1,128)}), s32[4,4,1,3]{0,2,3,1:T(1,128)S(1)}, u32[]{:S(2)}, u32[]{:S(2)}) async-start(s32[4,4,1,3]{0,2,3,1:T(1,128)} %copy.39), calls=%async_computation.1 | async-start | bytes 12288 | tf_op jit(solution)/shard_map/all_to_all | solution.py:69
  119.5 29.7 %copy-start.3 = (f32[4,8]{1,0:T(4,128)S(1)}, f32[4,8]{1,0:T(4,128)}, u32[]{:S(2)}) copy-start(f32[4,8]{1,0:T(4,128)} %param.13) | copy-start | bytes 388
  137.3 10.9 %all-to-all-start.3 = ((bf16[4,4,4,3,1024]{4,0,3,1,2:T(4,128)(2,1)}), bf16[4,4,4,3,1024]{4,0,3,1,2:T(4,128)(2,1)S(1)}, u32[]{:S(2)}, u32[]{:S(2)}) async-start(bf16[4,4,4,3,1024]{4,0,3,1,2:T(4,128)(2,1)} %copy.44), calls=%async_computation.3 | async-start | bytes 786432 | tf_op jit(solution)/shard_map/all_to_all | solution.py:119
Sparse Core Ops, SparseCore 0:
  33.9 18.8 all-gather.3
  54.4 19.6 all-gather.5
  75.7 34.4 all-gather.7
where the time goes:
time: 157 us
  waiting for transfers between devices  47.8 us (30%)
  blocking collectives  47.3 us (30%)
  matrix products  24.8 us (16%)
  between operations  13.3 us (8%)
  local copies, waits for them, and re-layouts  12.5 us (8%)
  starting transfers between devices  6.79 us (4%)
  other arithmetic  4.19 us (3%)
    all_gather x1, waiting for transfers between devices, shards(): lax.all_gather(adapter_pool_expand, 'dp', axis=1, tiled=True)  31.5 us
    all_to_all x1, blocking collectives, shards(): lax.all_to_all(outgoing, 'expert', split_axis=1, concat_axis=1, tiled=True)  17.8 us
    all_to_all x1, blocking collectives, shards(): lax.all_to_all(final_output, 'expert', split_axis=1, concat_axis=1, tiled...  16.5 us
    dot_general x1, matrix products, shards(): jnp.einsum('lrd,ldf->lrf', expert_rows, up_weight, preferred_element_type...  7.77 us
    all_gather x1, blocking collectives, shards(): shard_piece = lax.all_gather(hidden, 'dp', axis=2, tiled=True)  7.73 us
    dot_general x1, matrix products, shards(): jnp.einsum('lrd,ldf->lrf', expert_rows, gate_weight, preferred_element_ty...  7.69 us
    all_to_all x1, waiting for transfers between devices, shards(): lax.all_to_all(lax.all_to_all(final_output, 'expert', split_axis=1, conca...  7.39 us
    dot_general x1, matrix products, shards(): jnp.einsum('lrf,lfd->lrd', shard_piece, down_weight, preferred_element_ty...  6.87 us
  transfers between devices with their start and end apart: 5, of which 4 were waited for; matrix products, arithmetic and copies ran while one was open for 12% of the time, Pallas kernels for 0%

commit v1 on v0

v1 whole, which is shorter than its diff:
```python
import functools

import jax
import jax.numpy as jnp
from jax import lax
from jax.experimental import pallas as pl
from jax.experimental.pallas import tpu as pltpu
from jax.sharding import PartitionSpec as P

TOP = 8
EXPERTS = 16
SLOTS = 2
LANES = 128
BF = jnp.bfloat16
F32 = jnp.float32

VM = pl.BlockSpec(memory_space=pltpu.VMEM)
SM = pl.BlockSpec(memory_space=pltpu.SMEM)
HB = pl.BlockSpec(memory_space=pltpu.HBM)
ANY = pl.BlockSpec(memory_space=pl.ANY)


def in_vmem(x):
    return pltpu.with_memory_space_constraint(x, pltpu.VMEM)


def in_hbm(x):
    return pltpu.with_memory_space_constraint(x, pltpu.HBM)


def call(body, out_shape, operands, specs, limit, bytes_moved=0, scratch=()):
    return pl.pallas_call(
        body,
        out_shape=out_shape,
        in_specs=specs,
        out_specs=jax.tree.map(lambda _: VM, out_shape),
        scratch_shapes=scratch,
        cost_estimate=pl.CostEstimate(flops=0, bytes_accessed=bytes_moved, transcendentals=0),
        compiler_params=pltpu.CompilerParams(vmem_limit_bytes=limit),
    )(*operands)


def size_of(*arrays):
    total = 0
    for a in arrays:
        n = a.dtype.itemsize
        for s in a.shape[:-1]:
            n *= s
        total += n * (-(-a.shape[-1] // LANES) * LANES)
    return total


def prepare(*refs):
    y, held, sems = refs[6], refs[7:13], refs[13]
    copies = [pltpu.make_async_copy(refs[i], held[i], sems.at[i]) for i in range(6)]
    for c in copies:
        c.start()
    for c in copies:
        c.wait()
    ten, tok, ids, rw, owner, slot = held
    rows, width = tok.shape
    y[:, :width] = tok[...]
    lane = lax.broadcasted_iota(jnp.int32, (rows, LANES), 1)
    expert, piece = lane % EXPERTS, lane // EXPERTS
    w = jnp.zeros((rows, LANES), F32)
    for k in range(TOP):
        w += jnp.where(ids[:, k : k + 1] == expert, rw[:, k : k + 1], 0.0)
    high = w.astype(BF).astype(F32)
    mid = (w - high).astype(BF).astype(F32)
    low = w - high - mid
    y[:, width : width + LANES] = jnp.where(
        piece == 0, high, jnp.where(piece == 1, mid, jnp.where(piece == 2, low, 0.0))
    ).astype(BF)
    y[:, width + LANES :] = jnp.zeros((rows, LANES), BF)
    pages = [
        owner[pl.ds(ten[r], 1), :] * SLOTS + slot[pl.ds(ten[r], 1), :] for r in range(rows)
    ]
    y[:, width + LANES : width + LANES + EXPERTS] = (
        jnp.concatenate(pages, axis=0).astype(F32).astype(BF)
    )


def fetch(experts, dep, *refs):
    del dep
    count = len(experts)
    sems = refs[-1]
    copies = []
    for i, pick in enumerate(experts):
        src, dst = refs[i], refs[count + i]
        for j, e in enumerate(pick):
            copies.append(pltpu.make_async_copy(src.at[e], dst.at[j], sems.at[len(copies)]))
    for c in copies:
        c.start()
    for c in copies:
        c.wait()


def prefetch(dep, arrays, picks):
    shapes = [pltpu.VMEM((len(p),) + a.shape[1:], a.dtype) for a, p in zip(arrays, picks)]
    moved = sum(size_of(a) * len(p) // a.shape[0] for a, p in zip(arrays, picks))
    out = pl.pallas_call(
        functools.partial(fetch, picks),
        out_shape=shapes,
        in_specs=[ANY] + [HB] * len(arrays),
        out_specs=[VM] * len(arrays),
        scratch_shapes=[pltpu.SemaphoreType.DMA((sum(len(p) for p in picks),))],
        cost_estimate=pl.CostEstimate(flops=0, bytes_accessed=2 * moved, transcendentals=0),
        compiler_params=pltpu.CompilerParams(vmem_limit_bytes=1 << 20),
    )(dep, *[in_hbm(a) for a in arrays])
    return out


def join(count, *refs):
    out = refs[-1]
    out[...] = jnp.concatenate([r[...].astype(F32) for r in refs[:count]], axis=0).astype(BF)


def up_kernel(count, parts, *refs):
    x_refs, refs = refs[:count], refs[count:]
    held, refs = refs[: len(parts)], refs[len(parts) :]
    gate_hbm, up_hbm, h, slots, late, sems = refs
    experts, width = gate_hbm.shape[0], gate_hbm.shape[1]
    source = {"g": gate_hbm, "u": up_hbm}
    where_is, copies = {}, {}
    for ref, (kind, pick) in zip(held, parts):
        for j, e in enumerate(pick):
            where_is[kind, e] = (ref, j)
    spot = 0
    for e in range(experts):
        for kind in "gu":
            if (kind, e) not in where_is:
                copies[kind, e] = pltpu.make_async_copy(
                    source[kind].at[e], late.at[spot], sems.at[spot]
                )
                copies[kind, e].start()
                where_is[kind, e] = (late, spot)
                spot += 1
    first = lax.axis_index("expert") * experts
    x = jnp.concatenate([r[:, :width] for r in x_refs], axis=0)
    meta = jnp.concatenate([r[:, width : width + LANES] for r in x_refs], axis=0).astype(F32)
    slots[...] = jnp.concatenate([r[:, width + LANES :] for r in x_refs], axis=0)
    lane = lax.broadcasted_iota(jnp.int32, meta.shape, 1)

    def weights(kind, e):
        if (kind, e) in copies:
            copies[kind, e].wait()
        ref, j = where_is[kind, e]
        return ref[j]

    for e in range(experts):
        w = jnp.sum(jnp.where(lane % EXPERTS == first + e, meta, 0.0), axis=1, keepdims=True)
        a = jnp.dot(x, weights("g", e), preferred_element_type=F32)
        b = jnp.dot(x, weights("u", e), preferred_element_type=F32)
        h[e] = (a * jax.nn.sigmoid(a) * b * w).astype(BF)


def down_kernel(offs, block, *refs):
    n = len(offs)
    h_refs, refs = refs[:n], refs[n:]
    slots_ref, down, shrink, expand, keep, send, hs = refs
    me = lax.axis_index("dp")
    experts, rows, part = h_refs[0].shape
    first = lax.axis_index("expert") * experts
    for i, m in enumerate(offs):
        for p in range(n):
            q = offs.index(offs[p] ^ m)
            hs[me ^ m, :, p * block : (p + 1) * block, :] = h_refs[i][
                :, q * block : (q + 1) * block, :
            ]
    per = shrink.shape[0] // experts
    rank = per // SLOTS
    slot_values = slots_ref[...].astype(F32)
    lane16 = lax.broadcasted_iota(jnp.int32, slot_values.shape, 1)
    lane = lax.broadcasted_iota(jnp.int32, (rows, shrink.shape[0]), 1)
    wanted = me * SLOTS + (lane % per) // rank
    base = None
    small = jnp.zeros((rows, shrink.shape[0]), F32)
    joined = part % LANES == 0
    for e in range(experts):
        chosen = jnp.sum(
            jnp.where(lane16 == first + e, slot_values, 0.0), axis=1, keepdims=True
        ).astype(jnp.int32)
        pieces = [hs[c, e] for c in range(n)]
        cuts = [(c * part, (c + 1) * part) for c in range(n)]
        if joined:
            pieces, cuts = [jnp.concatenate(pieces, axis=1)], [(0, n * part)]
        full = jnp.zeros((rows, shrink.shape[0]), F32)
        for x, (lo, hi) in zip(pieces, cuts):
            term = jnp.dot(x, down[e, lo:hi, :], preferred_element_type=F32)
            base = term if base is None else base + term
            full += lax.dot_general(
                x, shrink[:, lo:hi], (((1,), (1,)), ((), ())), preferred_element_type=F32
            )
        small = jnp.where((lane // per == e) & (chosen == wanted), full, small)
    small = small.astype(BF)
    cols = base.shape[1]
    half = rows // 2
    for c in range(n):
        here = slice(c * cols, (c + 1) * cols)
        out = jnp.dot(small, expand[:, here], preferred_element_type=F32)
        out += jnp.where(me == c, base, 0.0)
        keep[:, here] = out[:half]
        send[:, here] = out[half:].astype(BF)


def halve(keep, got, new_keep, new_send):
    total = keep[...] + got[...].astype(F32)
    half = total.shape[0] // 2
    new_keep[...] = total[:half]
    new_send[...] = total[half:].astype(BF)


def split_rows(block, keep, got, own, *sends):
    total = keep[...] + got[...].astype(F32)
    own[...] = total[:block]
    for i, s in enumerate(sends):
        s[...] = total[(i + 1) * block : (i + 2) * block].astype(BF)


def finish(own, *refs):
    total = own[...]
    for r in refs[:-1]:
        total += r[...].astype(F32)
    refs[-1][...] = total.astype(BF)


def shards(tokens, expert_ids, route_weight, tenant_ids, gate, up, down, shrink, expand, owner, slot):
    n_z, n_dp = lax.axis_size("expert"), lax.axis_size("dp")
    rows, width = tokens.shape
    experts, _, part = gate.shape
    wide = width + 2 * LANES
    all_rows = rows * n_z * n_dp
    block = rows * n_z

    def over(x, axis, m):
        size = lax.axis_size(axis)
        return lax.ppermute(x, axis, [(i, i ^ m) for i in range(size)])

    roomy = 16 << 20
    inputs = (tenant_ids, tokens, expert_ids, route_weight, owner, slot)
    with jax.named_scope("prepare"):
        y = call(
            prepare,
            jax.ShapeDtypeStruct((rows, wide), BF),
            [in_hbm(a) for a in inputs],
            [HB] * len(inputs),
            roomy,
            scratch=[
                *[(pltpu.VMEM if i else pltpu.SMEM)(a.shape, a.dtype) for i, a in enumerate(inputs)],
                pltpu.SemaphoreType.DMA((len(inputs),)),
            ],
        )

    early = [[0], [1, 2], [1]] if experts >= 4 else [[], [], []]
    got = [over(y, "expert", k) for k in range(1, n_z)]
    held, parts = [], []
    if early[0]:
        g0, u0 = prefetch(y, [gate, up], [early[0], early[0]])
        held += [g0, u0]
        parts += [("g", early[0]), ("u", early[0])]
    blocks = [
        call(
            functools.partial(join, n_z),
            jax.ShapeDtypeStruct((block, wide), BF),
            (y, *got, *[in_vmem(a) for a in held]),
            [VM] * (n_z + len(held)),
            roomy,
        )
    ]
    offs = [0]
    bits = []
    b = n_dp // 2
    while b:
        bits.append(b)
        b //= 2
    lead = blocks[0]
    for b in bits:
        blocks = blocks + [over(a, "dp", b) for a in blocks]
        offs = offs + [o ^ b for o in offs]
    if early[1]:
        g1, u1 = prefetch(lead, [gate, up], [early[1], early[2]])
        held += [g1, u1]
        parts += [("g", early[1]), ("u", early[2])]

    late = 2 * experts - sum(len(p) for _, p in parts)
    x_bytes = all_rows * wide * 2
    with jax.named_scope("up"):
        h, slots = call(
            functools.partial(up_kernel, n_dp, parts),
            (
                jax.ShapeDtypeStruct((experts, all_rows, part), BF),
                jax.ShapeDtypeStruct((all_rows, LANES), BF),
            ),
            (*blocks, *[in_vmem(a) for a in held], in_hbm(gate), in_hbm(up)),
            [VM] * (n_dp + len(held)) + [HB, HB],
            (8 << 20) + 3 * x_bytes + late * size_of(gate) // experts,
            scratch=(
                pltpu.VMEM((late,) + gate.shape[1:], BF),
                pltpu.SemaphoreType.DMA((late,)),
            ),
        )

    chunks = [h]
    for b in bits:
        chunks = chunks + [over(a, "dp", b) for a in chunks]
    shrink2 = shrink.reshape(-1, shrink.shape[-1])
    expand2 = expand.reshape(-1, expand.shape[-1])
    every = list(range(experts))
    (down_v,) = prefetch(h, [down], [every])
    h_bytes = experts * all_rows * n_dp * max(part, LANES) * 2
    with jax.named_scope("down"):
        keep, send = call(
            functools.partial(down_kernel, offs, block),
            (
                jax.ShapeDtypeStruct((all_rows // 2, width), F32),
                jax.ShapeDtypeStruct((all_rows // 2, width), BF),
            ),
            (*chunks, slots, in_vmem(down_v), shrink2, expand2),
            [VM] * (n_dp + 4),
            (8 << 20) + 3 * h_bytes + all_rows * width * 4,
            scratch=(pltpu.VMEM((n_dp, experts, all_rows, part), BF),),
        )

    for b in bits[::-1][:-1]:
        arrived = over(send, "dp", b)
        half = keep.shape[0] // 2
        keep, send = call(
            halve,
            (
                jax.ShapeDtypeStruct((half, width), F32),
                jax.ShapeDtypeStruct((half, width), BF),
            ),
            (keep, arrived),
            [VM, VM],
            roomy + 4 * size_of(keep),
        )
    arrived = over(send, "dp", bits[0])
    own, *sends = call(
        functools.partial(split_rows, rows),
        (
            jax.ShapeDtypeStruct((rows, width), F32),
            *[jax.ShapeDtypeStruct((rows, width), BF) for _ in range(1, n_z)],
        ),
        (keep, arrived),
        [VM, VM],
        roomy + 4 * size_of(keep),
    )
    back = [over(s, "expert", k + 1) for k, s in enumerate(sends)]
    return call(
        finish,
        jax.ShapeDtypeStruct((rows, width), BF),
        (own, *back),
        [VM] * n_z,
        roomy,
    )


def solution(mesh):
    rows = ("group", "expert", "dp")
    in_specs = (
        P(rows, None),
        P(rows, None),
        P(rows, None),
        P(rows),
        P("expert", None, "dp"),
        P("expert", None, "dp"),
        P("expert", None, "dp"),
        P("expert", "dp", None, None),
        P("expert", "dp", None, None),
        P(),
        P(),
    )
    return jax.shard_map(
        shards, mesh=mesh, in_specs=in_specs, out_specs=P(rows, None), check_vma=False
    )
```

time: 157 us -> 59.6 us (0.38)
  blocking collectives: 47.3 us -> 0 us
  waiting for transfers between devices: 47.8 us -> 20.3 us
  matrix products: 24.8 us -> 0 us
  Pallas kernels: 0 us -> 23.3 us
  between operations: 13.3 us -> 0.13 us
  local copies, waits for them, and re-layouts: 12.5 us -> 0.01 us
  starting transfers between devices: 6.79 us -> 15.7 us
  other arithmetic: 4.19 us -> 0 us
    all_to_all x2 -> x0, blocking collectives: 34.3 us -> none  [the longest x1 17.8 us: shards(): lax.all_to_all(outgoing, 'expert', split_axis=1, concat_axis=1, tiled=True)]
    all_gather x3 -> x0, waiting for transfers between devices: 33.7 us -> none  [the longest x1 31.5 us: shards(): lax.all_gather(adapter_pool_expand, 'dp', axis=1, tiled=True)]
    dot_general x4 -> x0, matrix products: 24.8 us -> none  [the longest x1 7.77 us: shards(): jnp.einsum('lrd,ldf->lrf', expert_rows, up_weight, preferred_element_type...]
    pallas_call x0 -> x10, Pallas kernels: none -> 23.3 us  [the longest x7 12 us: call(): pl.pallas_call(body, out_shape=out_shape, in_specs=specs, out_specs=jax.t...]
    ppermute x0 -> x14, waiting for transfers between devices: none -> 20.3 us  [over(): return lax.ppermute(x, axis, [(i, i ^ m) for i in range(size)])]
    ppermute x0 -> x14, starting transfers between devices: none -> 15.7 us  [over(): return lax.ppermute(x, axis, [(i, i ^ m) for i in range(size)])]
    all_gather x2 -> x0, blocking collectives: 13 us -> none  [the longest x1 7.73 us: shards(): shard_piece = lax.all_gather(hidden, 'dp', axis=2, tiled=True)]
    all_to_all x2 -> x0, waiting for transfers between devices: 12.8 us -> none  [the longest x1 7.39 us: shards(): lax.all_to_all(lax.all_to_all(final_output, 'expert', split_axis=1, conca...]
  transfers between devices with their start and end apart: 5 -> 14, of which waited for: 4 -> 7; matrix products, arithmetic and copies ran while one was open for 12% -> 0% of each run, Pallas kernels for 0% -> 19%
where the time goes in v1:
time: 59.6 us; the launch traced here: 59.4 us
  Pallas kernels  23.3 us (39%)
  waiting for transfers between devices  20.3 us (34%)
  starting transfers between devices  15.7 us (26%)
    ppermute x14, waiting for transfers between devices, over(): return lax.ppermute(x, axis, [(i, i ^ m) for i in range(size)])  20.3 us
    ppermute x14, starting transfers between devices, over(): return lax.ppermute(x, axis, [(i, i ^ m) for i in range(size)])  15.7 us
    pallas_call x7, Pallas kernels, call(): pl.pallas_call(body, out_shape=out_shape, in_specs=specs, out_specs=jax.t...  12 us
    pallas_call x3, Pallas kernels, prefetch(): pl.pallas_call(functools.partial(fetch, picks), out_shape=shapes, in_spec...  11.3 us
  transfers between devices with their start and end apart: 14, of which 7 were waited for; matrix products, arithmetic and copies ran while one was open for 0% of the time, Pallas kernels for 19%

profile of v1, /device:TPU:0, one launch (start us, length us, event | category | flops | bytes accessed | tf_op | source)
XLA Modules:
  0.0 59.4 jit_solution(2627621069846021415)
XLA Ops:
  0.0 0.9 %prepare.1.dep.refs_0_ = bf16[4,4352]{1,0:T(4,128)(2,1)S(1)} custom-call(s32[4]{0:T(128)} %refs_0_.4, bf16[4,4096]{1,0:T(4,128)(2,1)} %refs_1_.3, s32[4,8]{1,0:T(4,128)} %refs_2_.1, f32[4,8]{1,0:T(4,128)} %refs_3_.1, s32[8,16]{1,0:T(8,128)} %refs_4_.1, s32[8,16]{1,0:T(8,128)} %refs_5_.1), custom_call_target="tpu_custom_call" | custom-call | tf_op jit(solution)/shard_map/prepare/pallas_call | solution.py:32
  0.9 5.1 %collective-permute-start.2 = (bf16[4,4352]{1,0:T(4,128)(2,1)S(1)}, bf16[4,4352]{1,0:T(4,128)(2,1)S(1)}, u32[]{:S(2)}, u32[]{:S(2)}) collective-permute-start(bf16[4,4352]{1,0:T(4,128)(2,1)S(1)} %prepare.1.dep.refs_0_), channel_id=1, source_target_pairs={{0,12},{4,8},{8,4},{12,0},{1,13},{5,9},{9,5},{13,1},{2,14},{6,10},... | collective-permute-start | bytes 104456 | tf_op jit(solution)/shard_map/ppermute | solution.py:237
  6.0 0.6 %collective-permute-start = (bf16[4,4352]{1,0:T(4,128)(2,1)S(1)}, bf16[4,4352]{1,0:T(4,128)(2,1)S(1)}, u32[]{:S(2)}, u32[]{:S(2)}) collective-permute-start(bf16[4,4352]{1,0:T(4,128)(2,1)S(1)} %prepare.1.dep.refs_0_), channel_id=1, source_target_pairs={{0,4},{4,0},{8,12},{12,8},{1,5},{5,1},{9,13},{13,9},{2,6},{6,2},{1... | collective-permute-start | bytes 104456 | tf_op jit(solution)/shard_map/ppermute | solution.py:237
  6.7 2.9 %shard_map.109 = (bf16[1,4096,384]{2,1,0:T(8,128)(2,1)S(1)}, bf16[1,4096,384]{2,1,0:T(8,128)(2,1)S(1)}) custom-call(bf16[4,4352]{1,0:T(4,128)(2,1)S(1)} %prepare.1.dep.refs_0_, bf16[4,4096,384]{2,1,0:T(8,128)(2,1)} %refs_8_.1, bf16[4,4096,384]{2,1,0:T(8,128)(2,1)} %refs_9_.1), custom_call_target="tpu_custom_call" | custom-call | bytes 12582912 | tf_op jit(solution)/shard_map/pallas_call | solution.py:101
  9.6 1.3 %collective-permute-done.1.refs_2_ = bf16[4,4352]{1,0:T(4,128)(2,1)S(1)} collective-permute-done((bf16[4,4352]{1,0:T(4,128)(2,1)S(1)}, bf16[4,4352]{1,0:T(4,128)(2,1)S(1)}, u32[]{:S(2)}, u32[]{:S(2)}) %collective-permute-start.1) | collective-permute-done | bytes 34848 | tf_op jit(solution)/shard_map/ppermute | solution.py:237
  10.9 1.6 %collective-permute-start.3 = (bf16[16,4352]{1,0:T(8,128)(2,1)S(1)}, bf16[16,4352]{1,0:T(8,128)(2,1)S(1)}, u32[]{:S(2)}, u32[]{:S(2)}) collective-permute-start(bf16[16,4352]{1,0:T(8,128)(2,1)S(1)} %shard_map.110.dep.refs_0_), channel_id=1, source_target_pairs={{0,2},{1,3},{2,0},{3,1},{4,6},{5,7},{6,4},{7,5},{8,10},{9,11},{10,... | collective-permute-start | bytes 417800 | tf_op jit(solution)/shard_map/ppermute | solution.py:237
  12.5 3.6 %collective-permute-done.3.refs_1_ = bf16[16,4352]{1,0:T(8,128)(2,1)S(1)} collective-permute-done((bf16[16,4352]{1,0:T(8,128)(2,1)S(1)}, bf16[16,4352]{1,0:T(8,128)(2,1)S(1)}, u32[]{:S(2)}, u32[]{:S(2)}) %collective-permute-start.3) | collective-permute-done | bytes 139296 | tf_op jit(solution)/shard_map/ppermute | solution.py:237
  16.0 3.8 %shard_map.111 = (bf16[2,4096,384]{2,1,0:T(8,128)(2,1)S(1)}, bf16[1,4096,384]{2,1,0:T(8,128)(2,1)S(1)}) custom-call(bf16[16,4352]{1,0:T(8,128)(2,1)S(1)} %shard_map.110.dep.refs_0_, bf16[4,4096,384]{2,1,0:T(8,128)(2,1)} %refs_8_.1, bf16[4,4096,384]{2,1,0:T(8,128)(2,1)} %refs_9_.1), custom_call_target="tpu_custom_call" | custom-call | bytes 18874368 | tf_op jit(solution)/shard_map/pallas_call | solution.py:101
  19.9 7.2 %up.1 = (bf16[4,64,384]{2,1,0:T(8,128)(2,1)S(1)}, bf16[64,128]{1,0:T(8,128)(2,1)S(1)}) custom-call(bf16[16,4352]{1,0:T(8,128)(2,1)S(1)} %shard_map.110.dep.refs_0_, bf16[16,4352]{1,0:T(8,128)(2,1)S(1)} %collective-permute-done.3.refs_1_, bf16[16,4352]{1,0:T(8,128)(2,1)S(1)} %collective-permute-done.4.refs_2_, ...), custom_call_target="tpu_custom_call" | custom-call | tf_op jit(solution)/shard_map/up/pallas_call | solution.py:32
  27.1 1.6 %collective-permute-start.6 = (bf16[4,64,384]{2,1,0:T(8,128)(2,1)S(1)}, bf16[4,64,384]{2,1,0:T(8,128)(2,1)S(1)}, u32[]{:S(2)}, u32[]{:S(2)}) collective-permute-start(bf16[4,64,384]{2,1,0:T(8,128)(2,1)S(1)} %get-tuple-element.23.dep.refs_0_), channel_id=1, source_target_pairs={{0,2},{1,3},{2,0},{3,1},{4,6},{5,7},{6,4},{7,5},{8,10},{9,11},{10,... | collective-permute-start | bytes 589832 | tf_op jit(solution)/shard_map/ppermute | solution.py:237
  28.6 0.2 collective-permute-start.7
  28.8 5.6 %collective-permute-done.6.refs_1_ = bf16[4,64,384]{2,1,0:T(8,128)(2,1)S(1)} collective-permute-done((bf16[4,64,384]{2,1,0:T(8,128)(2,1)S(1)}, bf16[4,64,384]{2,1,0:T(8,128)(2,1)S(1)}, u32[]{:S(2)}, u32[]{:S(2)}) %collective-permute-start.6) | collective-permute-done | bytes 196640 | tf_op jit(solution)/shard_map/ppermute | solution.py:237
  34.4 4.7 %shard_map.112.refs_5_ = bf16[4,1536,1024]{2,1,0:T(8,128)(2,1)S(1)} custom-call(bf16[4,64,384]{2,1,0:T(8,128)(2,1)S(1)} %get-tuple-element.23.dep.refs_0_, bf16[4,1536,1024]{2,1,0:T(8,128)(2,1)} %refs_0_.7), custom_call_target="tpu_custom_call" | custom-call | bytes 25165824 | tf_op jit(solution)/shard_map/pallas_call | solution.py:101
  39.2 3.2 %down.1 = (f32[32,4096]{1,0:T(8,128)S(1)}, bf16[32,4096]{1,0:T(8,128)(2,1)S(1)}) custom-call(bf16[4,64,384]{2,1,0:T(8,128)(2,1)S(1)} %get-tuple-element.23.dep.refs_0_, bf16[4,64,384]{2,1,0:T(8,128)(2,1)S(1)} %collective-permute-done.6.refs_1_, bf16[4,64,384]{2,1,0:T(8,128)(2,1)S(1)} %collective-permute-done.7.refs_2_, ...), custom_call_target="tpu_custom_call" | custom-call | tf_op jit(solution)/shard_map/down/pallas_call | solution.py:32
  42.3 0.6 collective-permute-start.9
  42.9 1.2 %collective-permute-done.9.got = bf16[32,4096]{1,0:T(8,128)(2,1)S(1)} collective-permute-done((bf16[32,4096]{1,0:T(8,128)(2,1)S(1)}, bf16[32,4096]{1,0:T(8,128)(2,1)S(1)}, u32[]{:S(2)}, u32[]{:S(2)}) %collective-permute-start.9) | collective-permute-done | bytes 262176 | tf_op jit(solution)/shard_map/ppermute | solution.py:237
  44.1 1.6 %collective-permute-start.10 = (bf16[16,4096]{1,0:T(8,128)(2,1)S(1)}, bf16[16,4096]{1,0:T(8,128)(2,1)S(1)}, u32[]{:S(2)}, u32[]{:S(2)}) collective-permute-start(bf16[16,4096]{1,0:T(8,128)(2,1)S(1)} %get-tuple-element.28), channel_id=1, source_target_pairs={{0,2},{1,3},{2,0},{3,1},{4,6},{5,7},{6,4},{7,5},{8,10},{9,11},{10,... | collective-permute-start | bytes 393224 | tf_op jit(solution)/shard_map/ppermute | solution.py:237
  45.7 4.3 %collective-permute-done.10.got = bf16[16,4096]{1,0:T(8,128)(2,1)S(1)} collective-permute-done((bf16[16,4096]{1,0:T(8,128)(2,1)S(1)}, bf16[16,4096]{1,0:T(8,128)(2,1)S(1)}, u32[]{:S(2)}, u32[]{:S(2)}) %collective-permute-start.10) | collective-permute-done | bytes 131104 | tf_op jit(solution)/shard_map/ppermute | solution.py:237
  50.0 0.2 collective-permute-start.11
  50.2 2.9 %collective-permute-start.12 = (bf16[4,4096]{1,0:T(4,128)(2,1)S(1)}, bf16[4,4096]{1,0:T(4,128)(2,1)S(1)}, u32[]{:S(2)}, u32[]{:S(2)}) collective-permute-start(bf16[4,4096]{1,0:T(4,128)(2,1)S(1)} %get-tuple-element.31), channel_id=1, source_target_pairs={{0,8},{4,12},{8,0},{12,4},{1,9},{5,13},{9,1},{13,5},{2,10},{6,14},... | collective-permute-start | bytes 98312 | tf_op jit(solution)/shard_map/ppermute | solution.py:237
  53.1 1.4 %collective-permute-start.13 = (bf16[4,4096]{1,0:T(4,128)(2,1)S(1)}, bf16[4,4096]{1,0:T(4,128)(2,1)S(1)}, u32[]{:S(2)}, u32[]{:S(2)}) collective-permute-start(bf16[4,4096]{1,0:T(4,128)(2,1)S(1)} %get-tuple-element.32), channel_id=1, source_target_pairs={{0,12},{4,8},{8,4},{12,0},{1,13},{5,9},{9,5},{13,1},{2,14},{6,10},... | collective-permute-start | bytes 98312 | tf_op jit(solution)/shard_map/ppermute | solution.py:237
  54.4 0.5 collective-permute-done.12.refs_1_
  55.0 3.8 %collective-permute-done.13.refs_2_ = bf16[4,4096]{1,0:T(4,128)(2,1)S(1)} collective-permute-done((bf16[4,4096]{1,0:T(4,128)(2,1)S(1)}, bf16[4,4096]{1,0:T(4,128)(2,1)S(1)}, u32[]{:S(2)}, u32[]{:S(2)}) %collective-permute-start.13) | collective-permute-done | bytes 32800 | tf_op jit(solution)/shard_map/ppermute | solution.py:237
  58.8 0.6 %shard_map.115 = bf16[4,4096]{1,0:T(4,128)(2,1)} custom-call(f32[4,4096]{1,0:T(4,128)S(1)} %get-tuple-element.29.own, bf16[4,4096]{1,0:T(4,128)(2,1)S(1)} %collective-permute-done.11.refs_0_, bf16[4,4096]{1,0:T(4,128)(2,1)S(1)} %collective-permute-done.12.refs_1_, bf16[4,4096]{1,0:T(4,128)(2,1)S(1)} %collective-permute-done.13.refs_2_), custom_call_target="tpu_custom_call" | custom-call | tf_op jit(solution)/shard_map/pallas_call | solution.py:32
  (18 shorter events, 0.2 us)
Async XLA Ops:
  0.9 8.6 %collective-permute-start.2 = (bf16[4,4352]{1,0:T(4,128)(2,1)S(1)}, bf16[4,4352]{1,0:T(4,128)(2,1)S(1)}, u32[]{:S(2)}, u32[]{:S(2)}) collective-permute-start(bf16[4,4352]{1,0:T(4,128)(2,1)S(1)} %prepare.1.dep.refs_0_), channel_id=1, source_target_pairs={{0,12},{4,8},{8,4},{12,0},{1,13},{5,9},{9,5},{13,1},{2,14},{6,10},... | collective-permute-start | bytes 104456 | tf_op jit(solution)/shard_map/ppermute | solution.py:237
  6.0 4.8 %collective-permute-start.1 = (bf16[4,4352]{1,0:T(4,128)(2,1)S(1)}, bf16[4,4352]{1,0:T(4,128)(2,1)S(1)}, u32[]{:S(2)}, u32[]{:S(2)}) collective-permute-start(bf16[4,4352]{1,0:T(4,128)(2,1)S(1)} %prepare.1.dep.refs_0_), channel_id=1, source_target_pairs={{0,8},{4,12},{8,0},{12,4},{1,9},{5,13},{9,1},{13,5},{2,10},{6,14},... | collective-permute-start | bytes 104456 | tf_op jit(solution)/shard_map/ppermute | solution.py:237
  6.0 4.8 %collective-permute-start = (bf16[4,4352]{1,0:T(4,128)(2,1)S(1)}, bf16[4,4352]{1,0:T(4,128)(2,1)S(1)}, u32[]{:S(2)}, u32[]{:S(2)}) collective-permute-start(bf16[4,4352]{1,0:T(4,128)(2,1)S(1)} %prepare.1.dep.refs_0_), channel_id=1, source_target_pairs={{0,4},{4,0},{8,12},{12,8},{1,5},{5,1},{9,13},{13,9},{2,6},{6,2},{1... | collective-permute-start | bytes 104456 | tf_op jit(solution)/shard_map/ppermute | solution.py:237
  10.9 5.1 %collective-permute-start.3 = (bf16[16,4352]{1,0:T(8,128)(2,1)S(1)}, bf16[16,4352]{1,0:T(8,128)(2,1)S(1)}, u32[]{:S(2)}, u32[]{:S(2)}) collective-permute-start(bf16[16,4352]{1,0:T(8,128)(2,1)S(1)} %shard_map.110.dep.refs_0_), channel_id=1, source_target_pairs={{0,2},{1,3},{2,0},{3,1},{4,6},{5,7},{6,4},{7,5},{8,10},{9,11},{10,... | collective-permute-start | bytes 417800 | tf_op jit(solution)/shard_map/ppermute | solution.py:237
  12.5 7.4 %collective-permute-start.4 = (bf16[16,4352]{1,0:T(8,128)(2,1)S(1)}, bf16[16,4352]{1,0:T(8,128)(2,1)S(1)}, u32[]{:S(2)}, u32[]{:S(2)}) collective-permute-start(bf16[16,4352]{1,0:T(8,128)(2,1)S(1)} %shard_map.110.dep.refs_0_), channel_id=1, source_target_pairs={{0,1},{1,0},{2,3},{3,2},{4,5},{5,4},{6,7},{7,6},{8,9},{9,8},{10,11... | collective-permute-start | bytes 417800 | tf_op jit(solution)/shard_map/ppermute | solution.py:237
  16.0 3.8 %collective-permute-start.5 = (bf16[16,4352]{1,0:T(8,128)(2,1)S(1)}, bf16[16,4352]{1,0:T(8,128)(2,1)S(1)}, u32[]{:S(2)}, u32[]{:S(2)}) collective-permute-start(bf16[16,4352]{1,0:T(8,128)(2,1)S(1)} %collective-permute-done.3.refs_1_), channel_id=1, source_target_pairs={{0,1},{1,0},{2,3},{3,2},{4,5},{5,4},{6,7},{7,6},{8,9},{9,8},{10,11... | collective-permute-start | bytes 417800 | tf_op jit(solution)/shard_map/ppermute | solution.py:237
  27.0 12.1 %copy-start = (bf16[4,2,16,4096]{3,2,1,0:T(8,128)(2,1)S(1)}, bf16[4,2,16,4096]{3,2,1,0:T(8,128)(2,1)}, u32[]{:S(2)}) copy-start(bf16[4,2,16,4096]{3,2,1,0:T(8,128)(2,1)} %param.19) | copy-start | bytes 3145732
  27.0 12.1 %copy-start.1 = (bf16[4,2,16,1536]{3,2,1,0:T(8,128)(2,1)S(1)}, bf16[4,2,16,1536]{3,2,1,0:T(8,128)(2,1)}, u32[]{:S(2)}) copy-start(bf16[4,2,16,1536]{3,2,1,0:T(8,128)(2,1)} %param.18) | copy-start | bytes 1179652
  27.1 7.4 %collective-permute-start.6 = (bf16[4,64,384]{2,1,0:T(8,128)(2,1)S(1)}, bf16[4,64,384]{2,1,0:T(8,128)(2,1)S(1)}, u32[]{:S(2)}, u32[]{:S(2)}) collective-permute-start(bf16[4,64,384]{2,1,0:T(8,128)(2,1)S(1)} %get-tuple-element.23.dep.refs_0_), channel_id=1, source_target_pairs={{0,2},{1,3},{2,0},{3,1},{4,6},{5,7},{6,4},{7,5},{8,10},{9,11},{10,... | collective-permute-start | bytes 589832 | tf_op jit(solution)/shard_map/ppermute | solution.py:237
  28.6 10.5 %collective-permute-start.7 = (bf16[4,64,384]{2,1,0:T(8,128)(2,1)S(1)}, bf16[4,64,384]{2,1,0:T(8,128)(2,1)S(1)}, u32[]{:S(2)}, u32[]{:S(2)}) collective-permute-start(bf16[4,64,384]{2,1,0:T(8,128)(2,1)S(1)} %get-tuple-element.23.dep.refs_0_), channel_id=1, source_target_pairs={{0,1},{1,0},{2,3},{3,2},{4,5},{5,4},{6,7},{7,6},{8,9},{9,8},{10,11... | collective-permute-start | bytes 589832 | tf_op jit(solution)/shard_map/ppermute | solution.py:237
  34.4 4.7 %collective-permute-start.8 = (bf16[4,64,384]{2,1,0:T(8,128)(2,1)S(1)}, bf16[4,64,384]{2,1,0:T(8,128)(2,1)S(1)}, u32[]{:S(2)}, u32[]{:S(2)}) collective-permute-start(bf16[4,64,384]{2,1,0:T(8,128)(2,1)S(1)} %collective-permute-done.6.refs_1_), channel_id=1, source_target_pairs={{0,1},{1,0},{2,3},{3,2},{4,5},{5,4},{6,7},{7,6},{8,9},{9,8},{10,11... | collective-permute-start | bytes 589832 | tf_op jit(solution)/shard_map/ppermute | solution.py:237
  42.3 1.7 %collective-permute-start.9 = (bf16[32,4096]{1,0:T(8,128)(2,1)S(1)}, bf16[32,4096]{1,0:T(8,128)(2,1)S(1)}, u32[]{:S(2)}, u32[]{:S(2)}) collective-permute-start(bf16[32,4096]{1,0:T(8,128)(2,1)S(1)} %get-tuple-element.26), channel_id=1, source_target_pairs={{0,1},{1,0},{2,3},{3,2},{4,5},{5,4},{6,7},{7,6},{8,9},{9,8},{10,11... | collective-permute-start | bytes 786440 | tf_op jit(solution)/shard_map/ppermute | solution.py:237
  44.1 5.8 %collective-permute-start.10 = (bf16[16,4096]{1,0:T(8,128)(2,1)S(1)}, bf16[16,4096]{1,0:T(8,128)(2,1)S(1)}, u32[]{:S(2)}, u32[]{:S(2)}) collective-permute-start(bf16[16,4096]{1,0:T(8,128)(2,1)S(1)} %get-tuple-element.28), channel_id=1, source_target_pairs={{0,2},{1,3},{2,0},{3,1},{4,6},{5,7},{6,4},{7,5},{8,10},{9,11},{10,... | collective-permute-start | bytes 393224 | tf_op jit(solution)/shard_map/ppermute | solution.py:237
  50.0 4.5 %collective-permute-start.11 = (bf16[4,4096]{1,0:T(4,128)(2,1)S(1)}, bf16[4,4096]{1,0:T(4,128)(2,1)S(1)}, u32[]{:S(2)}, u32[]{:S(2)}) collective-permute-start(bf16[4,4096]{1,0:T(4,128)(2,1)S(1)} %get-tuple-element.30), channel_id=1, source_target_pairs={{0,4},{4,0},{8,12},{12,8},{1,5},{5,1},{9,13},{13,9},{2,6},{6,2},{1... | collective-permute-start | bytes 98312 | tf_op jit(solution)/shard_map/ppermute | solution.py:237
  50.2 4.8 %collective-permute-start.12 = (bf16[4,4096]{1,0:T(4,128)(2,1)S(1)}, bf16[4,4096]{1,0:T(4,128)(2,1)S(1)}, u32[]{:S(2)}, u32[]{:S(2)}) collective-permute-start(bf16[4,4096]{1,0:T(4,128)(2,1)S(1)} %get-tuple-element.31), channel_id=1, source_target_pairs={{0,8},{4,12},{8,0},{12,4},{1,9},{5,13},{9,1},{13,5},{2,10},{6,14},... | collective-permute-start | bytes 98312 | tf_op jit(solution)/shard_map/ppermute | solution.py:237
  53.1 5.7 %collective-permute-start.13 = (bf16[4,4096]{1,0:T(4,128)(2,1)S(1)}, bf16[4,4096]{1,0:T(4,128)(2,1)S(1)}, u32[]{:S(2)}, u32[]{:S(2)}) collective-permute-start(bf16[4,4096]{1,0:T(4,128)(2,1)S(1)} %get-tuple-element.32), channel_id=1, source_target_pairs={{0,12},{4,8},{8,4},{12,0},{1,13},{5,9},{9,5},{13,1},{2,14},{6,10},... | collective-permute-start | bytes 98312 | tf_op jit(solution)/shard_map/ppermute | solution.py:237

commit v2 on v1

--- a/solution.py
+++ b/solution.py
@@ -15,9 +15,7 @@
 F32 = jnp.float32
 
 VM = pl.BlockSpec(memory_space=pltpu.VMEM)
-SM = pl.BlockSpec(memory_space=pltpu.SMEM)
 HB = pl.BlockSpec(memory_space=pltpu.HBM)
-ANY = pl.BlockSpec(memory_space=pl.ANY)
 
 
 def in_vmem(x):
@@ -51,7 +49,7 @@
 
 
 def prepare(*refs):
-    y, held, sems = refs[6], refs[7:13], refs[13]
+    y, held, sems = refs[9], refs[10:16], refs[16]
     copies = [pltpu.make_async_copy(refs[i], held[i], sems.at[i]) for i in range(6)]
     for c in copies:
         c.start()
@@ -61,7 +59,7 @@
     rows, width = tok.shape
     y[:, :width] = tok[...]
     lane = lax.broadcasted_iota(jnp.int32, (rows, LANES), 1)
-    expert, piece = lane % EXPERTS, lane // EXPERTS
+    expert, piece = lane & (EXPERTS - 1), lane >> (EXPERTS.bit_length() - 1)
     w = jnp.zeros((rows, LANES), F32)
     for k in range(TOP):
         w += jnp.where(ids[:, k : k + 1] == expert, rw[:, k : k + 1], 0.0)
@@ -80,77 +78,32 @@
     )
 
 
-def fetch(experts, dep, *refs):
-    del dep
-    count = len(experts)
-    sems = refs[-1]
-    copies = []
-    for i, pick in enumerate(experts):
-        src, dst = refs[i], refs[count + i]
-        for j, e in enumerate(pick):
-            copies.append(pltpu.make_async_copy(src.at[e], dst.at[j], sems.at[len(copies)]))
-    for c in copies:
-        c.start()
-    for c in copies:
-        c.wait()
-
-
-def prefetch(dep, arrays, picks):
-    shapes = [pltpu.VMEM((len(p),) + a.shape[1:], a.dtype) for a, p in zip(arrays, picks)]
-    moved = sum(size_of(a) * len(p) // a.shape[0] for a, p in zip(arrays, picks))
-    out = pl.pallas_call(
-        functools.partial(fetch, picks),
-        out_shape=shapes,
-        in_specs=[ANY] + [HB] * len(arrays),
-        out_specs=[VM] * len(arrays),
-        scratch_shapes=[pltpu.SemaphoreType.DMA((sum(len(p) for p in picks),))],
-        cost_estimate=pl.CostEstimate(flops=0, bytes_accessed=2 * moved, transcendentals=0),
-        compiler_params=pltpu.CompilerParams(vmem_limit_bytes=1 << 20),
-    )(dep, *[in_hbm(a) for a in arrays])
-    return out
-
-
 def join(count, *refs):
     out = refs[-1]
     out[...] = jnp.concatenate([r[...].astype(F32) for r in refs[:count]], axis=0).astype(BF)
 
 
-def up_kernel(count, parts, *refs):
-    x_refs, refs = refs[:count], refs[count:]
-    held, refs = refs[: len(parts)], refs[len(parts) :]
-    gate_hbm, up_hbm, h, slots, late, sems = refs
-    experts, width = gate_hbm.shape[0], gate_hbm.shape[1]
-    source = {"g": gate_hbm, "u": up_hbm}
-    where_is, copies = {}, {}
-    for ref, (kind, pick) in zip(held, parts):
-        for j, e in enumerate(pick):
-            where_is[kind, e] = (ref, j)
-    spot = 0
-    for e in range(experts):
-        for kind in "gu":
-            if (kind, e) not in where_is:
-                copies[kind, e] = pltpu.make_async_copy(
-                    source[kind].at[e], late.at[spot], sems.at[spot]
-                )
-                copies[kind, e].start()
-                where_is[kind, e] = (late, spot)
-                spot += 1
+def up_kernel(count, *refs):
+    x_refs = refs[:count]
+    gate, up, h, slots, xs = refs[count:]
+    experts, width = gate.shape[0], gate.shape[1]
     first = lax.axis_index("expert") * experts
-    x = jnp.concatenate([r[:, :width] for r in x_refs], axis=0)
+    block = x_refs[0].shape[0]
+    for i, r in enumerate(x_refs):
+        xs[i * block : (i + 1) * block] = r[:, :width]
     meta = jnp.concatenate([r[:, width : width + LANES] for r in x_refs], axis=0).astype(F32)
     slots[...] = jnp.concatenate([r[:, width + LANES :] for r in x_refs], axis=0)
     lane = lax.broadcasted_iota(jnp.int32, meta.shape, 1)
-
-    def weights(kind, e):
-        if (kind, e) in copies:
-            copies[kind, e].wait()
-        ref, j = where_is[kind, e]
-        return ref[j]
-
+    step = 256
     for e in range(experts):
-        w = jnp.sum(jnp.where(lane % EXPERTS == first + e, meta, 0.0), axis=1, keepdims=True)
-        a = jnp.dot(x, weights("g", e), preferred_element_type=F32)
-        b = jnp.dot(x, weights("u", e), preferred_element_type=F32)
+        w = jnp.sum(
+            jnp.where(lane & (EXPERTS - 1) == first + e, meta, 0.0), axis=1, keepdims=True
+        )
+        a = b = 0.0
+        for k in range(0, width, step):
+            x = xs[:, k : k + step]
+            a += jnp.dot(x, gate[e, k : k + step], preferred_element_type=F32)
+            b += jnp.dot(x, up[e, k : k + step], preferred_element_type=F32)
         h[e] = (a * jax.nn.sigmoid(a) * b * w).astype(BF)
 
 
@@ -242,8 +195,8 @@
         y = call(
             prepare,
             jax.ShapeDtypeStruct((rows, wide), BF),
-            [in_hbm(a) for a in inputs],
-            [HB] * len(inputs),
+            [in_hbm(a) for a in (*inputs, gate, up, down)],
+            [HB] * (len(inputs) + 3),
             roomy,
             scratch=[
                 *[(pltpu.VMEM if i else pltpu.SMEM)(a.shape, a.dtype) for i, a in enumerate(inputs)],
@@ -251,19 +204,13 @@
             ],
         )
 
-    early = [[0], [1, 2], [1]] if experts >= 4 else [[], [], []]
     got = [over(y, "expert", k) for k in range(1, n_z)]
-    held, parts = [], []
-    if early[0]:
-        g0, u0 = prefetch(y, [gate, up], [early[0], early[0]])
-        held += [g0, u0]
-        parts += [("g", early[0]), ("u", early[0])]
     blocks = [
         call(
             functools.partial(join, n_z),
             jax.ShapeDtypeStruct((block, wide), BF),
-            (y, *got, *[in_vmem(a) for a in held]),
-            [VM] * (n_z + len(held)),
+            (y, *got),
+            [VM] * n_z,
             roomy,
         )
     ]
@@ -273,31 +220,21 @@
     while b:
         bits.append(b)
         b //= 2
-    lead = blocks[0]
     for b in bits:
         blocks = blocks + [over(a, "dp", b) for a in blocks]
         offs = offs + [o ^ b for o in offs]
-    if early[1]:
-        g1, u1 = prefetch(lead, [gate, up], [early[1], early[2]])
-        held += [g1, u1]
-        parts += [("g", early[1]), ("u", early[2])]
-
-    late = 2 * experts - sum(len(p) for _, p in parts)
     x_bytes = all_rows * wide * 2
     with jax.named_scope("up"):
         h, slots = call(
-            functools.partial(up_kernel, n_dp, parts),
+            functools.partial(up_kernel, n_dp),
             (
                 jax.ShapeDtypeStruct((experts, all_rows, part), BF),
                 jax.ShapeDtypeStruct((all_rows, LANES), BF),
             ),
-            (*blocks, *[in_vmem(a) for a in held], in_hbm(gate), in_hbm(up)),
-            [VM] * (n_dp + len(held)) + [HB, HB],
-            (8 << 20) + 3 * x_bytes + late * size_of(gate) // experts,
-            scratch=(
-                pltpu.VMEM((late,) + gate.shape[1:], BF),
-                pltpu.SemaphoreType.DMA((late,)),
-            ),
+            (*blocks, in_vmem(gate), in_vmem(up)),
+            [VM] * n_dp + [VM, VM],
+            (8 << 20) + 3 * x_bytes,
+            scratch=(pltpu.VMEM((all_rows, width), BF),),
         )
 
     chunks = [h]
@@ -305,8 +242,6 @@
         chunks = chunks + [over(a, "dp", b) for a in chunks]
     shrink2 = shrink.reshape(-1, shrink.shape[-1])
     expand2 = expand.reshape(-1, expand.shape[-1])
-    every = list(range(experts))
-    (down_v,) = prefetch(h, [down], [every])
     h_bytes = experts * all_rows * n_dp * max(part, LANES) * 2
     with jax.named_scope("down"):
         keep, send = call(
@@ -315,7 +250,7 @@
                 jax.ShapeDtypeStruct((all_rows // 2, width), F32),
                 jax.ShapeDtypeStruct((all_rows // 2, width), BF),
             ),
-            (*chunks, slots, in_vmem(down_v), shrink2, expand2),
+            (*chunks, slots, in_vmem(down), shrink2, expand2),
             [VM] * (n_dp + 4),
             (8 << 20) + 3 * h_bytes + all_rows * width * 4,
             scratch=(pltpu.VMEM((n_dp, experts, all_rows, part), BF),),

time: 59.6 us -> 49.2 us (0.83)
  Pallas kernels: 23.3 us -> 8.92 us
  waiting for transfers between devices: 20.3 us -> 24.9 us
  starting transfers between devices: 15.7 us -> 15.1 us
    pallas_call x3 -> x0, Pallas kernels: 11.3 us -> none  [prefetch(): pl.pallas_call(functools.partial(fetch, picks), out_shape=shapes, in_spec...]
    ppermute x14, waiting for transfers between devices: 20.3 us -> 24.9 us  [over(): return lax.ppermute(x, axis, [(i, i ^ m) for i in range(size)])]
    pallas_call x7, Pallas kernels: 12 us -> 8.92 us  [call(): pl.pallas_call(body, out_shape=out_shape, in_specs=specs, out_specs=jax.t...]
    ppermute x14, starting transfers between devices: 15.7 us -> 15.1 us  [over(): return lax.ppermute(x, axis, [(i, i ^ m) for i in range(size)])]
  transfers between devices with their start and end apart: 14 -> 14, of which waited for: 7 -> 10; matrix products, arithmetic and copies ran while one was open for 0% -> 0% of each run, Pallas kernels for 19% -> 0%
where the time goes in v2:
time: 49.2 us; the launch traced here: 49 us
  waiting for transfers between devices  24.9 us (51%)
  starting transfers between devices  15.1 us (31%)
  Pallas kernels  8.92 us (18%)
    ppermute x14, waiting for transfers between devices, over(): return lax.ppermute(x, axis, [(i, i ^ m) for i in range(size)])  24.9 us
    ppermute x14, starting transfers between devices, over(): return lax.ppermute(x, axis, [(i, i ^ m) for i in range(size)])  15.1 us
    pallas_call x7, Pallas kernels, call(): pl.pallas_call(body, out_shape=out_shape, in_specs=specs, out_specs=jax.t...  8.92 us
  transfers between devices with their start and end apart: 14, of which 10 were waited for; matrix products, arithmetic and copies ran while one was open for 0% of the time, Pallas kernels for 0%

profile of v2, /device:TPU:0, one launch (start us, length us, event | category | flops | bytes accessed | tf_op | source)
XLA Modules:
  0.0 49.0 jit_solution(17518047765552840807)
XLA Ops:
  0.0 1.1 %prepare.1.refs_0_ = bf16[4,4352]{1,0:T(4,128)(2,1)S(1)} custom-call(s32[4]{0:T(128)} %refs_0_.1, bf16[4,4096]{1,0:T(4,128)(2,1)} %refs_1_.1, s32[4,8]{1,0:T(4,128)} %refs_2_.1, f32[4,8]{1,0:T(4,128)} %refs_3_.1, s32[8,16]{1,0:T(8,128)} %refs_4_.2, s32[8,16]{1,0:T(8,128)} %refs_5_.3, bf16[4,4096,384]{2,1,0:T(8,128)(2,1)} %refs_4_.3, ...), custom_call_target="tpu_custom_call" | custom-call | tf_op jit(solution)/shard_map/prepare/pallas_call | solution.py:30
  1.1 5.1 %collective-permute-start.2 = (bf16[4,4352]{1,0:T(4,128)(2,1)S(1)}, bf16[4,4352]{1,0:T(4,128)(2,1)S(1)}, u32[]{:S(2)}, u32[]{:S(2)}) collective-permute-start(bf16[4,4352]{1,0:T(4,128)(2,1)S(1)} %prepare.1.refs_0_), channel_id=1, source_target_pairs={{0,12},{4,8},{8,4},{12,0},{1,13},{5,9},{9,5},{13,1},{2,14},{6,10},... | collective-permute-start | bytes 104456 | tf_op jit(solution)/shard_map/ppermute | solution.py:190
  6.2 0.6 %collective-permute-start = (bf16[4,4352]{1,0:T(4,128)(2,1)S(1)}, bf16[4,4352]{1,0:T(4,128)(2,1)S(1)}, u32[]{:S(2)}, u32[]{:S(2)}) collective-permute-start(bf16[4,4352]{1,0:T(4,128)(2,1)S(1)} %prepare.1.refs_0_), channel_id=1, source_target_pairs={{0,4},{4,0},{8,12},{12,8},{1,5},{5,1},{9,13},{13,9},{2,6},{6,2},{1... | collective-permute-start | bytes 104456 | tf_op jit(solution)/shard_map/ppermute | solution.py:190
  6.8 1.3 %collective-permute-done.2.refs_3_ = bf16[4,4352]{1,0:T(4,128)(2,1)S(1)} collective-permute-done((bf16[4,4352]{1,0:T(4,128)(2,1)S(1)}, bf16[4,4352]{1,0:T(4,128)(2,1)S(1)}, u32[]{:S(2)}, u32[]{:S(2)}) %collective-permute-start.2) | collective-permute-done | bytes 34848 | tf_op jit(solution)/shard_map/ppermute | solution.py:190
  8.1 2.9 %collective-permute-done.1.refs_2_ = bf16[4,4352]{1,0:T(4,128)(2,1)S(1)} collective-permute-done((bf16[4,4352]{1,0:T(4,128)(2,1)S(1)}, bf16[4,4352]{1,0:T(4,128)(2,1)S(1)}, u32[]{:S(2)}, u32[]{:S(2)}) %collective-permute-start.1) | collective-permute-done | bytes 34848 | tf_op jit(solution)/shard_map/ppermute | solution.py:190
  11.1 0.0 slice-start.1
  11.1 1.6 %collective-permute-start.3 = (bf16[16,4352]{1,0:T(8,128)(2,1)S(1)}, bf16[16,4352]{1,0:T(8,128)(2,1)S(1)}, u32[]{:S(2)}, u32[]{:S(2)}) collective-permute-start(bf16[16,4352]{1,0:T(8,128)(2,1)S(1)} %shard_map.109.refs_0_), channel_id=1, source_target_pairs={{0,2},{1,3},{2,0},{3,1},{4,6},{5,7},{6,4},{7,5},{8,10},{9,11},{10,... | collective-permute-start | bytes 417800 | tf_op jit(solution)/shard_map/ppermute | solution.py:190
  12.7 3.6 %collective-permute-done.3.refs_1_ = bf16[16,4352]{1,0:T(8,128)(2,1)S(1)} collective-permute-done((bf16[16,4352]{1,0:T(8,128)(2,1)S(1)}, bf16[16,4352]{1,0:T(8,128)(2,1)S(1)}, u32[]{:S(2)}, u32[]{:S(2)}) %collective-permute-start.3) | collective-permute-done | bytes 139296 | tf_op jit(solution)/shard_map/ppermute | solution.py:190
  16.3 1.4 %collective-permute-done.5.refs_3_ = bf16[16,4352]{1,0:T(8,128)(2,1)S(1)} collective-permute-done((bf16[16,4352]{1,0:T(8,128)(2,1)S(1)}, bf16[16,4352]{1,0:T(8,128)(2,1)S(1)}, u32[]{:S(2)}, u32[]{:S(2)}) %collective-permute-start.5) | collective-permute-done | bytes 139296 | tf_op jit(solution)/shard_map/ppermute | solution.py:190
  17.6 3.9 %up.1 = (bf16[4,64,384]{2,1,0:T(8,128)(2,1)S(1)}, bf16[64,128]{1,0:T(8,128)(2,1)S(1)}) custom-call(bf16[16,4352]{1,0:T(8,128)(2,1)S(1)} %shard_map.109.refs_0_, bf16[16,4352]{1,0:T(8,128)(2,1)S(1)} %collective-permute-done.3.refs_1_, bf16[16,4352]{1,0:T(8,128)(2,1)S(1)} %collective-permute-done.4.refs_2_, ...), custom_call_target="tpu_custom_call" | custom-call | tf_op jit(solution)/shard_map/up/pallas_call | solution.py:30
  21.6 1.6 %collective-permute-start.6 = (bf16[4,64,384]{2,1,0:T(8,128)(2,1)S(1)}, bf16[4,64,384]{2,1,0:T(8,128)(2,1)S(1)}, u32[]{:S(2)}, u32[]{:S(2)}) collective-permute-start(bf16[4,64,384]{2,1,0:T(8,128)(2,1)S(1)} %get-tuple-element.15.refs_0_), channel_id=1, source_target_pairs={{0,2},{1,3},{2,0},{3,1},{4,6},{5,7},{6,4},{7,5},{8,10},{9,11},{10,... | collective-permute-start | bytes 589832 | tf_op jit(solution)/shard_map/ppermute | solution.py:190
  23.1 5.5 %collective-permute-done.6.refs_1_ = bf16[4,64,384]{2,1,0:T(8,128)(2,1)S(1)} collective-permute-done((bf16[4,64,384]{2,1,0:T(8,128)(2,1)S(1)}, bf16[4,64,384]{2,1,0:T(8,128)(2,1)S(1)}, u32[]{:S(2)}, u32[]{:S(2)}) %collective-permute-start.6) | collective-permute-done | bytes 196640 | tf_op jit(solution)/shard_map/ppermute | solution.py:190
  28.6 1.4 %collective-permute-done.8.refs_3_ = bf16[4,64,384]{2,1,0:T(8,128)(2,1)S(1)} collective-permute-done((bf16[4,64,384]{2,1,0:T(8,128)(2,1)S(1)}, bf16[4,64,384]{2,1,0:T(8,128)(2,1)S(1)}, u32[]{:S(2)}, u32[]{:S(2)}) %collective-permute-start.8) | collective-permute-done | bytes 196640 | tf_op jit(solution)/shard_map/ppermute | solution.py:190
  30.0 3.2 %down.1 = (f32[32,4096]{1,0:T(8,128)S(1)}, bf16[32,4096]{1,0:T(8,128)(2,1)S(1)}) custom-call(bf16[4,64,384]{2,1,0:T(8,128)(2,1)S(1)} %get-tuple-element.15.refs_0_, bf16[4,64,384]{2,1,0:T(8,128)(2,1)S(1)} %collective-permute-done.6.refs_1_, bf16[4,64,384]{2,1,0:T(8,128)(2,1)S(1)} %collective-permute-done.7.refs_2_, ...), custom_call_target="tpu_custom_call" | custom-call | tf_op jit(solution)/shard_map/down/pallas_call | solution.py:30
  33.2 0.2 collective-permute-start.9
  33.4 1.4 %collective-permute-done.9.got = bf16[32,4096]{1,0:T(8,128)(2,1)S(1)} collective-permute-done((bf16[32,4096]{1,0:T(8,128)(2,1)S(1)}, bf16[32,4096]{1,0:T(8,128)(2,1)S(1)}, u32[]{:S(2)}, u32[]{:S(2)}) %collective-permute-start.9) | collective-permute-done | bytes 262176 | tf_op jit(solution)/shard_map/ppermute | solution.py:190
  34.9 1.6 %collective-permute-start.10 = (bf16[16,4096]{1,0:T(8,128)(2,1)S(1)}, bf16[16,4096]{1,0:T(8,128)(2,1)S(1)}, u32[]{:S(2)}, u32[]{:S(2)}) collective-permute-start(bf16[16,4096]{1,0:T(8,128)(2,1)S(1)} %get-tuple-element.20), channel_id=1, source_target_pairs={{0,2},{1,3},{2,0},{3,1},{4,6},{5,7},{6,4},{7,5},{8,10},{9,11},{10,... | collective-permute-start | bytes 393224 | tf_op jit(solution)/shard_map/ppermute | solution.py:190
  36.4 4.0 %collective-permute-done.10.got = bf16[16,4096]{1,0:T(8,128)(2,1)S(1)} collective-permute-done((bf16[16,4096]{1,0:T(8,128)(2,1)S(1)}, bf16[16,4096]{1,0:T(8,128)(2,1)S(1)}, u32[]{:S(2)}, u32[]{:S(2)}) %collective-permute-start.10) | collective-permute-done | bytes 131104 | tf_op jit(solution)/shard_map/ppermute | solution.py:190
  40.5 0.1 collective-permute-start.11
  40.6 2.1 %collective-permute-start.12 = (bf16[4,4096]{1,0:T(4,128)(2,1)S(1)}, bf16[4,4096]{1,0:T(4,128)(2,1)S(1)}, u32[]{:S(2)}, u32[]{:S(2)}) collective-permute-start(bf16[4,4096]{1,0:T(4,128)(2,1)S(1)} %get-tuple-element.23), channel_id=1, source_target_pairs={{0,8},{4,12},{8,0},{12,4},{1,9},{5,13},{9,1},{13,5},{2,10},{6,14},... | collective-permute-start | bytes 98312 | tf_op jit(solution)/shard_map/ppermute | solution.py:190
  42.7 2.3 %collective-permute-start.13 = (bf16[4,4096]{1,0:T(4,128)(2,1)S(1)}, bf16[4,4096]{1,0:T(4,128)(2,1)S(1)}, u32[]{:S(2)}, u32[]{:S(2)}) collective-permute-start(bf16[4,4096]{1,0:T(4,128)(2,1)S(1)} %get-tuple-element.24), channel_id=1, source_target_pairs={{0,12},{4,8},{8,4},{12,0},{1,13},{5,9},{9,5},{13,1},{2,14},{6,10},... | collective-permute-start | bytes 98312 | tf_op jit(solution)/shard_map/ppermute | solution.py:190
  45.0 0.6 %collective-permute-done.12.refs_1_ = bf16[4,4096]{1,0:T(4,128)(2,1)S(1)} collective-permute-done((bf16[4,4096]{1,0:T(4,128)(2,1)S(1)}, bf16[4,4096]{1,0:T(4,128)(2,1)S(1)}, u32[]{:S(2)}, u32[]{:S(2)}) %collective-permute-start.12) | collective-permute-done | bytes 32800 | tf_op jit(solution)/shard_map/ppermute | solution.py:190
  45.5 2.9 %collective-permute-done.13.refs_2_ = bf16[4,4096]{1,0:T(4,128)(2,1)S(1)} collective-permute-done((bf16[4,4096]{1,0:T(4,128)(2,1)S(1)}, bf16[4,4096]{1,0:T(4,128)(2,1)S(1)}, u32[]{:S(2)}, u32[]{:S(2)}) %collective-permute-start.13) | collective-permute-done | bytes 32800 | tf_op jit(solution)/shard_map/ppermute | solution.py:190
  48.4 0.6 %shard_map.112 = bf16[4,4096]{1,0:T(4,128)(2,1)} custom-call(f32[4,4096]{1,0:T(4,128)S(1)} %get-tuple-element.21.own, bf16[4,4096]{1,0:T(4,128)(2,1)S(1)} %collective-permute-done.11.refs_0_, bf16[4,4096]{1,0:T(4,128)(2,1)S(1)} %collective-permute-done.12.refs_1_, bf16[4,4096]{1,0:T(4,128)(2,1)S(1)} %collective-permute-done.13.refs_2_), custom_call_target="tpu_custom_call" | custom-call | tf_op jit(solution)/shard_map/pallas_call | solution.py:30
  (26 shorter events, 0.2 us)
Async XLA Ops:
  0.0 17.6 %copy-start.1 = (bf16[4,4096,384]{2,1,0:T(8,128)(2,1)S(1)}, bf16[4,4096,384]{2,1,0:T(8,128)(2,1)}, u32[]{:S(2)}) copy-start(bf16[4,4096,384]{2,1,0:T(8,128)(2,1)} %refs_5_.4) | copy-start | bytes 37748740
  0.0 17.6 %copy-start = (bf16[4,4096,384]{2,1,0:T(8,128)(2,1)S(1)}, bf16[4,4096,384]{2,1,0:T(8,128)(2,1)}, u32[]{:S(2)}) copy-start(bf16[4,4096,384]{2,1,0:T(8,128)(2,1)} %refs_4_.3) | copy-start | bytes 37748740
  1.1 7.0 %collective-permute-start.2 = (bf16[4,4352]{1,0:T(4,128)(2,1)S(1)}, bf16[4,4352]{1,0:T(4,128)(2,1)S(1)}, u32[]{:S(2)}, u32[]{:S(2)}) collective-permute-start(bf16[4,4352]{1,0:T(4,128)(2,1)S(1)} %prepare.1.refs_0_), channel_id=1, source_target_pairs={{0,12},{4,8},{8,4},{12,0},{1,13},{5,9},{9,5},{13,1},{2,14},{6,10},... | collective-permute-start | bytes 104456 | tf_op jit(solution)/shard_map/ppermute | solution.py:190
  6.2 4.8 %collective-permute-start.1 = (bf16[4,4352]{1,0:T(4,128)(2,1)S(1)}, bf16[4,4352]{1,0:T(4,128)(2,1)S(1)}, u32[]{:S(2)}, u32[]{:S(2)}) collective-permute-start(bf16[4,4352]{1,0:T(4,128)(2,1)S(1)} %prepare.1.refs_0_), channel_id=1, source_target_pairs={{0,8},{4,12},{8,0},{12,4},{1,9},{5,13},{9,1},{13,5},{2,10},{6,14},... | collective-permute-start | bytes 104456 | tf_op jit(solution)/shard_map/ppermute | solution.py:190
  6.2 4.8 %collective-permute-start = (bf16[4,4352]{1,0:T(4,128)(2,1)S(1)}, bf16[4,4352]{1,0:T(4,128)(2,1)S(1)}, u32[]{:S(2)}, u32[]{:S(2)}) collective-permute-start(bf16[4,4352]{1,0:T(4,128)(2,1)S(1)} %prepare.1.refs_0_), channel_id=1, source_target_pairs={{0,4},{4,0},{8,12},{12,8},{1,5},{5,1},{9,13},{13,9},{2,6},{6,2},{1... | collective-permute-start | bytes 104456 | tf_op jit(solution)/shard_map/ppermute | solution.py:190
  11.0 19.0 %slice-start = ((s8[12582912]{0:T(1024)(128)(4,1)}), s8[4194304]{0:T(1024)(128)(4,1)S(1)}, s32[]{:S(2)}) async-start(s8[12582912]{0:T(1024)(128)(4,1)} %bitcast.2), calls=%async_computation | async-start | bytes 8388608
  11.1 18.9 %slice-start.1 = ((s8[12582912]{0:T(1024)(128)(4,1)}), s8[4194304]{0:T(1024)(128)(4,1)S(1)}, s32[]{:S(2)}) async-start(s8[12582912]{0:T(1024)(128)(4,1)} %bitcast.2), calls=%async_computation.1 | async-start | bytes 8388608
  11.1 18.9 %slice-start.2 = ((s8[12582912]{0:T(1024)(128)(4,1)}), s8[4194304]{0:T(1024)(128)(4,1)S(1)}, s32[]{:S(2)}) async-start(s8[12582912]{0:T(1024)(128)(4,1)} %bitcast.2), calls=%async_computation.2 | async-start | bytes 8388608
  11.1 18.9 %copy-start.2 = (bf16[4,2,16,4096]{3,2,1,0:T(8,128)(2,1)S(1)}, bf16[4,2,16,4096]{3,2,1,0:T(8,128)(2,1)}, u32[]{:S(2)}) copy-start(bf16[4,2,16,4096]{3,2,1,0:T(8,128)(2,1)} %param.19) | copy-start | bytes 3145732
  11.1 18.9 %copy-start.3 = (bf16[4,2,16,1536]{3,2,1,0:T(8,128)(2,1)S(1)}, bf16[4,2,16,1536]{3,2,1,0:T(8,128)(2,1)}, u32[]{:S(2)}) copy-start(bf16[4,2,16,1536]{3,2,1,0:T(8,128)(2,1)} %param.18) | copy-start | bytes 1179652
  11.1 5.1 %collective-permute-start.3 = (bf16[16,4352]{1,0:T(8,128)(2,1)S(1)}, bf16[16,4352]{1,0:T(8,128)(2,1)S(1)}, u32[]{:S(2)}, u32[]{:S(2)}) collective-permute-start(bf16[16,4352]{1,0:T(8,128)(2,1)S(1)} %shard_map.109.refs_0_), channel_id=1, source_target_pairs={{0,2},{1,3},{2,0},{3,1},{4,6},{5,7},{6,4},{7,5},{8,10},{9,11},{10,... | collective-permute-start | bytes 417800 | tf_op jit(solution)/shard_map/ppermute | solution.py:190
  12.7 3.6 %collective-permute-start.4 = (bf16[16,4352]{1,0:T(8,128)(2,1)S(1)}, bf16[16,4352]{1,0:T(8,128)(2,1)S(1)}, u32[]{:S(2)}, u32[]{:S(2)}) collective-permute-start(bf16[16,4352]{1,0:T(8,128)(2,1)S(1)} %shard_map.109.refs_0_), channel_id=1, source_target_pairs={{0,1},{1,0},{2,3},{3,2},{4,5},{5,4},{6,7},{7,6},{8,9},{9,8},{10,11... | collective-permute-start | bytes 417800 | tf_op jit(solution)/shard_map/ppermute | solution.py:190
  16.2 1.4 %collective-permute-start.5 = (bf16[16,4352]{1,0:T(8,128)(2,1)S(1)}, bf16[16,4352]{1,0:T(8,128)(2,1)S(1)}, u32[]{:S(2)}, u32[]{:S(2)}) collective-permute-start(bf16[16,4352]{1,0:T(8,128)(2,1)S(1)} %collective-permute-done.3.refs_1_), channel_id=1, source_target_pairs={{0,1},{1,0},{2,3},{3,2},{4,5},{5,4},{6,7},{7,6},{8,9},{9,8},{10,11... | collective-permute-start | bytes 417800 | tf_op jit(solution)/shard_map/ppermute | solution.py:190
  21.6 7.0 %collective-permute-start.6 = (bf16[4,64,384]{2,1,0:T(8,128)(2,1)S(1)}, bf16[4,64,384]{2,1,0:T(8,128)(2,1)S(1)}, u32[]{:S(2)}, u32[]{:S(2)}) collective-permute-start(bf16[4,64,384]{2,1,0:T(8,128)(2,1)S(1)} %get-tuple-element.15.refs_0_), channel_id=1, source_target_pairs={{0,2},{1,3},{2,0},{3,1},{4,6},{5,7},{6,4},{7,5},{8,10},{9,11},{10,... | collective-permute-start | bytes 589832 | tf_op jit(solution)/shard_map/ppermute | solution.py:190
  23.1 5.5 %collective-permute-start.7 = (bf16[4,64,384]{2,1,0:T(8,128)(2,1)S(1)}, bf16[4,64,384]{2,1,0:T(8,128)(2,1)S(1)}, u32[]{:S(2)}, u32[]{:S(2)}) collective-permute-start(bf16[4,64,384]{2,1,0:T(8,128)(2,1)S(1)} %get-tuple-element.15.refs_0_), channel_id=1, source_target_pairs={{0,1},{1,0},{2,3},{3,2},{4,5},{5,4},{6,7},{7,6},{8,9},{9,8},{10,11... | collective-permute-start | bytes 589832 | tf_op jit(solution)/shard_map/ppermute | solution.py:190
  28.6 1.4 %collective-permute-start.8 = (bf16[4,64,384]{2,1,0:T(8,128)(2,1)S(1)}, bf16[4,64,384]{2,1,0:T(8,128)(2,1)S(1)}, u32[]{:S(2)}, u32[]{:S(2)}) collective-permute-start(bf16[4,64,384]{2,1,0:T(8,128)(2,1)S(1)} %collective-permute-done.6.refs_1_), channel_id=1, source_target_pairs={{0,1},{1,0},{2,3},{3,2},{4,5},{5,4},{6,7},{7,6},{8,9},{9,8},{10,11... | collective-permute-start | bytes 589832 | tf_op jit(solution)/shard_map/ppermute | solution.py:190
  33.2 1.6 %collective-permute-start.9 = (bf16[32,4096]{1,0:T(8,128)(2,1)S(1)}, bf16[32,4096]{1,0:T(8,128)(2,1)S(1)}, u32[]{:S(2)}, u32[]{:S(2)}) collective-permute-start(bf16[32,4096]{1,0:T(8,128)(2,1)S(1)} %get-tuple-element.18), channel_id=1, source_target_pairs={{0,1},{1,0},{2,3},{3,2},{4,5},{5,4},{6,7},{7,6},{8,9},{9,8},{10,11... | collective-permute-start | bytes 786440 | tf_op jit(solution)/shard_map/ppermute | solution.py:190
  34.9 5.6 %collective-permute-start.10 = (bf16[16,4096]{1,0:T(8,128)(2,1)S(1)}, bf16[16,4096]{1,0:T(8,128)(2,1)S(1)}, u32[]{:S(2)}, u32[]{:S(2)}) collective-permute-start(bf16[16,4096]{1,0:T(8,128)(2,1)S(1)} %get-tuple-element.20), channel_id=1, source_target_pairs={{0,2},{1,3},{2,0},{3,1},{4,6},{5,7},{6,4},{7,5},{8,10},{9,11},{10,... | collective-permute-start | bytes 393224 | tf_op jit(solution)/shard_map/ppermute | solution.py:190
  40.5 4.5 %collective-permute-start.11 = (bf16[4,4096]{1,0:T(4,128)(2,1)S(1)}, bf16[4,4096]{1,0:T(4,128)(2,1)S(1)}, u32[]{:S(2)}, u32[]{:S(2)}) collective-permute-start(bf16[4,4096]{1,0:T(4,128)(2,1)S(1)} %get-tuple-element.22), channel_id=1, source_target_pairs={{0,4},{4,0},{8,12},{12,8},{1,5},{5,1},{9,13},{13,9},{2,6},{6,2},{1... | collective-permute-start | bytes 98312 | tf_op jit(solution)/shard_map/ppermute | solution.py:190
  40.6 4.9 %collective-permute-start.12 = (bf16[4,4096]{1,0:T(4,128)(2,1)S(1)}, bf16[4,4096]{1,0:T(4,128)(2,1)S(1)}, u32[]{:S(2)}, u32[]{:S(2)}) collective-permute-start(bf16[4,4096]{1,0:T(4,128)(2,1)S(1)} %get-tuple-element.23), channel_id=1, source_target_pairs={{0,8},{4,12},{8,0},{12,4},{1,9},{5,13},{9,1},{13,5},{2,10},{6,14},... | collective-permute-start | bytes 98312 | tf_op jit(solution)/shard_map/ppermute | solution.py:190
  42.7 5.7 %collective-permute-start.13 = (bf16[4,4096]{1,0:T(4,128)(2,1)S(1)}, bf16[4,4096]{1,0:T(4,128)(2,1)S(1)}, u32[]{:S(2)}, u32[]{:S(2)}) collective-permute-start(bf16[4,4096]{1,0:T(4,128)(2,1)S(1)} %get-tuple-element.24), channel_id=1, source_target_pairs={{0,12},{4,8},{8,4},{12,0},{1,13},{5,9},{9,5},{13,1},{2,14},{6,10},... | collective-permute-start | bytes 98312 | tf_op jit(solution)/shard_map/ppermute | solution.py:190

commit v3 on v2

--- a/solution.py
+++ b/solution.py
@@ -83,7 +83,11 @@
     out[...] = jnp.concatenate([r[...].astype(F32) for r in refs[:count]], axis=0).astype(BF)
 
 
-def up_kernel(count, *refs):
+def relay(x, *refs):
+    refs[-1][...] = x[...]
+
+
+def up_kernel(count, picked, *refs):
     x_refs = refs[:count]
     gate, up, h, slots, xs = refs[count:]
     experts, width = gate.shape[0], gate.shape[1]
@@ -95,7 +99,7 @@
     slots[...] = jnp.concatenate([r[:, width + LANES :] for r in x_refs], axis=0)
     lane = lax.broadcasted_iota(jnp.int32, meta.shape, 1)
     step = 256
-    for e in range(experts):
+    for i, e in enumerate(picked):
         w = jnp.sum(
             jnp.where(lane & (EXPERTS - 1) == first + e, meta, 0.0), axis=1, keepdims=True
         )
@@ -104,48 +108,75 @@
             x = xs[:, k : k + step]
             a += jnp.dot(x, gate[e, k : k + step], preferred_element_type=F32)
             b += jnp.dot(x, up[e, k : k + step], preferred_element_type=F32)
-        h[e] = (a * jax.nn.sigmoid(a) * b * w).astype(BF)
-
-
-def down_kernel(offs, block, *refs):
+        h[i] = (a * jax.nn.sigmoid(a) * b * w).astype(BF)
+
+
+def columns(ref, spot, size):
+    if size % LANES == 0:
+        return ref[:, pl.ds(pl.multiple_of(spot * size, size), size)]
+    picked = ref[:, :size]
+    for c in range(1, ref.shape[1] // size):
+        picked = jnp.where(spot == c, ref[:, c * size : (c + 1) * size], picked)
+    return picked
+
+
+def down_kernel(offs, block, terms, opens, closes, *refs):
     n = len(offs)
-    h_refs, refs = refs[:n], refs[n:]
-    slots_ref, down, shrink, expand, keep, send, hs = refs
+    pairs, refs = refs[: 2 * len(terms)], refs[2 * len(terms) :]
+    down, shrink, refs = refs[0], refs[1], refs[2:]
+    base = small = None
+    if not opens:
+        base, small, refs = refs[0][...], refs[1][...], refs[2:]
     me = lax.axis_index("dp")
-    experts, rows, part = h_refs[0].shape
+    odd = lax.rem(me, 2) == 1
+    experts, part = down.shape[0], pairs[0].shape[2]
+    rows, ranks = pairs[0].shape[1], shrink.shape[0]
+    per = ranks // experts
+    lane = lax.broadcasted_iota(jnp.int32, (rows, ranks), 1)
+
+    def ordered(ref, i, m):
+        cuts = [offs.index(o ^ m) * block for o in offs]
+        return jnp.concatenate([ref[i, c : c + block, :] for c in cuts], axis=0)
+
+    for t, (m, picked) in enumerate(terms):
+        pair = (me ^ m) // 2
+        for i, e in enumerate(picked):
+            mine, other = ordered(pairs[2 * t], i, m), ordered(pairs[2 * t + 1], i, m ^ 1)
+            x = [jnp.where(odd, other, mine), jnp.where(odd, mine, other)]
+            if part % LANES == 0:
+                x = [jnp.concatenate(x, axis=1)]
+            for j, piece in enumerate(x):
+                spot, size = pair * len(x) + j, piece.shape[1]
+                here = pl.ds(pl.multiple_of(spot * size, size), size)
+                term = jnp.dot(piece, down[e, here, :], preferred_element_type=F32)
+                base = term if base is None else base + term
+                term = lax.dot_general(
+                    piece,
+                    columns(shrink, spot, size),
+                    (((1,), (1,)), ((), ())),
+                    preferred_element_type=F32,
+                )
+                inside = (lane >= e * per) & (lane < (e + 1) * per)
+                term = jnp.where(inside, term, 0.0)
+                small = term if small is None else small + term
+    if not closes:
+        refs[0][...] = base
+        refs[1][...] = small
+        return
+    slots, expand, keep, send = refs
     first = lax.axis_index("expert") * experts
-    for i, m in enumerate(offs):
-        for p in range(n):
-            q = offs.index(offs[p] ^ m)
-            hs[me ^ m, :, p * block : (p + 1) * block, :] = h_refs[i][
-                :, q * block : (q + 1) * block, :
-            ]
-    per = shrink.shape[0] // experts
+    values = slots[...].astype(F32)
+    lane16 = lax.broadcasted_iota(jnp.int32, values.shape, 1)
     rank = per // SLOTS
-    slot_values = slots_ref[...].astype(F32)
-    lane16 = lax.broadcasted_iota(jnp.int32, slot_values.shape, 1)
-    lane = lax.broadcasted_iota(jnp.int32, (rows, shrink.shape[0]), 1)
-    wanted = me * SLOTS + (lane % per) // rank
-    base = None
-    small = jnp.zeros((rows, shrink.shape[0]), F32)
-    joined = part % LANES == 0
+    chosen = jnp.full((rows, ranks), -1.0, F32)
     for e in range(experts):
-        chosen = jnp.sum(
-            jnp.where(lane16 == first + e, slot_values, 0.0), axis=1, keepdims=True
-        ).astype(jnp.int32)
-        pieces = [hs[c, e] for c in range(n)]
-        cuts = [(c * part, (c + 1) * part) for c in range(n)]
-        if joined:
-            pieces, cuts = [jnp.concatenate(pieces, axis=1)], [(0, n * part)]
-        full = jnp.zeros((rows, shrink.shape[0]), F32)
-        for x, (lo, hi) in zip(pieces, cuts):
-            term = jnp.dot(x, down[e, lo:hi, :], preferred_element_type=F32)
-            base = term if base is None else base + term
-            full += lax.dot_general(
-                x, shrink[:, lo:hi], (((1,), (1,)), ((), ())), preferred_element_type=F32
-            )
-        small = jnp.where((lane // per == e) & (chosen == wanted), full, small)
-    small = small.astype(BF)
+        value = jnp.sum(jnp.where(lane16 == first + e, values, 0.0), axis=1, keepdims=True)
+        for s in range(SLOTS):
+            low_lane = e * per + s * rank
+            inside = (lane >= low_lane) & (lane < low_lane + rank)
+            mine = (me * SLOTS + s).astype(F32)
+            chosen = jnp.where(inside, value - mine, chosen)
+    small = jnp.where(chosen == 0.0, small, 0.0).astype(BF)
     cols = base.shape[1]
     half = rows // 2
     for c in range(n):
@@ -188,6 +219,15 @@
     def over(x, axis, m):
         size = lax.axis_size(axis)
         return lax.ppermute(x, axis, [(i, i ^ m) for i in range(size)])
+
+    def passed(x, behind):
+        return call(
+            relay,
+            jax.ShapeDtypeStruct(x.shape, x.dtype),
+            (x, *behind),
+            [VM] * (1 + len(behind)),
+            roomy + 2 * size_of(x, *behind),
+        )
 
     roomy = 16 << 20
     inputs = (tenant_ids, tokens, expert_ids, route_weight, owner, slot)
@@ -209,8 +249,8 @@
         call(
             functools.partial(join, n_z),
             jax.ShapeDtypeStruct((block, wide), BF),
-            (y, *got),
-            [VM] * n_z,
+            (y, *got, in_hbm(gate), in_hbm(up), in_hbm(down)),
+            [VM] * n_z + [HB] * 3,
             roomy,
         )
     ]
@@ -224,37 +264,69 @@
         blocks = blocks + [over(a, "dp", b) for a in blocks]
         offs = offs + [o ^ b for o in offs]
     x_bytes = all_rows * wide * 2
-    with jax.named_scope("up"):
-        h, slots = call(
-            functools.partial(up_kernel, n_dp),
-            (
-                jax.ShapeDtypeStruct((experts, all_rows, part), BF),
-                jax.ShapeDtypeStruct((all_rows, LANES), BF),
-            ),
-            (*blocks, in_vmem(gate), in_vmem(up)),
-            [VM] * n_dp + [VM, VM],
-            (8 << 20) + 3 * x_bytes,
-            scratch=(pltpu.VMEM((all_rows, width), BF),),
-        )
-
-    chunks = [h]
-    for b in bits:
-        chunks = chunks + [over(a, "dp", b) for a in chunks]
+    lists = [list(range(experts))]
+    if experts > 1:
+        lists = [lists[0][: experts // 2], lists[0][experts // 2 :]]
+    hidden = []
+    for picked in lists:
+        with jax.named_scope("up"):
+            h, slots = call(
+                functools.partial(up_kernel, n_dp, picked),
+                (
+                    jax.ShapeDtypeStruct((len(picked), all_rows, part), BF),
+                    jax.ShapeDtypeStruct((all_rows, LANES), BF),
+                ),
+                (*blocks, in_vmem(gate), in_vmem(up)),
+                [VM] * (n_dp + 2),
+                (8 << 20) + 3 * x_bytes,
+                scratch=(pltpu.VMEM((all_rows, width), BF),),
+            )
+        hidden.append({0: h})
+    for b in bits[:-1]:
+        for got in hidden:
+            got.update({m ^ b: over(a, "dp", b) for m, a in got.items()})
+
+    def between_cores(got, pairs, behind=()):
+        for m in pairs:
+            x = passed(got[m], behind) if behind else got[m]
+            got[m ^ 1] = over(x, "dp", 1)
+
+    others = list(range(2, n_dp, 2))
+    for got in hidden:
+        between_cores(got, [0] if got is hidden[-1] else [0, *others])
+
     shrink2 = shrink.reshape(-1, shrink.shape[-1])
     expand2 = expand.reshape(-1, expand.shape[-1])
     h_bytes = experts * all_rows * n_dp * max(part, LANES) * 2
-    with jax.named_scope("down"):
-        keep, send = call(
-            functools.partial(down_kernel, offs, block),
-            (
-                jax.ShapeDtypeStruct((all_rows // 2, width), F32),
-                jax.ShapeDtypeStruct((all_rows // 2, width), BF),
-            ),
-            (*chunks, slots, in_vmem(down), shrink2, expand2),
-            [VM] * (n_dp + 4),
-            (8 << 20) + 3 * h_bytes + all_rows * width * 4,
-            scratch=(pltpu.VMEM((n_dp, experts, all_rows, part), BF),),
-        )
+    cols = down.shape[2]
+    sums = (
+        jax.ShapeDtypeStruct((all_rows, cols), F32),
+        jax.ShapeDtypeStruct((all_rows, shrink2.shape[0]), F32),
+    )
+    halves = (
+        jax.ShapeDtypeStruct((all_rows // 2, width), F32),
+        jax.ShapeDtypeStruct((all_rows // 2, width), BF),
+    )
+    steps = [[(0, i) for i in range(len(lists))]]
+    for i in range(len(lists)):
+        steps.append([(m, i) for m in others])
+    carried = ()
+    for s, step in enumerate(steps):
+        opens, closes = s == 0, s == len(steps) - 1
+        if s == min(1, len(steps) - 1):
+            between_cores(hidden[-1], others, carried)
+        arrays = [a for m, i in step for a in (hidden[i][m], hidden[i][m ^ 1])]
+        terms = [(m, lists[i]) for m, i in step]
+        last = (slots, expand2) if closes else ()
+        with jax.named_scope("down"):
+            carried = call(
+                functools.partial(down_kernel, offs, block, terms, opens, closes),
+                halves if closes else sums,
+                (*arrays, in_vmem(down), shrink2, *carried, *last),
+                [VM] * (len(arrays) + 2 + len(carried) + len(last)),
+                (8 << 20) + 2 * h_bytes + 2 * all_rows * width * 4,
+            )
+    keep, send = carried
 
     for b in bits[::-1][:-1]:
         arrived = over(send, "dp", b)
@@ -280,7 +352,7 @@
         [VM, VM],
         roomy + 4 * size_of(keep),
     )
-    back = [over(s, "expert", k + 1) for k, s in enumerate(sends)]
+    back = [over(sends[k - 1], "expert", k) for k in range(n_z - 1, 0, -1)]
     return call(
         finish,
         jax.ShapeDtypeStruct((rows, width), BF),

time: 49.2 us -> 46.4 us (0.943)
  waiting for transfers between devices: 24.9 us -> 20.9 us
  Pallas kernels: 8.92 us -> 9.71 us
    ppermute x14 -> x17, waiting for transfers between devices: 24.9 us -> 20.9 us  [over(): return lax.ppermute(x, axis, [(i, i ^ m) for i in range(size)])]
    pallas_call x7 -> x11, Pallas kernels: 8.92 us -> 9.71 us  [call(): pl.pallas_call(body, out_shape=out_shape, in_specs=specs, out_specs=jax.t...]
    ppermute x14 -> x17, starting transfers between devices: 15.1 us -> 15.3 us  [over(): return lax.ppermute(x, axis, [(i, i ^ m) for i in range(size)])]
  transfers between devices with their start and end apart: 14 -> 17, of which waited for: 10 -> 13; matrix products, arithmetic and copies ran while one was open for 0% -> 0% of each run, Pallas kernels for 0% -> 9%
where the time goes in v3:
time: 46.4 us; the launch traced here: 46.2 us
  waiting for transfers between devices  20.9 us (45%)
  starting transfers between devices  15.3 us (33%)
  Pallas kernels  9.71 us (21%)
    ppermute x17, waiting for transfers between devices, over(): return lax.ppermute(x, axis, [(i, i ^ m) for i in range(size)])  20.9 us
    ppermute x17, starting transfers between devices, over(): return lax.ppermute(x, axis, [(i, i ^ m) for i in range(size)])  15.3 us
    pallas_call x11, Pallas kernels, call(): pl.pallas_call(body, out_shape=out_shape, in_specs=specs, out_specs=jax.t...  9.71 us
  transfers between devices with their start and end apart: 17, of which 13 were waited for; matrix products, arithmetic and copies ran while one was open for 0% of the time, Pallas kernels for 9%

profile of v3, /device:TPU:0, one launch (start us, length us, event | category | flops | bytes accessed | tf_op | source)
XLA Modules:
  0.0 46.2 jit_solution(1016085327563189295)
XLA Ops:
  0.0 1.1 %prepare.1.refs_0_ = bf16[4,4352]{1,0:T(4,128)(2,1)S(1)} custom-call(s32[4]{0:T(128)} %refs_0_.1, bf16[4,4096]{1,0:T(4,128)(2,1)} %refs_1_.1, s32[4,8]{1,0:T(4,128)} %refs_2_.3, f32[4,8]{1,0:T(4,128)} %refs_3_.1, s32[8,16]{1,0:T(8,128)} %refs_4_.5, s32[8,16]{1,0:T(8,128)} %refs_5_.4, bf16[4,4096,384]{2,1,0:T(8,128)(2,1)} %refs_4_.8, ...), custom_call_target="tpu_custom_call" | custom-call | tf_op jit(solution)/shard_map/prepare/pallas_call | solution.py:30
  1.1 5.1 %collective-permute-start.2 = (bf16[4,4352]{1,0:T(4,128)(2,1)S(1)}, bf16[4,4352]{1,0:T(4,128)(2,1)S(1)}, u32[]{:S(2)}, u32[]{:S(2)}) collective-permute-start(bf16[4,4352]{1,0:T(4,128)(2,1)S(1)} %prepare.1.refs_0_), channel_id=1, source_target_pairs={{0,12},{4,8},{8,4},{12,0},{1,13},{5,9},{9,5},{13,1},{2,14},{6,10},... | collective-permute-start | bytes 104456 | tf_op jit(solution)/shard_map/ppermute | solution.py:221
  6.2 0.6 %collective-permute-start = (bf16[4,4352]{1,0:T(4,128)(2,1)S(1)}, bf16[4,4352]{1,0:T(4,128)(2,1)S(1)}, u32[]{:S(2)}, u32[]{:S(2)}) collective-permute-start(bf16[4,4352]{1,0:T(4,128)(2,1)S(1)} %prepare.1.refs_0_), channel_id=1, source_target_pairs={{0,4},{4,0},{8,12},{12,8},{1,5},{5,1},{9,13},{13,9},{2,6},{6,2},{1... | collective-permute-start | bytes 104456 | tf_op jit(solution)/shard_map/ppermute | solution.py:221
  6.9 1.3 %collective-permute-done.2.refs_3_ = bf16[4,4352]{1,0:T(4,128)(2,1)S(1)} collective-permute-done((bf16[4,4352]{1,0:T(4,128)(2,1)S(1)}, bf16[4,4352]{1,0:T(4,128)(2,1)S(1)}, u32[]{:S(2)}, u32[]{:S(2)}) %collective-permute-start.2) | collective-permute-done | bytes 34848 | tf_op jit(solution)/shard_map/ppermute | solution.py:221
  8.2 2.9 %collective-permute-done.1.refs_2_ = bf16[4,4352]{1,0:T(4,128)(2,1)S(1)} collective-permute-done((bf16[4,4352]{1,0:T(4,128)(2,1)S(1)}, bf16[4,4352]{1,0:T(4,128)(2,1)S(1)}, u32[]{:S(2)}, u32[]{:S(2)}) %collective-permute-start.1) | collective-permute-done | bytes 34848 | tf_op jit(solution)/shard_map/ppermute | solution.py:221
  11.1 1.6 %collective-permute-start.3 = (bf16[16,4352]{1,0:T(8,128)(2,1)S(1)}, bf16[16,4352]{1,0:T(8,128)(2,1)S(1)}, u32[]{:S(2)}, u32[]{:S(2)}) collective-permute-start(bf16[16,4352]{1,0:T(8,128)(2,1)S(1)} %shard_map.109.refs_0_), channel_id=1, source_target_pairs={{0,2},{1,3},{2,0},{3,1},{4,6},{5,7},{6,4},{7,5},{8,10},{9,11},{10,... | collective-permute-start | bytes 417800 | tf_op jit(solution)/shard_map/ppermute | solution.py:221
  12.7 3.6 %collective-permute-done.3.refs_1_ = bf16[16,4352]{1,0:T(8,128)(2,1)S(1)} collective-permute-done((bf16[16,4352]{1,0:T(8,128)(2,1)S(1)}, bf16[16,4352]{1,0:T(8,128)(2,1)S(1)}, u32[]{:S(2)}, u32[]{:S(2)}) %collective-permute-start.3) | collective-permute-done | bytes 139296 | tf_op jit(solution)/shard_map/ppermute | solution.py:221
  16.3 1.4 %collective-permute-done.5.refs_3_ = bf16[16,4352]{1,0:T(8,128)(2,1)S(1)} collective-permute-done((bf16[16,4352]{1,0:T(8,128)(2,1)S(1)}, bf16[16,4352]{1,0:T(8,128)(2,1)S(1)}, u32[]{:S(2)}, u32[]{:S(2)}) %collective-permute-start.5) | collective-permute-done | bytes 139296 | tf_op jit(solution)/shard_map/ppermute | solution.py:221
  17.7 2.5 %up.3 = (bf16[2,64,384]{2,1,0:T(8,128)(2,1)S(1)}, bf16[64,128]{1,0:T(8,128)(2,1)}) custom-call(bf16[16,4352]{1,0:T(8,128)(2,1)S(1)} %shard_map.109.refs_0_, bf16[16,4352]{1,0:T(8,128)(2,1)S(1)} %collective-permute-done.3.refs_1_, bf16[16,4352]{1,0:T(8,128)(2,1)S(1)} %collective-permute-done.4.refs_2_, bf16[16,4352]{1,0:T(8,128)(2,1)S(1)} %collective-permute-done.5.refs_3_, ...), custom_call_target="tpu_custom_call" | custom-call | tf_op jit(solution)/shard_map/up/pallas_call | solution.py:30
  20.1 1.6 %collective-permute-start.10 = (bf16[2,64,384]{2,1,0:T(8,128)(2,1)S(1)}, bf16[2,64,384]{2,1,0:T(8,128)(2,1)S(1)}, u32[]{:S(2)}, u32[]{:S(2)}) collective-permute-start(bf16[2,64,384]{2,1,0:T(8,128)(2,1)S(1)} %get-tuple-element.21.refs_0_), channel_id=1, source_target_pairs={{0,2},{1,3},{2,0},{3,1},{4,6},{5,7},{6,4},{7,5},{8,10},{9,11},{10,... | collective-permute-start | bytes 294920 | tf_op jit(solution)/shard_map/ppermute | solution.py:221
  21.7 2.0 %up.2 = (bf16[2,64,384]{2,1,0:T(8,128)(2,1)S(1)}, bf16[64,128]{1,0:T(8,128)(2,1)S(1)}) custom-call(bf16[16,4352]{1,0:T(8,128)(2,1)S(1)} %shard_map.109.refs_0_, bf16[16,4352]{1,0:T(8,128)(2,1)S(1)} %collective-permute-done.3.refs_1_, bf16[16,4352]{1,0:T(8,128)(2,1)S(1)} %collective-permute-done.4.refs_2_, ...), custom_call_target="tpu_custom_call" | custom-call | tf_op jit(solution)/shard_map/up/pallas_call | solution.py:30
  24.3 0.5 %collective-permute-start.6 = (bf16[2,64,384]{2,1,0:T(8,128)(2,1)S(1)}, bf16[2,64,384]{2,1,0:T(8,128)(2,1)S(1)}, u32[]{:S(2)}, u32[]{:S(2)}) collective-permute-start(bf16[2,64,384]{2,1,0:T(8,128)(2,1)S(1)} %get-tuple-element.20.refs_2_), channel_id=1, source_target_pairs={{0,2},{1,3},{2,0},{3,1},{4,6},{5,7},{6,4},{7,5},{8,10},{9,11},{10,... | collective-permute-start | bytes 294920 | tf_op jit(solution)/shard_map/ppermute | solution.py:221
  25.3 1.5 %down.3 = (f32[64,1024]{1,0:T(8,128)S(1)}, f32[64,128]{1,0:T(8,128)S(1)}) custom-call(bf16[2,64,384]{2,1,0:T(8,128)(2,1)S(1)} %get-tuple-element.21.refs_0_, bf16[2,64,384]{2,1,0:T(8,128)(2,1)S(1)} %collective-permute-done.7.refs_1_, bf16[2,64,384]{2,1,0:T(8,128)(2,1)S(1)} %get-tuple-element.20.refs_2_, ...), custom_call_target="tpu_custom_call" | custom-call | tf_op jit(solution)/shard_map/down/pallas_call | solution.py:30
  26.8 2.3 %collective-permute-done.6.x.refs_0_ = bf16[2,64,384]{2,1,0:T(8,128)(2,1)S(1)} collective-permute-done((bf16[2,64,384]{2,1,0:T(8,128)(2,1)S(1)}, bf16[2,64,384]{2,1,0:T(8,128)(2,1)S(1)}, u32[]{:S(2)}, u32[]{:S(2)}) %collective-permute-start.6) | collective-permute-done | bytes 98336 | tf_op jit(solution)/shard_map/ppermute | solution.py:221
  29.2 0.8 %down.4 = (f32[64,1024]{1,0:T(8,128)S(1)}, f32[64,128]{1,0:T(8,128)S(1)}) custom-call(bf16[2,64,384]{2,1,0:T(8,128)(2,1)S(1)} %collective-permute-done.10.refs_0_, bf16[2,64,384]{2,1,0:T(8,128)(2,1)S(1)} %collective-permute-done.11.refs_1_, bf16[4,1536,1024]{2,1,0:T(8,128)(2,1)S(1)} %bitcast.3, bf16[128,1536]{1,0:T(8,128)(2,1)S(1)} %bitcast.11, ...), custom_call_target="tpu_custom_call" | custom-call | tf_op jit(solution)/shard_map/down/pallas_call | solution.py:30
  30.5 1.1 %down.5 = (f32[32,4096]{1,0:T(8,128)S(1)}, bf16[32,4096]{1,0:T(8,128)(2,1)S(1)}) custom-call(bf16[2,64,384]{2,1,0:T(8,128)(2,1)S(1)} %collective-permute-done.6.x.refs_0_, bf16[2,64,384]{2,1,0:T(8,128)(2,1)S(1)} %collective-permute-done.9.refs_1_, bf16[4,1536,1024]{2,1,0:T(8,128)(2,1)S(1)} %bitcast.3, bf16[128,1536]{1,0:T(8,128)(2,1)S(1)} %bitcast.12, ...), custom_call_target="tpu_custom_call" | custom-call | tf_op jit(solution)/shard_map/down/pallas_call | solution.py:30
  31.8 1.4 %collective-permute-done.12.got = bf16[32,4096]{1,0:T(8,128)(2,1)S(1)} collective-permute-done((bf16[32,4096]{1,0:T(8,128)(2,1)S(1)}, bf16[32,4096]{1,0:T(8,128)(2,1)S(1)}, u32[]{:S(2)}, u32[]{:S(2)}) %collective-permute-start.12) | collective-permute-done | bytes 262176 | tf_op jit(solution)/shard_map/ppermute | solution.py:221
  33.2 0.6 %collective-permute-start.13 = (bf16[16,4096]{1,0:T(8,128)(2,1)S(1)}, bf16[16,4096]{1,0:T(8,128)(2,1)S(1)}, u32[]{:S(2)}, u32[]{:S(2)}) collective-permute-start(bf16[16,4096]{1,0:T(8,128)(2,1)S(1)} %get-tuple-element.30), channel_id=1, source_target_pairs={{0,2},{1,3},{2,0},{3,1},{4,6},{5,7},{6,4},{7,5},{8,10},{9,11},{10,... | collective-permute-start | bytes 393224 | tf_op jit(solution)/shard_map/ppermute | solution.py:221
  33.8 5.0 %collective-permute-done.13.got = bf16[16,4096]{1,0:T(8,128)(2,1)S(1)} collective-permute-done((bf16[16,4096]{1,0:T(8,128)(2,1)S(1)}, bf16[16,4096]{1,0:T(8,128)(2,1)S(1)}, u32[]{:S(2)}, u32[]{:S(2)}) %collective-permute-start.13) | collective-permute-done | bytes 131104 | tf_op jit(solution)/shard_map/ppermute | solution.py:221
  38.9 1.5 %collective-permute-start.14 = (bf16[4,4096]{1,0:T(4,128)(2,1)S(1)}, bf16[4,4096]{1,0:T(4,128)(2,1)S(1)}, u32[]{:S(2)}, u32[]{:S(2)}) collective-permute-start(bf16[4,4096]{1,0:T(4,128)(2,1)S(1)} %get-tuple-element.32), channel_id=1, source_target_pairs={{0,12},{4,8},{8,4},{12,0},{1,13},{5,9},{9,5},{13,1},{2,14},{6,10},... | collective-permute-start | bytes 98312 | tf_op jit(solution)/shard_map/ppermute | solution.py:221
  40.4 0.6 %collective-permute-start.15 = (bf16[4,4096]{1,0:T(4,128)(2,1)S(1)}, bf16[4,4096]{1,0:T(4,128)(2,1)S(1)}, u32[]{:S(2)}, u32[]{:S(2)}) collective-permute-start(bf16[4,4096]{1,0:T(4,128)(2,1)S(1)} %get-tuple-element.33), channel_id=1, source_target_pairs={{0,8},{4,12},{8,0},{12,4},{1,9},{5,13},{9,1},{13,5},{2,10},{6,14},... | collective-permute-start | bytes 98312 | tf_op jit(solution)/shard_map/ppermute | solution.py:221
  41.0 2.3 %collective-permute-start.16 = (bf16[4,4096]{1,0:T(4,128)(2,1)S(1)}, bf16[4,4096]{1,0:T(4,128)(2,1)S(1)}, u32[]{:S(2)}, u32[]{:S(2)}) collective-permute-start(bf16[4,4096]{1,0:T(4,128)(2,1)S(1)} %get-tuple-element.34), channel_id=1, source_target_pairs={{0,4},{4,0},{8,12},{12,8},{1,5},{5,1},{9,13},{13,9},{2,6},{6,2},{1... | collective-permute-start | bytes 98312 | tf_op jit(solution)/shard_map/ppermute | solution.py:221
  43.3 1.5 %collective-permute-done.14.refs_0_ = bf16[4,4096]{1,0:T(4,128)(2,1)S(1)} collective-permute-done((bf16[4,4096]{1,0:T(4,128)(2,1)S(1)}, bf16[4,4096]{1,0:T(4,128)(2,1)S(1)}, u32[]{:S(2)}, u32[]{:S(2)}) %collective-permute-start.14) | collective-permute-done | bytes 32800 | tf_op jit(solution)/shard_map/ppermute | solution.py:221
  45.5 0.6 %shard_map.113 = bf16[4,4096]{1,0:T(4,128)(2,1)} custom-call(f32[4,4096]{1,0:T(4,128)S(1)} %get-tuple-element.31.own, bf16[4,4096]{1,0:T(4,128)(2,1)S(1)} %collective-permute-done.14.refs_0_, bf16[4,4096]{1,0:T(4,128)(2,1)S(1)} %collective-permute-done.15.refs_1_, bf16[4,4096]{1,0:T(4,128)(2,1)S(1)} %collective-permute-done.16.refs_2_), custom_call_target="tpu_custom_call" | custom-call | tf_op jit(solution)/shard_map/pallas_call | solution.py:30
  (53 shorter events, 2.7 us)
Async XLA Ops:
  0.0 17.6 %slice-start.3 = ((s8[12582912]{0:T(1024)(128)(4,1)}), s8[4194304]{0:T(1024)(128)(4,1)S(1)}, s32[]{:S(2)}) async-start(s8[12582912]{0:T(1024)(128)(4,1)} %bitcast.4), calls=%async_computation.3 | async-start | bytes 8388608
  0.0 17.6 %slice-start.4 = ((s8[12582912]{0:T(1024)(128)(4,1)}), s8[4194304]{0:T(1024)(128)(4,1)S(1)}, s32[]{:S(2)}) async-start(s8[12582912]{0:T(1024)(128)(4,1)} %bitcast.4), calls=%async_computation.4 | async-start | bytes 8388608
  0.0 17.6 %slice-start.6 = ((s8[12582912]{0:T(1024)(128)(4,1)}), s8[4194304]{0:T(1024)(128)(4,1)S(1)}, s32[]{:S(2)}) async-start(s8[12582912]{0:T(1024)(128)(4,1)} %bitcast.6), calls=%async_computation.6 | async-start | bytes 8388608
  0.0 17.6 %slice-start.7 = ((s8[12582912]{0:T(1024)(128)(4,1)}), s8[4194304]{0:T(1024)(128)(4,1)S(1)}, s32[]{:S(2)}) async-start(s8[12582912]{0:T(1024)(128)(4,1)} %bitcast.6), calls=%async_computation.7 | async-start | bytes 8388608
  1.1 16.6 %slice-start.5 = ((s8[12582912]{0:T(1024)(128)(4,1)}), s8[4194304]{0:T(1024)(128)(4,1)S(1)}, s32[]{:S(2)}) async-start(s8[12582912]{0:T(1024)(128)(4,1)} %bitcast.4), calls=%async_computation.5 | async-start | bytes 8388608
  1.1 16.6 %slice-start.8 = ((s8[12582912]{0:T(1024)(128)(4,1)}), s8[4194304]{0:T(1024)(128)(4,1)S(1)}, s32[]{:S(2)}) async-start(s8[12582912]{0:T(1024)(128)(4,1)} %bitcast.6), calls=%async_computation.8 | async-start | bytes 8388608
  1.1 7.0 %collective-permute-start.2 = (bf16[4,4352]{1,0:T(4,128)(2,1)S(1)}, bf16[4,4352]{1,0:T(4,128)(2,1)S(1)}, u32[]{:S(2)}, u32[]{:S(2)}) collective-permute-start(bf16[4,4352]{1,0:T(4,128)(2,1)S(1)} %prepare.1.refs_0_), channel_id=1, source_target_pairs={{0,12},{4,8},{8,4},{12,0},{1,13},{5,9},{9,5},{13,1},{2,14},{6,10},... | collective-permute-start | bytes 104456 | tf_op jit(solution)/shard_map/ppermute | solution.py:221
  6.2 4.8 %collective-permute-start.1 = (bf16[4,4352]{1,0:T(4,128)(2,1)S(1)}, bf16[4,4352]{1,0:T(4,128)(2,1)S(1)}, u32[]{:S(2)}, u32[]{:S(2)}) collective-permute-start(bf16[4,4352]{1,0:T(4,128)(2,1)S(1)} %prepare.1.refs_0_), channel_id=1, source_target_pairs={{0,8},{4,12},{8,0},{12,4},{1,9},{5,13},{9,1},{13,5},{2,10},{6,14},... | collective-permute-start | bytes 104456 | tf_op jit(solution)/shard_map/ppermute | solution.py:221
  6.2 4.8 %collective-permute-start = (bf16[4,4352]{1,0:T(4,128)(2,1)S(1)}, bf16[4,4352]{1,0:T(4,128)(2,1)S(1)}, u32[]{:S(2)}, u32[]{:S(2)}) collective-permute-start(bf16[4,4352]{1,0:T(4,128)(2,1)S(1)} %prepare.1.refs_0_), channel_id=1, source_target_pairs={{0,4},{4,0},{8,12},{12,8},{1,5},{5,1},{9,13},{13,9},{2,6},{6,2},{1... | collective-permute-start | bytes 104456 | tf_op jit(solution)/shard_map/ppermute | solution.py:221
  11.1 10.6 %slice-start.10 = ((s8[12582912]{0:T(1024)(128)(4,1)}), s8[4194304]{0:T(1024)(128)(4,1)S(1)}, s32[]{:S(2)}) async-start(s8[12582912]{0:T(1024)(128)(4,1)} %bitcast.8), calls=%async_computation.10 | async-start | bytes 8388608
  11.1 5.1 %collective-permute-start.3 = (bf16[16,4352]{1,0:T(8,128)(2,1)S(1)}, bf16[16,4352]{1,0:T(8,128)(2,1)S(1)}, u32[]{:S(2)}, u32[]{:S(2)}) collective-permute-start(bf16[16,4352]{1,0:T(8,128)(2,1)S(1)} %shard_map.109.refs_0_), channel_id=1, source_target_pairs={{0,2},{1,3},{2,0},{3,1},{4,6},{5,7},{6,4},{7,5},{8,10},{9,11},{10,... | collective-permute-start | bytes 417800 | tf_op jit(solution)/shard_map/ppermute | solution.py:221
  12.7 3.6 %collective-permute-start.4 = (bf16[16,4352]{1,0:T(8,128)(2,1)S(1)}, bf16[16,4352]{1,0:T(8,128)(2,1)S(1)}, u32[]{:S(2)}, u32[]{:S(2)}) collective-permute-start(bf16[16,4352]{1,0:T(8,128)(2,1)S(1)} %shard_map.109.refs_0_), channel_id=1, source_target_pairs={{0,1},{1,0},{2,3},{3,2},{4,5},{5,4},{6,7},{7,6},{8,9},{9,8},{10,11... | collective-permute-start | bytes 417800 | tf_op jit(solution)/shard_map/ppermute | solution.py:221
  16.3 1.4 %collective-permute-start.5 = (bf16[16,4352]{1,0:T(8,128)(2,1)S(1)}, bf16[16,4352]{1,0:T(8,128)(2,1)S(1)}, u32[]{:S(2)}, u32[]{:S(2)}) collective-permute-start(bf16[16,4352]{1,0:T(8,128)(2,1)S(1)} %collective-permute-done.3.refs_1_), channel_id=1, source_target_pairs={{0,1},{1,0},{2,3},{3,2},{4,5},{5,4},{6,7},{7,6},{8,9},{9,8},{10,11... | collective-permute-start | bytes 417800 | tf_op jit(solution)/shard_map/ppermute | solution.py:221
  20.1 4.9 %collective-permute-start.10 = (bf16[2,64,384]{2,1,0:T(8,128)(2,1)S(1)}, bf16[2,64,384]{2,1,0:T(8,128)(2,1)S(1)}, u32[]{:S(2)}, u32[]{:S(2)}) collective-permute-start(bf16[2,64,384]{2,1,0:T(8,128)(2,1)S(1)} %get-tuple-element.21.refs_0_), channel_id=1, source_target_pairs={{0,2},{1,3},{2,0},{3,1},{4,6},{5,7},{6,4},{7,5},{8,10},{9,11},{10,... | collective-permute-start | bytes 294920 | tf_op jit(solution)/shard_map/ppermute | solution.py:221
  23.7 1.4 %collective-permute-start.8 = (bf16[2,64,384]{2,1,0:T(8,128)(2,1)S(1)}, bf16[2,64,384]{2,1,0:T(8,128)(2,1)S(1)}, u32[]{:S(2)}, u32[]{:S(2)}) collective-permute-start(bf16[2,64,384]{2,1,0:T(8,128)(2,1)S(1)} %get-tuple-element.20.refs_2_), channel_id=1, source_target_pairs={{0,1},{1,0},{2,3},{3,2},{4,5},{5,4},{6,7},{7,6},{8,9},{9,8},{10,11... | collective-permute-start | bytes 294920 | tf_op jit(solution)/shard_map/ppermute | solution.py:221
  23.8 1.4 %collective-permute-start.7 = (bf16[2,64,384]{2,1,0:T(8,128)(2,1)S(1)}, bf16[2,64,384]{2,1,0:T(8,128)(2,1)S(1)}, u32[]{:S(2)}, u32[]{:S(2)}) collective-permute-start(bf16[2,64,384]{2,1,0:T(8,128)(2,1)S(1)} %get-tuple-element.21.refs_0_), channel_id=1, source_target_pairs={{0,1},{1,0},{2,3},{3,2},{4,5},{5,4},{6,7},{7,6},{8,9},{9,8},{10,11... | collective-permute-start | bytes 294920 | tf_op jit(solution)/shard_map/ppermute | solution.py:221
  24.3 4.8 %collective-permute-start.6 = (bf16[2,64,384]{2,1,0:T(8,128)(2,1)S(1)}, bf16[2,64,384]{2,1,0:T(8,128)(2,1)S(1)}, u32[]{:S(2)}, u32[]{:S(2)}) collective-permute-start(bf16[2,64,384]{2,1,0:T(8,128)(2,1)S(1)} %get-tuple-element.20.refs_2_), channel_id=1, source_target_pairs={{0,2},{1,3},{2,0},{3,1},{4,6},{5,7},{6,4},{7,5},{8,10},{9,11},{10,... | collective-permute-start | bytes 294920 | tf_op jit(solution)/shard_map/ppermute | solution.py:221
  25.1 4.1 %collective-permute-start.11 = (bf16[2,64,384]{2,1,0:T(8,128)(2,1)S(1)}, bf16[2,64,384]{2,1,0:T(8,128)(2,1)S(1)}, u32[]{:S(2)}, u32[]{:S(2)}) collective-permute-start(bf16[2,64,384]{2,1,0:T(8,128)(2,1)S(1)} %collective-permute-done.10.refs_0_), channel_id=1, source_target_pairs={{0,1},{1,0},{2,3},{3,2},{4,5},{5,4},{6,7},{7,6},{8,9},{9,8},{10,11... | collective-permute-start | bytes 294920 | tf_op jit(solution)/shard_map/ppermute | solution.py:221
  29.1 1.4 %collective-permute-start.9 = (bf16[2,64,384]{2,1,0:T(8,128)(2,1)S(1)}, bf16[2,64,384]{2,1,0:T(8,128)(2,1)S(1)}, u32[]{:S(2)}, u32[]{:S(2)}) collective-permute-start(bf16[2,64,384]{2,1,0:T(8,128)(2,1)S(1)} %shard_map.110), channel_id=1, source_target_pairs={{0,1},{1,0},{2,3},{3,2},{4,5},{5,4},{6,7},{7,6},{8,9},{9,8},{10,11... | collective-permute-start | bytes 294920 | tf_op jit(solution)/shard_map/ppermute | solution.py:221
  31.5 1.6 %collective-permute-start.12 = (bf16[32,4096]{1,0:T(8,128)(2,1)S(1)}, bf16[32,4096]{1,0:T(8,128)(2,1)S(1)}, u32[]{:S(2)}, u32[]{:S(2)}) collective-permute-start(bf16[32,4096]{1,0:T(8,128)(2,1)S(1)} %get-tuple-element.28), channel_id=1, source_target_pairs={{0,1},{1,0},{2,3},{3,2},{4,5},{5,4},{6,7},{7,6},{8,9},{9,8},{10,11... | collective-permute-start | bytes 786440 | tf_op jit(solution)/shard_map/ppermute | solution.py:221
  33.2 5.6 %collective-permute-start.13 = (bf16[16,4096]{1,0:T(8,128)(2,1)S(1)}, bf16[16,4096]{1,0:T(8,128)(2,1)S(1)}, u32[]{:S(2)}, u32[]{:S(2)}) collective-permute-start(bf16[16,4096]{1,0:T(8,128)(2,1)S(1)} %get-tuple-element.30), channel_id=1, source_target_pairs={{0,2},{1,3},{2,0},{3,1},{4,6},{5,7},{6,4},{7,5},{8,10},{9,11},{10,... | collective-permute-start | bytes 393224 | tf_op jit(solution)/shard_map/ppermute | solution.py:221
  38.9 5.9 %collective-permute-start.14 = (bf16[4,4096]{1,0:T(4,128)(2,1)S(1)}, bf16[4,4096]{1,0:T(4,128)(2,1)S(1)}, u32[]{:S(2)}, u32[]{:S(2)}) collective-permute-start(bf16[4,4096]{1,0:T(4,128)(2,1)S(1)} %get-tuple-element.32), channel_id=1, source_target_pairs={{0,12},{4,8},{8,4},{12,0},{1,13},{5,9},{9,5},{13,1},{2,14},{6,10},... | collective-permute-start | bytes 98312 | tf_op jit(solution)/shard_map/ppermute | solution.py:221
  40.4 4.8 %collective-permute-start.15 = (bf16[4,4096]{1,0:T(4,128)(2,1)S(1)}, bf16[4,4096]{1,0:T(4,128)(2,1)S(1)}, u32[]{:S(2)}, u32[]{:S(2)}) collective-permute-start(bf16[4,4096]{1,0:T(4,128)(2,1)S(1)} %get-tuple-element.33), channel_id=1, source_target_pairs={{0,8},{4,12},{8,0},{12,4},{1,9},{5,13},{9,1},{13,5},{2,10},{6,14},... | collective-permute-start | bytes 98312 | tf_op jit(solution)/shard_map/ppermute | solution.py:221
  41.0 4.5 %collective-permute-start.16 = (bf16[4,4096]{1,0:T(4,128)(2,1)S(1)}, bf16[4,4096]{1,0:T(4,128)(2,1)S(1)}, u32[]{:S(2)}, u32[]{:S(2)}) collective-permute-start(bf16[4,4096]{1,0:T(4,128)(2,1)S(1)} %get-tuple-element.34), channel_id=1, source_target_pairs={{0,4},{4,0},{8,12},{12,8},{1,5},{5,1},{9,13},{13,9},{2,6},{6,2},{1... | collective-permute-start | bytes 98312 | tf_op jit(solution)/shard_map/ppermute | solution.py:221
  (7 other events, 46.9 us)

commit v4 on v3

v4 whole, which is shorter than its diff:
```python
import functools

import jax
import jax.numpy as jnp
from jax import lax
from jax.experimental import pallas as pl
from jax.experimental.pallas import tpu as pltpu
from jax.sharding import PartitionSpec as P

TOP = 8
EXPERTS = 16
SLOTS = 2
CAP = 3
LANES = 128
PIECES = 3
PARTS = 2
BF = jnp.bfloat16
F32 = jnp.float32

VM = pl.BlockSpec(memory_space=pltpu.VMEM)
HB = pl.BlockSpec(memory_space=pltpu.HBM)


def in_vmem(x):
    return pltpu.with_memory_space_constraint(x, pltpu.VMEM)


def in_hbm(x):
    return pltpu.with_memory_space_constraint(x, pltpu.HBM)


def shape(dims, dtype=BF):
    return jax.ShapeDtypeStruct(tuple(dims), dtype)


def size_of(*arrays):
    total = 0
    for a in arrays:
        n = jnp.dtype(a.dtype).itemsize
        for s in a.shape[:-1]:
            n *= s
        total += n * (-(-a.shape[-1] // LANES) * LANES)
    return total


def call(body, out_shape, operands, specs=None, room=2 << 20, scratch=()):
    specs = specs or [VM] * len(operands)
    held = [a for a, s in zip(operands, specs) if s is VM and size_of(a) < 1 << 20]
    limit = room + size_of(*held, *jax.tree.leaves(out_shape))
    return pl.pallas_call(
        body,
        out_shape=out_shape,
        in_specs=specs,
        out_specs=jax.tree.map(lambda _: VM, out_shape),
        scratch_shapes=scratch,
        cost_estimate=pl.CostEstimate(flops=0, bytes_accessed=0, transcendentals=0),
        compiler_params=pltpu.CompilerParams(vmem_limit_bytes=limit),
    )(*operands)


def prepare(*refs):
    ins, y, held, sems = refs[:6], refs[9], refs[10:16], refs[16]
    copies = [pltpu.make_async_copy(s, d, sems.at[i]) for i, (s, d) in enumerate(zip(ins, held))]
    for c in copies:
        c.start()
    for c in copies:
        c.wait()
    ten, tok, ids, rw, owner, slot = held
    rows, width = tok.shape
    y[:, :width] = tok[...]
    lane = lax.broadcasted_iota(jnp.int32, (rows, LANES), 1)
    expert, piece = lane & (EXPERTS - 1), lane >> (EXPERTS.bit_length() - 1)
    w = jnp.zeros((rows, LANES), F32)
    routed = jnp.zeros((rows, LANES), F32)
    for k in range(TOP):
        same = ids[:, k : k + 1] == expert
        w += jnp.where(same, rw[:, k : k + 1], 0.0)
        routed += jnp.where(same, 1.0, 0.0)
    places = [routed[:1]]
    for r in range(1, rows):
        places.append(places[-1] + routed[r : r + 1])
    place = jnp.concatenate(places, axis=0) * routed
    high = w.astype(BF).astype(F32)
    mid = (w - high).astype(BF).astype(F32)
    low = w - high - mid
    block = jnp.zeros((rows, LANES), F32)
    for i, value in enumerate((high, mid, low, place)):
        block = jnp.where(piece == i, value, block)
    y[:, width : width + LANES] = block.astype(BF)
    y[:, width + LANES :] = jnp.zeros((rows, LANES), BF)
    pages = [
        owner[pl.ds(ten[r], 1), :] * SLOTS + slot[pl.ds(ten[r], 1), :] for r in range(rows)
    ]
    y[:, width + LANES : width + LANES + EXPERTS] = (
        jnp.concatenate(pages, axis=0).astype(F32).astype(BF)
    )


def join_blocks(count, *refs):
    parts = [r[...].astype(F32) for r in refs[:count]]
    refs[-1][...] = jnp.concatenate(parts, axis=0).astype(BF)


def relay(x, *refs):
    refs[-1][...] = x[...]


def column(meta, lane, wanted):
    return jnp.sum(jnp.where(lane == wanted, meta, 0.0), axis=1, keepdims=True)


def picks(meta, lane, expert, each, flip):
    rows = meta.shape[0]
    place = column(meta, lane, PIECES * EXPERTS + expert).astype(jnp.int32)
    block = lax.broadcasted_iota(jnp.int32, (rows, 1), 0) >> (each.bit_length() - 1)
    target = jnp.where(place > 0, (block ^ flip) * CAP + place - 1, -1)
    slots = rows // each * CAP
    spot = lax.broadcasted_iota(jnp.int32, (rows, slots), 1)
    return jnp.where(spot == target, 1.0, 0.0).astype(BF)


def gather_rows(places, *refs):
    blocks, xs, info = refs[: len(places)], refs[-2], refs[-1]
    size, width = blocks[0].shape[0], xs.shape[1]
    in_order = [blocks[places.index(i)] for i in range(len(places))]
    for i in range(0, len(places), 2):
        pair = [r[...].astype(F32) for r in in_order[i : i + 2]]
        both = jnp.concatenate(pair, axis=0).astype(BF)
        xs[i * size : (i + 2) * size] = both[:, :width]
        info[i * size : (i + 2) * size] = both[:, width:]


def up_kernel(picked, each, *refs):
    xs, info, gate, up, h, packed = refs
    experts, width = gate.shape[0], gate.shape[1]
    first = lax.axis_index("expert") * experts
    meta = info[:, :LANES].astype(F32)
    lane = lax.broadcasted_iota(jnp.int32, meta.shape, 1)
    weight = jnp.where(lane < PIECES * EXPERTS, meta, 0.0)
    step = 256
    for i, e in enumerate(picked):
        w = column(weight, lane & (EXPERTS - 1), first + e)
        a = b = 0.0
        for k in range(0, width, step):
            x = xs[:, k : k + step]
            a += jnp.dot(x, gate[e, k : k + step], preferred_element_type=F32)
            b += jnp.dot(x, up[e, k : k + step], preferred_element_type=F32)
        hidden = (a * jax.nn.sigmoid(a) * b * w).astype(BF)
        h[i] = hidden
        packed[i] = lax.dot_general(
            picks(meta, lane, first + e, each, 0),
            hidden,
            (((0,), (0,)), ((), ())),
            preferred_element_type=F32,
        ).astype(BF)


def columns(ref, spot, size):
    if size % LANES == 0:
        return ref[:, pl.ds(pl.multiple_of(spot * size, size), size)]
    picked = ref[:, :size]
    for c in range(1, ref.shape[1] // size):
        picked = jnp.where(spot == c, ref[:, c * size : (c + 1) * size], picked)
    return picked


def down_kernel(each, n, flips, terms, opens, cut, *refs):
    pairs, refs = refs[: 2 * len(terms)], refs[2 * len(terms) :]
    (info, down, shrink), refs = refs[:3], refs[3:]
    base = small = spreads = here_ref = None
    if not opens:
        base, small, here_ref = refs[0][...], refs[1][...], refs[2]
        refs = refs[3:]
        if flips:
            spreads, refs = refs[0], refs[1:]
    me = lax.axis_index("dp")
    odd = lax.rem(me, 2) == 1
    experts = down.shape[0]
    part = pairs[0].shape[2]
    rows, ranks = info.shape[0], shrink.shape[0]
    half, per = rows // 2, ranks // experts
    cols = down.shape[2]
    across = slice(0, cols)
    if cut is not None:
        across = slice(cut * (cols // PARTS), (cut + 1) * (cols // PARTS))
        base = base[:, across]
    first = lax.axis_index("expert") * experts
    meta = info[:, :LANES].astype(F32)
    lane16 = lax.broadcasted_iota(jnp.int32, meta.shape, 1)
    lane = lax.broadcasted_iota(jnp.int32, (rows, ranks), 1)

    def spread(e, m):
        flip = (m & 1) * (half // each) + (m >> 1)
        return picks(meta, lane16, first + e, each, flip)

    def turned(m):
        flip = (m & 1) * (half // each) + (m >> 1)
        there = lax.broadcasted_iota(jnp.int32, (rows, rows), 0) ^ (flip * each)
        return jnp.where(lax.broadcasted_iota(jnp.int32, (rows, rows), 1) == there, 1.0, 0.0).astype(BF)

    def ordered(ref, i, e, m):
        if m == 0:
            return ref[i]
        if ref.shape[1] == rows:
            return jnp.dot(turned(m), ref[i], preferred_element_type=F32).astype(BF)
        known = spreads is not None and m in flips
        one_hot = spreads[flips.index(m) * experts + e] if known else spread(e, m)
        return jnp.dot(one_hot, ref[i], preferred_element_type=F32).astype(BF)

    for t, (m, picked) in enumerate(terms):
        pair = (me ^ m) // 2
        for i, e in enumerate(picked):
            mine = ordered(pairs[2 * t], i, e, m)
            other = ordered(pairs[2 * t + 1], i, e, m ^ 1)
            x = [jnp.where(odd, other, mine), jnp.where(odd, mine, other)]
            if part % LANES == 0:
                x = [jnp.concatenate(x, axis=1)]
            for j, piece in enumerate(x):
                spot, size = pair * len(x) + j, piece.shape[1]
                at = pl.ds(pl.multiple_of(spot * size, size), size)
                term = jnp.dot(piece, down[e, at, across], preferred_element_type=F32)
                base = term if base is None else base + term
                if cut:
                    continue
                term = lax.dot_general(
                    piece,
                    columns(shrink, spot, size),
                    (((1,), (1,)), ((), ())),
                    preferred_element_type=F32,
                )
                inside = (lane >= e * per) & (lane < (e + 1) * per)
                term = jnp.where(inside, term, 0.0)
                small = term if small is None else small + term
    if opens:
        refs[0][...] = base
        refs[1][...] = small
        values = info[:, LANES:].astype(F32)
        rank = per // SLOTS
        away = jnp.full((rows, ranks), -1.0, F32)
        for e in range(experts):
            value = column(values, lane16, first + e)
            for s in range(SLOTS):
                low = e * per + s * rank
                inside = (lane >= low) & (lane < low + rank)
                away = jnp.where(inside, value - (me * SLOTS + s).astype(F32), away)
        refs[2][...] = jnp.where(away == 0.0, 1.0, 0.0)
        for f, m in enumerate(flips):
            for e in range(experts):
                refs[3][f * experts + e] = spread(e, m)
        return
    if cut is None:
        refs[0][...] = base
        refs[1][...] = small
        return
    if cut == 0:
        expand, keep, send, ready = refs
        small = (small * here_ref[...]).astype(BF)
        ready[...] = small
    else:
        expand, ready, keep, send = refs
        small = ready[...]
    size = cols // PARTS
    for c in range(n):
        here = slice(c * size, (c + 1) * size)
        there = slice(c * cols + across.start, c * cols + across.stop)
        out = jnp.dot(small, expand[:, there], preferred_element_type=F32)
        out += jnp.where(me == c, base, 0.0)
        keep[:, here] = out[:half]
        send[:, here] = out[half:].astype(BF)


def add_and_deal(size, count, sets, *refs):
    ins, outs = refs[: count * sets], refs[count * sets :]
    width = ins[0].shape[1]
    for s in range(sets):
        total = ins[s * count][...]
        for r in ins[s * count + 1 : (s + 1) * count]:
            total += r[...].astype(F32)
        parts = [total[r : r + size] for r in range(0, total.shape[0], size)]
        for i, o in enumerate(outs):
            dealt = jnp.concatenate(parts[i :: len(outs)], axis=0)
            o[:, s * width : (s + 1) * width] = dealt.astype(o.dtype)


def finish(cols, *refs):
    total = refs[0][...]
    for r in refs[1:-1]:
        total += r[...].astype(F32)
    size, n = cols // PARTS, total.shape[1] // cols
    for p in range(PARTS):
        for c in range(n):
            at = (p * n + c) * size
            to = c * cols + p * size
            refs[-1][:, to : to + size] = total[:, at : at + size].astype(BF)


def shards(tokens, expert_ids, route_weight, tenant_ids, gate, up, down, shrink, expand, owner, slot):
    n_z, n_dp = lax.axis_size("expert"), lax.axis_size("dp")
    n_x = n_dp // 2
    rows, width = tokens.shape
    experts, _, part = gate.shape
    wide = width + 2 * LANES
    block = rows * n_x
    half_rows = block * n_z
    all_rows = 2 * half_rows
    x_bits = [b for b in (2, 4, 8, 16, 32, 64) if b < n_dp]

    def over(x, axis, m):
        return lax.ppermute(x, axis, [(i, i ^ m) for i in range(lax.axis_size(axis))])

    inputs = (tenant_ids, tokens, expert_ids, route_weight, owner, slot)
    weights = [in_hbm(a) for a in (gate, up, down)]
    with jax.named_scope("prepare"):
        y = call(
            prepare,
            shape((rows, wide)),
            [*[in_hbm(a) for a in inputs], *weights],
            [HB] * (len(inputs) + 3),
            scratch=[
                *[(pltpu.VMEM if i else pltpu.SMEM)(a.shape, a.dtype) for i, a in enumerate(inputs)],
                pltpu.SemaphoreType.DMA((len(inputs),)),
            ],
        )

    blocks = [y]
    for b in x_bits:
        blocks = blocks + [over(a, "dp", b) for a in blocks]
    with jax.named_scope("join"):
        lead = call(
            functools.partial(join_blocks, n_x),
            shape((block, wide)),
            (*blocks, *weights),
            [VM] * n_x + [HB] * 3,
            room=(2 << 20) + 4 * block * wide,
        )
    along_z = {k: over(lead, "expert", k) if k else lead for k in range(n_z)}
    places = [0, *range(n_z - 1, 0, -1)]
    places += [k + n_z for k in places]
    gathered = [along_z[k] for k in places[:n_z]]
    gathered += [over(a, "dp", 1) for a in gathered]

    lists = [list(range(experts))]
    if experts > 1:
        lists = [lists[0][: experts // 2], lists[0][experts // 2 :]]
    packed_rows = all_rows // rows * CAP
    with jax.named_scope("gather"):
        xs, info = call(
            functools.partial(gather_rows, places),
            [shape((all_rows, width)), shape((all_rows, 2 * LANES))],
            gathered,
        )
    hidden = []
    for picked in lists:
        with jax.named_scope("up"):
            h, packed = call(
                functools.partial(up_kernel, picked, rows),
                [
                    shape((len(picked), all_rows, part)),
                    shape((len(picked), packed_rows, part)),
                ],
                (xs, info, in_vmem(gate), in_vmem(up)),
                room=(4 << 20) + 4 * all_rows * (packed_rows + 4 * part + 8 * LANES),
            )
        hidden.append({0: h, "packed": packed})
    for got in hidden:
        moved = {0: got["packed"] if got is hidden[-1] else got[0]}
        for b in x_bits:
            moved.update({m | b: over(a, "dp", b) for m, a in moved.items()})
        got.update({m: a for m, a in moved.items() if m})

    def between_cores(got, pairs, behind=()):
        for m in pairs:
            x = got[m] if m else got["packed"]
            if behind:
                x = call(relay, shape(x.shape), (x, *behind))
            got[m ^ 1] = over(x, "dp", 1)

    others = list(range(2, n_dp, 2))
    for got in hidden:
        between_cores(got, [0] if got is hidden[-1] else [0, *others])

    shrink2 = shrink.reshape(-1, shrink.shape[-1])
    expand2 = expand.reshape(-1, expand.shape[-1])
    cols = down.shape[2]
    ranks = shrink2.shape[0]
    sums = [shape((all_rows, cols), F32), shape((all_rows, ranks), F32)]
    spreads = shape(((n_dp - 2) * experts, all_rows, packed_rows))
    flips = list(range(2, n_dp)) if size_of(spreads) < 1 << 20 else []
    steps = [[(0, i) for i in range(len(lists))]]
    steps += [[(m, i) for m in others] for i in range(len(lists))]
    carried, routing = [], []

    def add_terms(step, opens, cut, outs, after):
        arrays = [a for m, i in step for a in (hidden[i][m], hidden[i][m ^ 1])]
        terms = [(m, lists[i]) for m, i in step]
        with jax.named_scope("down"):
            return call(
                functools.partial(down_kernel, rows, n_dp, flips, terms, opens, cut),
                outs,
                [*arrays, *(info, in_vmem(down), shrink2), *carried, *routing, *after],
                room=(6 << 20) + 4 * all_rows * (4 * cols + 2 * packed_rows + 4 * part),
            )

    for s, step in enumerate(steps[:-1]):
        if s == 1:
            between_cores(hidden[-1], others, carried)
        outs = list(sums)
        if s == 0:
            outs += [shape((all_rows, ranks), F32)] + ([spreads] if flips else [])
        carried = add_terms(step, s == 0, None, outs, [])
        if s == 0:
            carried, routing = carried[:2], carried[2:]
    if len(steps) == 2:
        between_cores(hidden[-1], others, carried)

    some = width // PARTS
    arrived, after = [], [expand2]
    for cut in range(PARTS):
        outs = [shape((half_rows, some), F32), shape((half_rows, some))]
        ready = shape((all_rows, ranks))
        keep, send, *more = add_terms(
            steps[-1], False, cut, outs + ([ready] if cut == 0 else []), after
        )
        after = after + more
        terms, left = [keep, over(send, "dp", 1)], n_x
        for b in x_bits[::-1]:
            left //= 2
            dims = (n_z * left * rows, some)
            kept = call(
                functools.partial(add_and_deal, left * rows, 2, 1),
                [shape(dims, F32), shape(dims)],
                terms,
                room=(2 << 20) + 3 * size_of(terms[0]),
            )
            terms = [kept[0], over(kept[1], "dp", b)]
        arrived += terms
    kept = call(
        functools.partial(add_and_deal, rows, 2, PARTS),
        [shape((rows, width), F32)] + [shape((rows, width))] * (n_z - 1),
        arrived,
        room=(2 << 20) + 6 * size_of(arrived[0]),
    )
    back = [over(kept[k], "expert", k) for k in range(n_z - 1, 0, -1)]
    with jax.named_scope("finish"):
        return call(
            functools.partial(finish, cols),
            shape((rows, width)),
            [kept[0], *back],
        )


def solution(mesh):
    rows = ("group", "expert", "dp")
    in_specs = (
        P(rows, None),
        P(rows, None),
        P(rows, None),
        P(rows),
        P("expert", None, "dp"),
        P("expert", None, "dp"),
        P("expert", None, "dp"),
        P("expert", "dp", None, None),
        P("expert", "dp", None, None),
        P(),
        P(),
    )
    return jax.shard_map(
        shards, mesh=mesh, in_specs=in_specs, out_specs=P(rows, None), check_vma=False
    )
```

time: 46.4 us -> 45.7 us (0.985)
  waiting for transfers between devices: 20.9 us -> 16.4 us
  starting transfers between devices: 15.3 us -> 18 us
  Pallas kernels: 9.71 us -> 10.8 us
    ppermute x17 -> x21, waiting for transfers between devices: 20.9 us -> 16.4 us  [over(): lax.ppermute(x, axis, [(i, i ^ m) for i in range(lax.axis_size(axis))])]
    ppermute x17 -> x21, starting transfers between devices: 15.3 us -> 18 us  [over(): lax.ppermute(x, axis, [(i, i ^ m) for i in range(lax.axis_size(axis))])]
    pallas_call x11 -> x14, Pallas kernels: 9.71 us -> 10.8 us  [call(): pl.pallas_call(body, out_shape=out_shape, in_specs=specs, out_specs=jax.t...]
  transfers between devices with their start and end apart: 17 -> 21, of which waited for: 13 -> 15; matrix products, arithmetic and copies ran while one was open for 0% -> 0% of each run, Pallas kernels for 9% -> 13%
where the time goes in v4:
time: 45.7 us; the launch traced here: 45.5 us
  starting transfers between devices  18 us (39%)
  waiting for transfers between devices  16.4 us (36%)
  Pallas kernels  10.8 us (24%)
    ppermute x21, starting transfers between devices, over(): lax.ppermute(x, axis, [(i, i ^ m) for i in range(lax.axis_size(axis))])  18 us
    ppermute x21, waiting for transfers between devices, over(): lax.ppermute(x, axis, [(i, i ^ m) for i in range(lax.axis_size(axis))])  16.4 us
    pallas_call x14, Pallas kernels, call(): pl.pallas_call(body, out_shape=out_shape, in_specs=specs, out_specs=jax.t...  10.8 us
  transfers between devices with their start and end apart: 21, of which 15 were waited for; matrix products, arithmetic and copies ran while one was open for 0% of the time, Pallas kernels for 13%

profile of v4, /device:TPU:0, one launch (start us, length us, event | category | flops | bytes accessed | tf_op | source)
XLA Modules:
  0.0 45.5 jit_solution(6786475346380994740)
XLA Ops:
  0.0 1.1 %prepare.1.refs_0_ = bf16[4,4352]{1,0:T(4,128)(2,1)S(1)} custom-call(s32[4]{0:T(128)} %refs_0_.1, bf16[4,4096]{1,0:T(4,128)(2,1)} %refs_1_.1, s32[4,8]{1,0:T(4,128)} %refs_2_.4, f32[4,8]{1,0:T(4,128)} %refs_3_.7, s32[8,16]{1,0:T(8,128)} %refs_4_.2, s32[8,16]{1,0:T(8,128)} %refs_5_.2, bf16[4,4096,384]{2,1,0:T(8,128)(2,1)} %refs_2_.7, ...), custom_call_target="tpu_custom_call" | custom-call | tf_op jit(solution)/shard_map/prepare/pallas_call | solution.py:50
  1.1 3.0 %collective-permute-start = (bf16[4,4352]{1,0:T(4,128)(2,1)S(1)}, bf16[4,4352]{1,0:T(4,128)(2,1)S(1)}, u32[]{:S(2)}, u32[]{:S(2)}) collective-permute-start(bf16[4,4352]{1,0:T(4,128)(2,1)S(1)} %prepare.1.refs_0_), channel_id=1, source_target_pairs={{0,2},{1,3},{2,0},{3,1},{4,6},{5,7},{6,4},{7,5},{8,10},{9,11},{10,... | collective-permute-start | bytes 104456 | tf_op jit(solution)/shard_map/ppermute | solution.py:309
  4.1 1.9 %collective-permute-done.refs_1_ = bf16[4,4352]{1,0:T(4,128)(2,1)S(1)} collective-permute-done((bf16[4,4352]{1,0:T(4,128)(2,1)S(1)}, bf16[4,4352]{1,0:T(4,128)(2,1)S(1)}, u32[]{:S(2)}, u32[]{:S(2)}) %collective-permute-start) | collective-permute-done | bytes 34848 | tf_op jit(solution)/shard_map/ppermute | solution.py:309
  6.1 4.2 %collective-permute-start.1 = (bf16[8,4352]{1,0:T(8,128)(2,1)S(1)}, bf16[8,4352]{1,0:T(8,128)(2,1)S(1)}, u32[]{:S(2)}, u32[]{:S(2)}) collective-permute-start(bf16[8,4352]{1,0:T(8,128)(2,1)S(1)} %join.1.refs_0_), channel_id=1, source_target_pairs={{0,12},{4,8},{8,4},{12,0},{1,13},{5,9},{9,5},{13,1},{2,14},{6,10},... | collective-permute-start | bytes 208904 | tf_op jit(solution)/shard_map/ppermute | solution.py:309
  10.3 0.6 %collective-permute-start.3 = (bf16[8,4352]{1,0:T(8,128)(2,1)S(1)}, bf16[8,4352]{1,0:T(8,128)(2,1)S(1)}, u32[]{:S(2)}, u32[]{:S(2)}) collective-permute-start(bf16[8,4352]{1,0:T(8,128)(2,1)S(1)} %join.1.refs_0_), channel_id=1, source_target_pairs={{0,4},{4,0},{8,12},{12,8},{1,5},{5,1},{9,13},{13,9},{2,6},{6,2},{1... | collective-permute-start | bytes 208904 | tf_op jit(solution)/shard_map/ppermute | solution.py:309
  10.9 1.9 %collective-permute-done.1.refs_1_ = bf16[8,4352]{1,0:T(8,128)(2,1)S(1)} collective-permute-done((bf16[8,4352]{1,0:T(8,128)(2,1)S(1)}, bf16[8,4352]{1,0:T(8,128)(2,1)S(1)}, u32[]{:S(2)}, u32[]{:S(2)}) %collective-permute-start.1) | collective-permute-done | bytes 69664 | tf_op jit(solution)/shard_map/ppermute | solution.py:309
  12.8 2.9 %collective-permute-done.2.refs_2_ = bf16[8,4352]{1,0:T(8,128)(2,1)S(1)} collective-permute-done((bf16[8,4352]{1,0:T(8,128)(2,1)S(1)}, bf16[8,4352]{1,0:T(8,128)(2,1)S(1)}, u32[]{:S(2)}, u32[]{:S(2)}) %collective-permute-start.2) | collective-permute-done | bytes 69664 | tf_op jit(solution)/shard_map/ppermute | solution.py:309
  16.2 0.7 %collective-permute-done.6.refs_6_ = bf16[8,4352]{1,0:T(8,128)(2,1)S(1)} collective-permute-done((bf16[8,4352]{1,0:T(8,128)(2,1)S(1)}, bf16[8,4352]{1,0:T(8,128)(2,1)S(1)}, u32[]{:S(2)}, u32[]{:S(2)}) %collective-permute-start.6) | collective-permute-done | bytes 69664 | tf_op jit(solution)/shard_map/ppermute | solution.py:309
  17.2 2.2 %up.3 = (bf16[2,64,384]{2,1,0:T(8,128)(2,1)S(1)}, bf16[2,48,384]{2,1,0:T(8,128)(2,1)S(1)}) custom-call(bf16[64,4096]{1,0:T(8,128)(2,1)S(1)} %get-tuple-element.30.refs_0_, bf16[64,256]{1,0:T(8,128)(2,1)S(1)} %get-tuple-element.31.refs_1_.refs_4_.refs_2_, bf16[4,4096,384]{2,1,0:T(8,128)(2,1)S(1)} %bitcast.5, bf16[4,4096,384]{2,1,0:T(8,128)(2,1)S(1)} %bitcast.7), custom_call_target="tpu_custom_call" | custom-call | tf_op jit(solution)/shard_map/up/pallas_call | solution.py:50
  19.5 1.6 %collective-permute-start.12 = (bf16[2,64,384]{2,1,0:T(8,128)(2,1)S(1)}, bf16[2,64,384]{2,1,0:T(8,128)(2,1)S(1)}, u32[]{:S(2)}, u32[]{:S(2)}) collective-permute-start(bf16[2,64,384]{2,1,0:T(8,128)(2,1)S(1)} %get-tuple-element.33.refs_0_), channel_id=1, source_target_pairs={{0,2},{1,3},{2,0},{3,1},{4,6},{5,7},{6,4},{7,5},{8,10},{9,11},{10,... | collective-permute-start | bytes 294920 | tf_op jit(solution)/shard_map/ppermute | solution.py:309
  21.0 2.2 %up.2 = (bf16[2,64,384]{2,1,0:T(8,128)(2,1)S(1)}, bf16[2,48,384]{2,1,0:T(8,128)(2,1)S(1)}) custom-call(bf16[64,4096]{1,0:T(8,128)(2,1)S(1)} %get-tuple-element.30.refs_0_, bf16[64,256]{1,0:T(8,128)(2,1)S(1)} %get-tuple-element.31.refs_1_.refs_4_.refs_2_, bf16[4,4096,384]{2,1,0:T(8,128)(2,1)S(1)} %bitcast.5, bf16[4,4096,384]{2,1,0:T(8,128)(2,1)S(1)} %bitcast.7), custom_call_target="tpu_custom_call" | custom-call | tf_op jit(solution)/shard_map/up/pallas_call | solution.py:50
  24.8 1.8 %down.4 = (f32[64,1024]{1,0:T(8,128)S(1)}, f32[64,128]{1,0:T(8,128)S(1)}, f32[64,128]{1,0:T(8,128)S(1)}, bf16[8,64,48]{2,1,0:T(8,128)(2,1)S(1)}) custom-call(bf16[2,64,384]{2,1,0:T(8,128)(2,1)S(1)} %get-tuple-element.33.refs_0_, bf16[2,48,384]{2,1,0:T(8,128)(2,1)S(1)} %collective-permute-done.9.refs_1_, bf16[2,64,384]{2,1,0:T(8,128)(2,1)S(1)} %get-tuple-element.35.refs_2_, ...), custom_call_target="tpu_custom_call" | custom-call | tf_op jit(solution)/shard_map/down/pallas_call | solution.py:50
  26.6 1.7 %collective-permute-done.8.x.refs_0_ = bf16[2,48,384]{2,1,0:T(8,128)(2,1)S(1)} collective-permute-done((bf16[2,48,384]{2,1,0:T(8,128)(2,1)S(1)}, bf16[2,48,384]{2,1,0:T(8,128)(2,1)S(1)}, u32[]{:S(2)}, u32[]{:S(2)}) %collective-permute-start.8) | collective-permute-done | bytes 73760 | tf_op jit(solution)/shard_map/ppermute | solution.py:309
  28.3 1.0 %down.5 = (f32[64,1024]{1,0:T(8,128)S(1)}, f32[64,128]{1,0:T(8,128)S(1)}) custom-call(bf16[2,64,384]{2,1,0:T(8,128)(2,1)S(1)} %collective-permute-done.12.refs_0_, bf16[2,64,384]{2,1,0:T(8,128)(2,1)S(1)} %collective-permute-done.13.refs_1_, bf16[64,256]{1,0:T(8,128)(2,1)S(1)} %get-tuple-element.31.refs_1_.refs_4_.refs_2_, ...), custom_call_target="tpu_custom_call" | custom-call | tf_op jit(solution)/shard_map/down/pallas_call | solution.py:50
  29.6 1.0 %down.6 = (f32[32,2048]{1,0:T(8,128)S(1)}, bf16[32,2048]{1,0:T(8,128)(2,1)S(1)}, bf16[64,128]{1,0:T(8,128)(2,1)S(1)}) custom-call(bf16[2,48,384]{2,1,0:T(8,128)(2,1)S(1)} %collective-permute-done.8.x.refs_0_, bf16[2,48,384]{2,1,0:T(8,128)(2,1)S(1)} %collective-permute-done.11.refs_1_, bf16[64,256]{1,0:T(8,128)(2,1)S(1)} %get-tuple-element.31.refs_1_.refs_4_.refs_2_, ...), custom_call_target="tpu_custom_call" | custom-call | tf_op jit(solution)/shard_map/down/pallas_call | solution.py:50
  30.8 0.7 %down.7 = (f32[32,2048]{1,0:T(8,128)S(1)}, bf16[32,2048]{1,0:T(8,128)(2,1)S(1)}) custom-call(bf16[2,48,384]{2,1,0:T(8,128)(2,1)S(1)} %collective-permute-done.8.x.refs_0_, bf16[2,48,384]{2,1,0:T(8,128)(2,1)S(1)} %collective-permute-done.11.refs_1_, bf16[64,256]{1,0:T(8,128)(2,1)S(1)} %get-tuple-element.31.refs_1_.refs_4_.refs_2_, ...), custom_call_target="tpu_custom_call" | custom-call | tf_op jit(solution)/shard_map/down/pallas_call | solution.py:50
  33.0 1.2 %collective-permute-start.17 = (bf16[16,2048]{1,0:T(8,128)(2,1)S(1)}, bf16[16,2048]{1,0:T(8,128)(2,1)S(1)}, u32[]{:S(2)}, u32[]{:S(2)}) collective-permute-start(bf16[16,2048]{1,0:T(8,128)(2,1)S(1)} %get-tuple-element.50), channel_id=1, source_target_pairs={{0,2},{1,3},{2,0},{3,1},{4,6},{5,7},{6,4},{7,5},{8,10},{9,11},{10,... | collective-permute-start | bytes 196616 | tf_op jit(solution)/shard_map/ppermute | solution.py:309
  34.2 2.5 %collective-permute-done.15.refs_1_ = bf16[16,2048]{1,0:T(8,128)(2,1)S(1)} collective-permute-done((bf16[16,2048]{1,0:T(8,128)(2,1)S(1)}, bf16[16,2048]{1,0:T(8,128)(2,1)S(1)}, u32[]{:S(2)}, u32[]{:S(2)}) %collective-permute-start.15) | collective-permute-done | bytes 65568 | tf_op jit(solution)/shard_map/ppermute | solution.py:309
  36.7 1.0 %collective-permute-done.17.refs_3_ = bf16[16,2048]{1,0:T(8,128)(2,1)S(1)} collective-permute-done((bf16[16,2048]{1,0:T(8,128)(2,1)S(1)}, bf16[16,2048]{1,0:T(8,128)(2,1)S(1)}, u32[]{:S(2)}, u32[]{:S(2)}) %collective-permute-start.17) | collective-permute-done | bytes 65568 | tf_op jit(solution)/shard_map/ppermute | solution.py:309
  37.8 2.3 %collective-permute-start.18 = (bf16[4,4096]{1,0:T(4,128)(2,1)S(1)}, bf16[4,4096]{1,0:T(4,128)(2,1)S(1)}, u32[]{:S(2)}, u32[]{:S(2)}) collective-permute-start(bf16[4,4096]{1,0:T(4,128)(2,1)S(1)} %get-tuple-element.52), channel_id=1, source_target_pairs={{0,12},{4,8},{8,4},{12,0},{1,13},{5,9},{9,5},{13,1},{2,14},{6,10},... | collective-permute-start | bytes 98312 | tf_op jit(solution)/shard_map/ppermute | solution.py:309
  40.0 2.2 %collective-permute-start.20 = (bf16[4,4096]{1,0:T(4,128)(2,1)S(1)}, bf16[4,4096]{1,0:T(4,128)(2,1)S(1)}, u32[]{:S(2)}, u32[]{:S(2)}) collective-permute-start(bf16[4,4096]{1,0:T(4,128)(2,1)S(1)} %get-tuple-element.54), channel_id=1, source_target_pairs={{0,4},{4,0},{8,12},{12,8},{1,5},{5,1},{9,13},{13,9},{2,6},{6,2},{1... | collective-permute-start | bytes 98312 | tf_op jit(solution)/shard_map/ppermute | solution.py:309
  42.2 1.4 %collective-permute-done.18.refs_1_ = bf16[4,4096]{1,0:T(4,128)(2,1)S(1)} collective-permute-done((bf16[4,4096]{1,0:T(4,128)(2,1)S(1)}, bf16[4,4096]{1,0:T(4,128)(2,1)S(1)}, u32[]{:S(2)}, u32[]{:S(2)}) %collective-permute-start.18) | collective-permute-done | bytes 32800 | tf_op jit(solution)/shard_map/ppermute | solution.py:309
  43.6 1.2 %collective-permute-done.19.refs_2_ = bf16[4,4096]{1,0:T(4,128)(2,1)S(1)} collective-permute-done((bf16[4,4096]{1,0:T(4,128)(2,1)S(1)}, bf16[4,4096]{1,0:T(4,128)(2,1)S(1)}, u32[]{:S(2)}, u32[]{:S(2)}) %collective-permute-start.19) | collective-permute-done | bytes 32800 | tf_op jit(solution)/shard_map/ppermute | solution.py:309
  44.9 0.6 %finish.1 = bf16[4,4096]{1,0:T(4,128)(2,1)} custom-call(f32[4,4096]{1,0:T(4,128)S(1)} %get-tuple-element.51.refs_0_, bf16[4,4096]{1,0:T(4,128)(2,1)S(1)} %collective-permute-done.18.refs_1_, bf16[4,4096]{1,0:T(4,128)(2,1)S(1)} %collective-permute-done.19.refs_2_, bf16[4,4096]{1,0:T(4,128)(2,1)S(1)} %collective-permute-done.20.refs_3_), custom_call_target="tpu_custom_call" | custom-call | tf_op jit(solution)/shard_map/finish/pallas_call | solution.py:50
  (57 shorter events, 4.4 us)
Async XLA Ops:
  0.0 17.1 %slice-start.4 = ((s8[12582912]{0:T(1024)(128)(4,1)}), s8[4194304]{0:T(1024)(128)(4,1)S(1)}, s32[]{:S(2)}) async-start(s8[12582912]{0:T(1024)(128)(4,1)} %bitcast.4), calls=%async_computation.4 | async-start | bytes 8388608
  0.0 17.1 %slice-start.6 = ((s8[12582912]{0:T(1024)(128)(4,1)}), s8[4194304]{0:T(1024)(128)(4,1)S(1)}, s32[]{:S(2)}) async-start(s8[12582912]{0:T(1024)(128)(4,1)} %bitcast.6), calls=%async_computation.6 | async-start | bytes 8388608
  0.0 17.1 %slice-start.7 = ((s8[12582912]{0:T(1024)(128)(4,1)}), s8[4194304]{0:T(1024)(128)(4,1)S(1)}, s32[]{:S(2)}) async-start(s8[12582912]{0:T(1024)(128)(4,1)} %bitcast.6), calls=%async_computation.7 | async-start | bytes 8388608
  1.1 4.9 %collective-permute-start = (bf16[4,4352]{1,0:T(4,128)(2,1)S(1)}, bf16[4,4352]{1,0:T(4,128)(2,1)S(1)}, u32[]{:S(2)}, u32[]{:S(2)}) collective-permute-start(bf16[4,4352]{1,0:T(4,128)(2,1)S(1)} %prepare.1.refs_0_), channel_id=1, source_target_pairs={{0,2},{1,3},{2,0},{3,1},{4,6},{5,7},{6,4},{7,5},{8,10},{9,11},{10,... | collective-permute-start | bytes 104456 | tf_op jit(solution)/shard_map/ppermute | solution.py:309
  6.1 6.7 %collective-permute-start.1 = (bf16[8,4352]{1,0:T(8,128)(2,1)S(1)}, bf16[8,4352]{1,0:T(8,128)(2,1)S(1)}, u32[]{:S(2)}, u32[]{:S(2)}) collective-permute-start(bf16[8,4352]{1,0:T(8,128)(2,1)S(1)} %join.1.refs_0_), channel_id=1, source_target_pairs={{0,12},{4,8},{8,4},{12,0},{1,13},{5,9},{9,5},{13,1},{2,14},{6,10},... | collective-permute-start | bytes 208904 | tf_op jit(solution)/shard_map/ppermute | solution.py:309
  10.3 5.4 %collective-permute-start.2 = (bf16[8,4352]{1,0:T(8,128)(2,1)S(1)}, bf16[8,4352]{1,0:T(8,128)(2,1)S(1)}, u32[]{:S(2)}, u32[]{:S(2)}) collective-permute-start(bf16[8,4352]{1,0:T(8,128)(2,1)S(1)} %join.1.refs_0_), channel_id=1, source_target_pairs={{0,8},{4,12},{8,0},{12,4},{1,9},{5,13},{9,1},{13,5},{2,10},{6,14},... | collective-permute-start | bytes 208904 | tf_op jit(solution)/shard_map/ppermute | solution.py:309
  10.3 5.4 %collective-permute-start.3 = (bf16[8,4352]{1,0:T(8,128)(2,1)S(1)}, bf16[8,4352]{1,0:T(8,128)(2,1)S(1)}, u32[]{:S(2)}, u32[]{:S(2)}) collective-permute-start(bf16[8,4352]{1,0:T(8,128)(2,1)S(1)} %join.1.refs_0_), channel_id=1, source_target_pairs={{0,4},{4,0},{8,12},{12,8},{1,5},{5,1},{9,13},{13,9},{2,6},{6,2},{1... | collective-permute-start | bytes 208904 | tf_op jit(solution)/shard_map/ppermute | solution.py:309
  10.9 5.2 %collective-permute-start.4 = (bf16[8,4352]{1,0:T(8,128)(2,1)S(1)}, bf16[8,4352]{1,0:T(8,128)(2,1)S(1)}, u32[]{:S(2)}, u32[]{:S(2)}) collective-permute-start(bf16[8,4352]{1,0:T(8,128)(2,1)S(1)} %join.1.refs_0_), channel_id=1, source_target_pairs={{0,1},{1,0},{2,3},{3,2},{4,5},{5,4},{6,7},{7,6},{8,9},{9,8},{10,11... | collective-permute-start | bytes 208904 | tf_op jit(solution)/shard_map/ppermute | solution.py:309
  12.8 3.4 %collective-permute-start.5 = (bf16[8,4352]{1,0:T(8,128)(2,1)S(1)}, bf16[8,4352]{1,0:T(8,128)(2,1)S(1)}, u32[]{:S(2)}, u32[]{:S(2)}) collective-permute-start(bf16[8,4352]{1,0:T(8,128)(2,1)S(1)} %collective-permute-done.1.refs_1_), channel_id=1, source_target_pairs={{0,1},{1,0},{2,3},{3,2},{4,5},{5,4},{6,7},{7,6},{8,9},{9,8},{10,11... | collective-permute-start | bytes 208904 | tf_op jit(solution)/shard_map/ppermute | solution.py:309
  15.6 1.3 %collective-permute-start.6 = (bf16[8,4352]{1,0:T(8,128)(2,1)S(1)}, bf16[8,4352]{1,0:T(8,128)(2,1)S(1)}, u32[]{:S(2)}, u32[]{:S(2)}) collective-permute-start(bf16[8,4352]{1,0:T(8,128)(2,1)S(1)} %collective-permute-done.2.refs_2_), channel_id=1, source_target_pairs={{0,1},{1,0},{2,3},{3,2},{4,5},{5,4},{6,7},{7,6},{8,9},{9,8},{10,11... | collective-permute-start | bytes 208904 | tf_op jit(solution)/shard_map/ppermute | solution.py:309
  15.6 1.4 %collective-permute-start.7 = (bf16[8,4352]{1,0:T(8,128)(2,1)S(1)}, bf16[8,4352]{1,0:T(8,128)(2,1)S(1)}, u32[]{:S(2)}, u32[]{:S(2)}) collective-permute-start(bf16[8,4352]{1,0:T(8,128)(2,1)S(1)} %collective-permute-done.3.refs_3_), channel_id=1, source_target_pairs={{0,1},{1,0},{2,3},{3,2},{4,5},{5,4},{6,7},{7,6},{8,9},{9,8},{10,11... | collective-permute-start | bytes 208904 | tf_op jit(solution)/shard_map/ppermute | solution.py:309
  19.5 5.1 %collective-permute-start.12 = (bf16[2,64,384]{2,1,0:T(8,128)(2,1)S(1)}, bf16[2,64,384]{2,1,0:T(8,128)(2,1)S(1)}, u32[]{:S(2)}, u32[]{:S(2)}) collective-permute-start(bf16[2,64,384]{2,1,0:T(8,128)(2,1)S(1)} %get-tuple-element.33.refs_0_), channel_id=1, source_target_pairs={{0,2},{1,3},{2,0},{3,1},{4,6},{5,7},{6,4},{7,5},{8,10},{9,11},{10,... | collective-permute-start | bytes 294920 | tf_op jit(solution)/shard_map/ppermute | solution.py:309
  23.3 1.3 %collective-permute-start.9 = (bf16[2,48,384]{2,1,0:T(8,128)(2,1)S(1)}, bf16[2,48,384]{2,1,0:T(8,128)(2,1)S(1)}, u32[]{:S(2)}, u32[]{:S(2)}) collective-permute-start(bf16[2,48,384]{2,1,0:T(8,128)(2,1)S(1)} %get-tuple-element.34), channel_id=1, source_target_pairs={{0,1},{1,0},{2,3},{3,2},{4,5},{5,4},{6,7},{7,6},{8,9},{9,8},{10,11... | collective-permute-start | bytes 221192 | tf_op jit(solution)/shard_map/ppermute | solution.py:309
  23.4 1.4 %collective-permute-start.10 = (bf16[2,48,384]{2,1,0:T(8,128)(2,1)S(1)}, bf16[2,48,384]{2,1,0:T(8,128)(2,1)S(1)}, u32[]{:S(2)}, u32[]{:S(2)}) collective-permute-start(bf16[2,48,384]{2,1,0:T(8,128)(2,1)S(1)} %get-tuple-element.32), channel_id=1, source_target_pairs={{0,1},{1,0},{2,3},{3,2},{4,5},{5,4},{6,7},{7,6},{8,9},{9,8},{10,11... | collective-permute-start | bytes 221192 | tf_op jit(solution)/shard_map/ppermute | solution.py:309
  23.9 4.4 %collective-permute-start.8 = (bf16[2,48,384]{2,1,0:T(8,128)(2,1)S(1)}, bf16[2,48,384]{2,1,0:T(8,128)(2,1)S(1)}, u32[]{:S(2)}, u32[]{:S(2)}) collective-permute-start(bf16[2,48,384]{2,1,0:T(8,128)(2,1)S(1)} %get-tuple-element.32), channel_id=1, source_target_pairs={{0,2},{1,3},{2,0},{3,1},{4,6},{5,7},{6,4},{7,5},{8,10},{9,11},{10,... | collective-permute-start | bytes 221192 | tf_op jit(solution)/shard_map/ppermute | solution.py:309
  24.6 3.7 %collective-permute-start.13 = (bf16[2,64,384]{2,1,0:T(8,128)(2,1)S(1)}, bf16[2,64,384]{2,1,0:T(8,128)(2,1)S(1)}, u32[]{:S(2)}, u32[]{:S(2)}) collective-permute-start(bf16[2,64,384]{2,1,0:T(8,128)(2,1)S(1)} %collective-permute-done.12.refs_0_), channel_id=1, source_target_pairs={{0,1},{1,0},{2,3},{3,2},{4,5},{5,4},{6,7},{7,6},{8,9},{9,8},{10,11... | collective-permute-start | bytes 294920 | tf_op jit(solution)/shard_map/ppermute | solution.py:309
  28.2 1.3 %collective-permute-start.11 = (bf16[2,48,384]{2,1,0:T(8,128)(2,1)S(1)}, bf16[2,48,384]{2,1,0:T(8,128)(2,1)S(1)}, u32[]{:S(2)}, u32[]{:S(2)}) collective-permute-start(bf16[2,48,384]{2,1,0:T(8,128)(2,1)S(1)} %shard_map.109), channel_id=1, source_target_pairs={{0,1},{1,0},{2,3},{3,2},{4,5},{5,4},{6,7},{7,6},{8,9},{9,8},{10,11... | collective-permute-start | bytes 221192 | tf_op jit(solution)/shard_map/ppermute | solution.py:309
  30.5 1.4 %collective-permute-start.14 = (bf16[32,2048]{1,0:T(8,128)(2,1)S(1)}, bf16[32,2048]{1,0:T(8,128)(2,1)S(1)}, u32[]{:S(2)}, u32[]{:S(2)}) collective-permute-start(bf16[32,2048]{1,0:T(8,128)(2,1)S(1)} %get-tuple-element.43), channel_id=1, source_target_pairs={{0,1},{1,0},{2,3},{3,2},{4,5},{5,4},{6,7},{7,6},{8,9},{9,8},{10,11... | collective-permute-start | bytes 393224 | tf_op jit(solution)/shard_map/ppermute | solution.py:309
  31.6 1.4 %collective-permute-start.16 = (bf16[32,2048]{1,0:T(8,128)(2,1)S(1)}, bf16[32,2048]{1,0:T(8,128)(2,1)S(1)}, u32[]{:S(2)}, u32[]{:S(2)}) collective-permute-start(bf16[32,2048]{1,0:T(8,128)(2,1)S(1)} %get-tuple-element.48), channel_id=1, source_target_pairs={{0,1},{1,0},{2,3},{3,2},{4,5},{5,4},{6,7},{7,6},{8,9},{9,8},{10,11... | collective-permute-start | bytes 393224 | tf_op jit(solution)/shard_map/ppermute | solution.py:309
  32.0 4.7 %collective-permute-start.15 = (bf16[16,2048]{1,0:T(8,128)(2,1)S(1)}, bf16[16,2048]{1,0:T(8,128)(2,1)S(1)}, u32[]{:S(2)}, u32[]{:S(2)}) collective-permute-start(bf16[16,2048]{1,0:T(8,128)(2,1)S(1)} %get-tuple-element.45), channel_id=1, source_target_pairs={{0,2},{1,3},{2,0},{3,1},{4,6},{5,7},{6,4},{7,5},{8,10},{9,11},{10,... | collective-permute-start | bytes 196616 | tf_op jit(solution)/shard_map/ppermute | solution.py:309
  33.0 4.7 %collective-permute-start.17 = (bf16[16,2048]{1,0:T(8,128)(2,1)S(1)}, bf16[16,2048]{1,0:T(8,128)(2,1)S(1)}, u32[]{:S(2)}, u32[]{:S(2)}) collective-permute-start(bf16[16,2048]{1,0:T(8,128)(2,1)S(1)} %get-tuple-element.50), channel_id=1, source_target_pairs={{0,2},{1,3},{2,0},{3,1},{4,6},{5,7},{6,4},{7,5},{8,10},{9,11},{10,... | collective-permute-start | bytes 196616 | tf_op jit(solution)/shard_map/ppermute | solution.py:309
  37.8 5.9 %collective-permute-start.18 = (bf16[4,4096]{1,0:T(4,128)(2,1)S(1)}, bf16[4,4096]{1,0:T(4,128)(2,1)S(1)}, u32[]{:S(2)}, u32[]{:S(2)}) collective-permute-start(bf16[4,4096]{1,0:T(4,128)(2,1)S(1)} %get-tuple-element.52), channel_id=1, source_target_pairs={{0,12},{4,8},{8,4},{12,0},{1,13},{5,9},{9,5},{13,1},{2,14},{6,10},... | collective-permute-start | bytes 98312 | tf_op jit(solution)/shard_map/ppermute | solution.py:309
  40.0 4.8 %collective-permute-start.19 = (bf16[4,4096]{1,0:T(4,128)(2,1)S(1)}, bf16[4,4096]{1,0:T(4,128)(2,1)S(1)}, u32[]{:S(2)}, u32[]{:S(2)}) collective-permute-start(bf16[4,4096]{1,0:T(4,128)(2,1)S(1)} %get-tuple-element.53), channel_id=1, source_target_pairs={{0,8},{4,12},{8,0},{12,4},{1,9},{5,13},{9,1},{13,5},{2,10},{6,14},... | collective-permute-start | bytes 98312 | tf_op jit(solution)/shard_map/ppermute | solution.py:309
  40.0 4.8 %collective-permute-start.20 = (bf16[4,4096]{1,0:T(4,128)(2,1)S(1)}, bf16[4,4096]{1,0:T(4,128)(2,1)S(1)}, u32[]{:S(2)}, u32[]{:S(2)}) collective-permute-start(bf16[4,4096]{1,0:T(4,128)(2,1)S(1)} %get-tuple-element.54), channel_id=1, source_target_pairs={{0,4},{4,0},{8,12},{12,8},{1,5},{5,1},{9,13},{13,9},{2,6},{6,2},{1... | collective-permute-start | bytes 98312 | tf_op jit(solution)/shard_map/ppermute | solution.py:309
  (8 other events, 75.3 us)

commit v5 on v4

--- a/solution.py
+++ b/solution.py
@@ -83,17 +83,14 @@
     high = w.astype(BF).astype(F32)
     mid = (w - high).astype(BF).astype(F32)
     low = w - high - mid
-    block = jnp.zeros((rows, LANES), F32)
-    for i, value in enumerate((high, mid, low, place)):
-        block = jnp.where(piece == i, value, block)
-    y[:, width : width + LANES] = block.astype(BF)
-    y[:, width + LANES :] = jnp.zeros((rows, LANES), BF)
     pages = [
         owner[pl.ds(ten[r], 1), :] * SLOTS + slot[pl.ds(ten[r], 1), :] for r in range(rows)
     ]
-    y[:, width + LANES : width + LANES + EXPERTS] = (
-        jnp.concatenate(pages, axis=0).astype(F32).astype(BF)
-    )
+    slots = jnp.concatenate(pages, axis=0).astype(F32)
+    block = jnp.concatenate([slots] * (LANES // EXPERTS), axis=1)
+    for i, value in enumerate((high, mid, low, place)):
+        block = jnp.where(piece == i, value, block)
+    y[:, width:] = block.astype(BF)
 
 
 def join_blocks(count, *refs):
@@ -131,10 +128,10 @@
 
 
 def up_kernel(picked, each, *refs):
-    xs, info, gate, up, h, packed = refs
+    xs, info, gate, up, h, *packed = refs
     experts, width = gate.shape[0], gate.shape[1]
     first = lax.axis_index("expert") * experts
-    meta = info[:, :LANES].astype(F32)
+    meta = info[...].astype(F32)
     lane = lax.broadcasted_iota(jnp.int32, meta.shape, 1)
     weight = jnp.where(lane < PIECES * EXPERTS, meta, 0.0)
     step = 256
@@ -147,7 +144,9 @@
             b += jnp.dot(x, up[e, k : k + step], preferred_element_type=F32)
         hidden = (a * jax.nn.sigmoid(a) * b * w).astype(BF)
         h[i] = hidden
-        packed[i] = lax.dot_general(
+        if not packed:
+            continue
+        packed[0][i] = lax.dot_general(
             picks(meta, lane, first + e, each, 0),
             hidden,
             (((0,), (0,)), ((), ())),
@@ -185,7 +184,7 @@
         across = slice(cut * (cols // PARTS), (cut + 1) * (cols // PARTS))
         base = base[:, across]
     first = lax.axis_index("expert") * experts
-    meta = info[:, :LANES].astype(F32)
+    meta = info[...].astype(F32)
     lane16 = lax.broadcasted_iota(jnp.int32, meta.shape, 1)
     lane = lax.broadcasted_iota(jnp.int32, (rows, ranks), 1)
 
@@ -201,6 +200,8 @@
     def ordered(ref, i, e, m):
         if m == 0:
             return ref[i]
+        if ref.shape[1] == rows and m == 1:
+            return jnp.concatenate([ref[i, half:], ref[i, :half]], axis=0)
         if ref.shape[1] == rows:
             return jnp.dot(turned(m), ref[i], preferred_element_type=F32).astype(BF)
         known = spreads is not None and m in flips
@@ -234,11 +235,10 @@
     if opens:
         refs[0][...] = base
         refs[1][...] = small
-        values = info[:, LANES:].astype(F32)
         rank = per // SLOTS
         away = jnp.full((rows, ranks), -1.0, F32)
         for e in range(experts):
-            value = column(values, lane16, first + e)
+            value = column(meta, lane16, (PIECES + 1) * EXPERTS + first + e)
             for s in range(SLOTS):
                 low = e * per + s * rank
                 inside = (lane >= low) & (lane < low + rank)
@@ -299,7 +299,7 @@
     n_x = n_dp // 2
     rows, width = tokens.shape
     experts, _, part = gate.shape
-    wide = width + 2 * LANES
+    wide = width + LANES
     block = rows * n_x
     half_rows = block * n_z
     all_rows = 2 * half_rows
@@ -346,31 +346,31 @@
     with jax.named_scope("gather"):
         xs, info = call(
             functools.partial(gather_rows, places),
-            [shape((all_rows, width)), shape((all_rows, 2 * LANES))],
+            [shape((all_rows, width)), shape((all_rows, LANES))],
             gathered,
         )
     hidden = []
     for picked in lists:
         with jax.named_scope("up"):
-            h, packed = call(
+            outs = [shape((len(picked), all_rows, part))]
+            if picked is lists[-1]:
+                outs.append(shape((len(picked), packed_rows, part)))
+            h, *packed = call(
                 functools.partial(up_kernel, picked, rows),
-                [
-                    shape((len(picked), all_rows, part)),
-                    shape((len(picked), packed_rows, part)),
-                ],
+                outs,
                 (xs, info, in_vmem(gate), in_vmem(up)),
                 room=(4 << 20) + 4 * all_rows * (packed_rows + 4 * part + 8 * LANES),
             )
-        hidden.append({0: h, "packed": packed})
+        hidden.append({0: h, "sent": packed[0] if packed else h})
     for got in hidden:
-        moved = {0: got["packed"] if got is hidden[-1] else got[0]}
+        moved = {0: got["sent"]}
         for b in x_bits:
             moved.update({m | b: over(a, "dp", b) for m, a in moved.items()})
         got.update({m: a for m, a in moved.items() if m})
 
     def between_cores(got, pairs, behind=()):
         for m in pairs:
-            x = got[m] if m else got["packed"]
+            x = got[m] if m else got["sent"]
             if behind:
                 x = call(relay, shape(x.shape), (x, *behind))
             got[m ^ 1] = over(x, "dp", 1)

time: 45.7 us -> 45.4 us (level)
  no operation moved by 1% of the time
where the time goes in v5:
time: 45.4 us; the launch traced here: 45.2 us
  starting transfers between devices  18 us (40%)
  waiting for transfers between devices  16.4 us (36%)
  Pallas kernels  10.5 us (23%)
    ppermute x21, starting transfers between devices, over(): lax.ppermute(x, axis, [(i, i ^ m) for i in range(lax.axis_size(axis))])  18 us
    ppermute x21, waiting for transfers between devices, over(): lax.ppermute(x, axis, [(i, i ^ m) for i in range(lax.axis_size(axis))])  16.4 us
    pallas_call x14, Pallas kernels, call(): pl.pallas_call(body, out_shape=out_shape, in_specs=specs, out_specs=jax.t...  10.5 us
  transfers between devices with their start and end apart: 21, of which 15 were waited for; matrix products, arithmetic and copies ran while one was open for 0% of the time, Pallas kernels for 13%

profile of v5, /device:TPU:0, one launch (start us, length us, event | category | flops | bytes accessed | tf_op | source)
XLA Modules:
  0.0 45.2 jit_solution(12592736437608804821)
XLA Ops:
  0.0 1.1 %prepare.1.refs_0_ = bf16[4,4224]{1,0:T(4,128)(2,1)S(1)} custom-call(s32[4]{0:T(128)} %refs_0_.1, bf16[4,4096]{1,0:T(4,128)(2,1)} %refs_1_.1, s32[4,8]{1,0:T(4,128)} %refs_2_.4, f32[4,8]{1,0:T(4,128)} %refs_3_.7, s32[8,16]{1,0:T(8,128)} %refs_4_.2, s32[8,16]{1,0:T(8,128)} %refs_5_.2, bf16[4,4096,384]{2,1,0:T(8,128)(2,1)} %refs_2_.7, ...), custom_call_target="tpu_custom_call" | custom-call | tf_op jit(solution)/shard_map/prepare/pallas_call | solution.py:50
  1.1 3.0 %collective-permute-start = (bf16[4,4224]{1,0:T(4,128)(2,1)S(1)}, bf16[4,4224]{1,0:T(4,128)(2,1)S(1)}, u32[]{:S(2)}, u32[]{:S(2)}) collective-permute-start(bf16[4,4224]{1,0:T(4,128)(2,1)S(1)} %prepare.1.refs_0_), channel_id=1, source_target_pairs={{0,2},{1,3},{2,0},{3,1},{4,6},{5,7},{6,4},{7,5},{8,10},{9,11},{10,... | collective-permute-start | bytes 101384 | tf_op jit(solution)/shard_map/ppermute | solution.py:309
  4.1 1.9 %collective-permute-done.refs_1_ = bf16[4,4224]{1,0:T(4,128)(2,1)S(1)} collective-permute-done((bf16[4,4224]{1,0:T(4,128)(2,1)S(1)}, bf16[4,4224]{1,0:T(4,128)(2,1)S(1)}, u32[]{:S(2)}, u32[]{:S(2)}) %collective-permute-start) | collective-permute-done | bytes 33824 | tf_op jit(solution)/shard_map/ppermute | solution.py:309
  6.1 4.2 %collective-permute-start.1 = (bf16[8,4224]{1,0:T(8,128)(2,1)S(1)}, bf16[8,4224]{1,0:T(8,128)(2,1)S(1)}, u32[]{:S(2)}, u32[]{:S(2)}) collective-permute-start(bf16[8,4224]{1,0:T(8,128)(2,1)S(1)} %join.1.refs_0_), channel_id=1, source_target_pairs={{0,12},{4,8},{8,4},{12,0},{1,13},{5,9},{9,5},{13,1},{2,14},{6,10},... | collective-permute-start | bytes 202760 | tf_op jit(solution)/shard_map/ppermute | solution.py:309
  10.3 0.6 %collective-permute-start.3 = (bf16[8,4224]{1,0:T(8,128)(2,1)S(1)}, bf16[8,4224]{1,0:T(8,128)(2,1)S(1)}, u32[]{:S(2)}, u32[]{:S(2)}) collective-permute-start(bf16[8,4224]{1,0:T(8,128)(2,1)S(1)} %join.1.refs_0_), channel_id=1, source_target_pairs={{0,4},{4,0},{8,12},{12,8},{1,5},{5,1},{9,13},{13,9},{2,6},{6,2},{1... | collective-permute-start | bytes 202760 | tf_op jit(solution)/shard_map/ppermute | solution.py:309
  10.9 1.8 %collective-permute-done.1.refs_1_ = bf16[8,4224]{1,0:T(8,128)(2,1)S(1)} collective-permute-done((bf16[8,4224]{1,0:T(8,128)(2,1)S(1)}, bf16[8,4224]{1,0:T(8,128)(2,1)S(1)}, u32[]{:S(2)}, u32[]{:S(2)}) %collective-permute-start.1) | collective-permute-done | bytes 67616 | tf_op jit(solution)/shard_map/ppermute | solution.py:309
  12.7 2.8 %collective-permute-done.2.refs_2_ = bf16[8,4224]{1,0:T(8,128)(2,1)S(1)} collective-permute-done((bf16[8,4224]{1,0:T(8,128)(2,1)S(1)}, bf16[8,4224]{1,0:T(8,128)(2,1)S(1)}, u32[]{:S(2)}, u32[]{:S(2)}) %collective-permute-start.2) | collective-permute-done | bytes 67616 | tf_op jit(solution)/shard_map/ppermute | solution.py:309
  16.0 0.7 %collective-permute-done.6.refs_6_ = bf16[8,4224]{1,0:T(8,128)(2,1)S(1)} collective-permute-done((bf16[8,4224]{1,0:T(8,128)(2,1)S(1)}, bf16[8,4224]{1,0:T(8,128)(2,1)S(1)}, u32[]{:S(2)}, u32[]{:S(2)}) %collective-permute-start.6) | collective-permute-done | bytes 67616 | tf_op jit(solution)/shard_map/ppermute | solution.py:309
  17.1 2.0 %up.3.refs_0_ = bf16[2,64,384]{2,1,0:T(8,128)(2,1)S(1)} custom-call(bf16[64,4096]{1,0:T(8,128)(2,1)S(1)} %get-tuple-element.28.refs_0_, bf16[64,128]{1,0:T(8,128)(2,1)S(1)} %get-tuple-element.29.refs_1_.refs_4_.refs_2_, bf16[4,4096,384]{2,1,0:T(8,128)(2,1)S(1)} %bitcast.5, bf16[4,4096,384]{2,1,0:T(8,128)(2,1)S(1)} %bitcast.7), custom_call_target="tpu_custom_call" | custom-call | tf_op jit(solution)/shard_map/up/pallas_call | solution.py:50
  19.1 1.6 %collective-permute-start.12 = (bf16[2,64,384]{2,1,0:T(8,128)(2,1)S(1)}, bf16[2,64,384]{2,1,0:T(8,128)(2,1)S(1)}, u32[]{:S(2)}, u32[]{:S(2)}) collective-permute-start(bf16[2,64,384]{2,1,0:T(8,128)(2,1)S(1)} %up.3.refs_0_), channel_id=1, source_target_pairs={{0,2},{1,3},{2,0},{3,1},{4,6},{5,7},{6,4},{7,5},{8,10},{9,11},{10,... | collective-permute-start | bytes 294920 | tf_op jit(solution)/shard_map/ppermute | solution.py:309
  20.7 2.2 %up.2 = (bf16[2,64,384]{2,1,0:T(8,128)(2,1)S(1)}, bf16[2,48,384]{2,1,0:T(8,128)(2,1)S(1)}) custom-call(bf16[64,4096]{1,0:T(8,128)(2,1)S(1)} %get-tuple-element.28.refs_0_, bf16[64,128]{1,0:T(8,128)(2,1)S(1)} %get-tuple-element.29.refs_1_.refs_4_.refs_2_, bf16[4,4096,384]{2,1,0:T(8,128)(2,1)S(1)} %bitcast.5, bf16[4,4096,384]{2,1,0:T(8,128)(2,1)S(1)} %bitcast.7), custom_call_target="tpu_custom_call" | custom-call | tf_op jit(solution)/shard_map/up/pallas_call | solution.py:50
  24.4 1.7 %down.4 = (f32[64,1024]{1,0:T(8,128)S(1)}, f32[64,128]{1,0:T(8,128)S(1)}, f32[64,128]{1,0:T(8,128)S(1)}, bf16[8,64,48]{2,1,0:T(8,128)(2,1)S(1)}) custom-call(bf16[2,64,384]{2,1,0:T(8,128)(2,1)S(1)} %up.3.refs_0_, bf16[2,64,384]{2,1,0:T(8,128)(2,1)S(1)} %collective-permute-done.9.refs_1_, bf16[2,64,384]{2,1,0:T(8,128)(2,1)S(1)} %get-tuple-element.31.refs_2_, ...), custom_call_target="tpu_custom_call" | custom-call | tf_op jit(solution)/shard_map/down/pallas_call | solution.py:50
  26.2 1.7 %collective-permute-done.8.x.refs_0_ = bf16[2,48,384]{2,1,0:T(8,128)(2,1)S(1)} collective-permute-done((bf16[2,48,384]{2,1,0:T(8,128)(2,1)S(1)}, bf16[2,48,384]{2,1,0:T(8,128)(2,1)S(1)}, u32[]{:S(2)}, u32[]{:S(2)}) %collective-permute-start.8) | collective-permute-done | bytes 73760 | tf_op jit(solution)/shard_map/ppermute | solution.py:309
  27.9 1.0 %down.5 = (f32[64,1024]{1,0:T(8,128)S(1)}, f32[64,128]{1,0:T(8,128)S(1)}) custom-call(bf16[2,64,384]{2,1,0:T(8,128)(2,1)S(1)} %collective-permute-done.12.refs_0_, bf16[2,64,384]{2,1,0:T(8,128)(2,1)S(1)} %collective-permute-done.13.refs_1_, bf16[64,128]{1,0:T(8,128)(2,1)S(1)} %get-tuple-element.29.refs_1_.refs_4_.refs_2_, ...), custom_call_target="tpu_custom_call" | custom-call | tf_op jit(solution)/shard_map/down/pallas_call | solution.py:50
  29.2 1.0 %down.6 = (f32[32,2048]{1,0:T(8,128)S(1)}, bf16[32,2048]{1,0:T(8,128)(2,1)S(1)}, bf16[64,128]{1,0:T(8,128)(2,1)S(1)}) custom-call(bf16[2,48,384]{2,1,0:T(8,128)(2,1)S(1)} %collective-permute-done.8.x.refs_0_, bf16[2,48,384]{2,1,0:T(8,128)(2,1)S(1)} %collective-permute-done.11.refs_1_, bf16[64,128]{1,0:T(8,128)(2,1)S(1)} %get-tuple-element.29.refs_1_.refs_4_.refs_2_, ...), custom_call_target="tpu_custom_call" | custom-call | tf_op jit(solution)/shard_map/down/pallas_call | solution.py:50
  30.5 0.7 %down.7 = (f32[32,2048]{1,0:T(8,128)S(1)}, bf16[32,2048]{1,0:T(8,128)(2,1)S(1)}) custom-call(bf16[2,48,384]{2,1,0:T(8,128)(2,1)S(1)} %collective-permute-done.8.x.refs_0_, bf16[2,48,384]{2,1,0:T(8,128)(2,1)S(1)} %collective-permute-done.11.refs_1_, bf16[64,128]{1,0:T(8,128)(2,1)S(1)} %get-tuple-element.29.refs_1_.refs_4_.refs_2_, ...), custom_call_target="tpu_custom_call" | custom-call | tf_op jit(solution)/shard_map/down/pallas_call | solution.py:50
  32.7 1.2 %collective-permute-start.17 = (bf16[16,2048]{1,0:T(8,128)(2,1)S(1)}, bf16[16,2048]{1,0:T(8,128)(2,1)S(1)}, u32[]{:S(2)}, u32[]{:S(2)}) collective-permute-start(bf16[16,2048]{1,0:T(8,128)(2,1)S(1)} %get-tuple-element.46), channel_id=1, source_target_pairs={{0,2},{1,3},{2,0},{3,1},{4,6},{5,7},{6,4},{7,5},{8,10},{9,11},{10,... | collective-permute-start | bytes 196616 | tf_op jit(solution)/shard_map/ppermute | solution.py:309
  33.8 2.5 %collective-permute-done.15.refs_1_ = bf16[16,2048]{1,0:T(8,128)(2,1)S(1)} collective-permute-done((bf16[16,2048]{1,0:T(8,128)(2,1)S(1)}, bf16[16,2048]{1,0:T(8,128)(2,1)S(1)}, u32[]{:S(2)}, u32[]{:S(2)}) %collective-permute-start.15) | collective-permute-done | bytes 65568 | tf_op jit(solution)/shard_map/ppermute | solution.py:309
  36.3 1.0 %collective-permute-done.17.refs_3_ = bf16[16,2048]{1,0:T(8,128)(2,1)S(1)} collective-permute-done((bf16[16,2048]{1,0:T(8,128)(2,1)S(1)}, bf16[16,2048]{1,0:T(8,128)(2,1)S(1)}, u32[]{:S(2)}, u32[]{:S(2)}) %collective-permute-start.17) | collective-permute-done | bytes 65568 | tf_op jit(solution)/shard_map/ppermute | solution.py:309
  37.4 2.2 %collective-permute-start.18 = (bf16[4,4096]{1,0:T(4,128)(2,1)S(1)}, bf16[4,4096]{1,0:T(4,128)(2,1)S(1)}, u32[]{:S(2)}, u32[]{:S(2)}) collective-permute-start(bf16[4,4096]{1,0:T(4,128)(2,1)S(1)} %get-tuple-element.48), channel_id=1, source_target_pairs={{0,12},{4,8},{8,4},{12,0},{1,13},{5,9},{9,5},{13,1},{2,14},{6,10},... | collective-permute-start | bytes 98312 | tf_op jit(solution)/shard_map/ppermute | solution.py:309
  39.6 2.2 %collective-permute-start.20 = (bf16[4,4096]{1,0:T(4,128)(2,1)S(1)}, bf16[4,4096]{1,0:T(4,128)(2,1)S(1)}, u32[]{:S(2)}, u32[]{:S(2)}) collective-permute-start(bf16[4,4096]{1,0:T(4,128)(2,1)S(1)} %get-tuple-element.50), channel_id=1, source_target_pairs={{0,4},{4,0},{8,12},{12,8},{1,5},{5,1},{9,13},{13,9},{2,6},{6,2},{1... | collective-permute-start | bytes 98312 | tf_op jit(solution)/shard_map/ppermute | solution.py:309
  41.8 1.4 %collective-permute-done.18.refs_1_ = bf16[4,4096]{1,0:T(4,128)(2,1)S(1)} collective-permute-done((bf16[4,4096]{1,0:T(4,128)(2,1)S(1)}, bf16[4,4096]{1,0:T(4,128)(2,1)S(1)}, u32[]{:S(2)}, u32[]{:S(2)}) %collective-permute-start.18) | collective-permute-done | bytes 32800 | tf_op jit(solution)/shard_map/ppermute | solution.py:309
  43.3 1.3 %collective-permute-done.19.refs_2_ = bf16[4,4096]{1,0:T(4,128)(2,1)S(1)} collective-permute-done((bf16[4,4096]{1,0:T(4,128)(2,1)S(1)}, bf16[4,4096]{1,0:T(4,128)(2,1)S(1)}, u32[]{:S(2)}, u32[]{:S(2)}) %collective-permute-start.19) | collective-permute-done | bytes 32800 | tf_op jit(solution)/shard_map/ppermute | solution.py:309
  44.6 0.6 %finish.1 = bf16[4,4096]{1,0:T(4,128)(2,1)} custom-call(f32[4,4096]{1,0:T(4,128)S(1)} %get-tuple-element.47.refs_0_, bf16[4,4096]{1,0:T(4,128)(2,1)S(1)} %collective-permute-done.18.refs_1_, bf16[4,4096]{1,0:T(4,128)(2,1)S(1)} %collective-permute-done.19.refs_2_, bf16[4,4096]{1,0:T(4,128)(2,1)S(1)} %collective-permute-done.20.refs_3_), custom_call_target="tpu_custom_call" | custom-call | tf_op jit(solution)/shard_map/finish/pallas_call | solution.py:50
  (57 shorter events, 4.5 us)
Async XLA Ops:
  0.0 17.0 %slice-start.4 = ((s8[12582912]{0:T(1024)(128)(4,1)}), s8[4194304]{0:T(1024)(128)(4,1)S(1)}, s32[]{:S(2)}) async-start(s8[12582912]{0:T(1024)(128)(4,1)} %bitcast.4), calls=%async_computation.4 | async-start | bytes 8388608
  0.0 17.0 %slice-start.6 = ((s8[12582912]{0:T(1024)(128)(4,1)}), s8[4194304]{0:T(1024)(128)(4,1)S(1)}, s32[]{:S(2)}) async-start(s8[12582912]{0:T(1024)(128)(4,1)} %bitcast.6), calls=%async_computation.6 | async-start | bytes 8388608
  0.0 17.0 %slice-start.7 = ((s8[12582912]{0:T(1024)(128)(4,1)}), s8[4194304]{0:T(1024)(128)(4,1)S(1)}, s32[]{:S(2)}) async-start(s8[12582912]{0:T(1024)(128)(4,1)} %bitcast.6), calls=%async_computation.7 | async-start | bytes 8388608
  1.1 4.9 %collective-permute-start = (bf16[4,4224]{1,0:T(4,128)(2,1)S(1)}, bf16[4,4224]{1,0:T(4,128)(2,1)S(1)}, u32[]{:S(2)}, u32[]{:S(2)}) collective-permute-start(bf16[4,4224]{1,0:T(4,128)(2,1)S(1)} %prepare.1.refs_0_), channel_id=1, source_target_pairs={{0,2},{1,3},{2,0},{3,1},{4,6},{5,7},{6,4},{7,5},{8,10},{9,11},{10,... | collective-permute-start | bytes 101384 | tf_op jit(solution)/shard_map/ppermute | solution.py:309
  6.1 6.7 %collective-permute-start.1 = (bf16[8,4224]{1,0:T(8,128)(2,1)S(1)}, bf16[8,4224]{1,0:T(8,128)(2,1)S(1)}, u32[]{:S(2)}, u32[]{:S(2)}) collective-permute-start(bf16[8,4224]{1,0:T(8,128)(2,1)S(1)} %join.1.refs_0_), channel_id=1, source_target_pairs={{0,12},{4,8},{8,4},{12,0},{1,13},{5,9},{9,5},{13,1},{2,14},{6,10},... | collective-permute-start | bytes 202760 | tf_op jit(solution)/shard_map/ppermute | solution.py:309
  10.3 5.3 %collective-permute-start.2 = (bf16[8,4224]{1,0:T(8,128)(2,1)S(1)}, bf16[8,4224]{1,0:T(8,128)(2,1)S(1)}, u32[]{:S(2)}, u32[]{:S(2)}) collective-permute-start(bf16[8,4224]{1,0:T(8,128)(2,1)S(1)} %join.1.refs_0_), channel_id=1, source_target_pairs={{0,8},{4,12},{8,0},{12,4},{1,9},{5,13},{9,1},{13,5},{2,10},{6,14},... | collective-permute-start | bytes 202760 | tf_op jit(solution)/shard_map/ppermute | solution.py:309
  10.3 5.3 %collective-permute-start.3 = (bf16[8,4224]{1,0:T(8,128)(2,1)S(1)}, bf16[8,4224]{1,0:T(8,128)(2,1)S(1)}, u32[]{:S(2)}, u32[]{:S(2)}) collective-permute-start(bf16[8,4224]{1,0:T(8,128)(2,1)S(1)} %join.1.refs_0_), channel_id=1, source_target_pairs={{0,4},{4,0},{8,12},{12,8},{1,5},{5,1},{9,13},{13,9},{2,6},{6,2},{1... | collective-permute-start | bytes 202760 | tf_op jit(solution)/shard_map/ppermute | solution.py:309
  10.9 5.1 %collective-permute-start.4 = (bf16[8,4224]{1,0:T(8,128)(2,1)S(1)}, bf16[8,4224]{1,0:T(8,128)(2,1)S(1)}, u32[]{:S(2)}, u32[]{:S(2)}) collective-permute-start(bf16[8,4224]{1,0:T(8,128)(2,1)S(1)} %join.1.refs_0_), channel_id=1, source_target_pairs={{0,1},{1,0},{2,3},{3,2},{4,5},{5,4},{6,7},{7,6},{8,9},{9,8},{10,11... | collective-permute-start | bytes 202760 | tf_op jit(solution)/shard_map/ppermute | solution.py:309
  12.7 3.3 %collective-permute-start.5 = (bf16[8,4224]{1,0:T(8,128)(2,1)S(1)}, bf16[8,4224]{1,0:T(8,128)(2,1)S(1)}, u32[]{:S(2)}, u32[]{:S(2)}) collective-permute-start(bf16[8,4224]{1,0:T(8,128)(2,1)S(1)} %collective-permute-done.1.refs_1_), channel_id=1, source_target_pairs={{0,1},{1,0},{2,3},{3,2},{4,5},{5,4},{6,7},{7,6},{8,9},{9,8},{10,11... | collective-permute-start | bytes 202760 | tf_op jit(solution)/shard_map/ppermute | solution.py:309
  15.5 1.3 %collective-permute-start.6 = (bf16[8,4224]{1,0:T(8,128)(2,1)S(1)}, bf16[8,4224]{1,0:T(8,128)(2,1)S(1)}, u32[]{:S(2)}, u32[]{:S(2)}) collective-permute-start(bf16[8,4224]{1,0:T(8,128)(2,1)S(1)} %collective-permute-done.2.refs_2_), channel_id=1, source_target_pairs={{0,1},{1,0},{2,3},{3,2},{4,5},{5,4},{6,7},{7,6},{8,9},{9,8},{10,11... | collective-permute-start | bytes 202760 | tf_op jit(solution)/shard_map/ppermute | solution.py:309
  15.5 1.4 %collective-permute-start.7 = (bf16[8,4224]{1,0:T(8,128)(2,1)S(1)}, bf16[8,4224]{1,0:T(8,128)(2,1)S(1)}, u32[]{:S(2)}, u32[]{:S(2)}) collective-permute-start(bf16[8,4224]{1,0:T(8,128)(2,1)S(1)} %collective-permute-done.3.refs_3_), channel_id=1, source_target_pairs={{0,1},{1,0},{2,3},{3,2},{4,5},{5,4},{6,7},{7,6},{8,9},{9,8},{10,11... | collective-permute-start | bytes 202760 | tf_op jit(solution)/shard_map/ppermute | solution.py:309
  19.1 5.1 %collective-permute-start.12 = (bf16[2,64,384]{2,1,0:T(8,128)(2,1)S(1)}, bf16[2,64,384]{2,1,0:T(8,128)(2,1)S(1)}, u32[]{:S(2)}, u32[]{:S(2)}) collective-permute-start(bf16[2,64,384]{2,1,0:T(8,128)(2,1)S(1)} %up.3.refs_0_), channel_id=1, source_target_pairs={{0,2},{1,3},{2,0},{3,1},{4,6},{5,7},{6,4},{7,5},{8,10},{9,11},{10,... | collective-permute-start | bytes 294920 | tf_op jit(solution)/shard_map/ppermute | solution.py:309
  20.7 3.7 %collective-permute-start.9 = (bf16[2,64,384]{2,1,0:T(8,128)(2,1)S(1)}, bf16[2,64,384]{2,1,0:T(8,128)(2,1)S(1)}, u32[]{:S(2)}, u32[]{:S(2)}) collective-permute-start(bf16[2,64,384]{2,1,0:T(8,128)(2,1)S(1)} %up.3.refs_0_), channel_id=1, source_target_pairs={{0,1},{1,0},{2,3},{3,2},{4,5},{5,4},{6,7},{7,6},{8,9},{9,8},{10,11... | collective-permute-start | bytes 294920 | tf_op jit(solution)/shard_map/ppermute | solution.py:309
  23.0 1.4 %collective-permute-start.10 = (bf16[2,48,384]{2,1,0:T(8,128)(2,1)S(1)}, bf16[2,48,384]{2,1,0:T(8,128)(2,1)S(1)}, u32[]{:S(2)}, u32[]{:S(2)}) collective-permute-start(bf16[2,48,384]{2,1,0:T(8,128)(2,1)S(1)} %get-tuple-element.30), channel_id=1, source_target_pairs={{0,1},{1,0},{2,3},{3,2},{4,5},{5,4},{6,7},{7,6},{8,9},{9,8},{10,11... | collective-permute-start | bytes 221192 | tf_op jit(solution)/shard_map/ppermute | solution.py:309
  23.5 4.4 %collective-permute-start.8 = (bf16[2,48,384]{2,1,0:T(8,128)(2,1)S(1)}, bf16[2,48,384]{2,1,0:T(8,128)(2,1)S(1)}, u32[]{:S(2)}, u32[]{:S(2)}) collective-permute-start(bf16[2,48,384]{2,1,0:T(8,128)(2,1)S(1)} %get-tuple-element.30), channel_id=1, source_target_pairs={{0,2},{1,3},{2,0},{3,1},{4,6},{5,7},{6,4},{7,5},{8,10},{9,11},{10,... | collective-permute-start | bytes 221192 | tf_op jit(solution)/shard_map/ppermute | solution.py:309
  24.2 3.7 %collective-permute-start.13 = (bf16[2,64,384]{2,1,0:T(8,128)(2,1)S(1)}, bf16[2,64,384]{2,1,0:T(8,128)(2,1)S(1)}, u32[]{:S(2)}, u32[]{:S(2)}) collective-permute-start(bf16[2,64,384]{2,1,0:T(8,128)(2,1)S(1)} %collective-permute-done.12.refs_0_), channel_id=1, source_target_pairs={{0,1},{1,0},{2,3},{3,2},{4,5},{5,4},{6,7},{7,6},{8,9},{9,8},{10,11... | collective-permute-start | bytes 294920 | tf_op jit(solution)/shard_map/ppermute | solution.py:309
  27.9 1.3 %collective-permute-start.11 = (bf16[2,48,384]{2,1,0:T(8,128)(2,1)S(1)}, bf16[2,48,384]{2,1,0:T(8,128)(2,1)S(1)}, u32[]{:S(2)}, u32[]{:S(2)}) collective-permute-start(bf16[2,48,384]{2,1,0:T(8,128)(2,1)S(1)} %shard_map.109), channel_id=1, source_target_pairs={{0,1},{1,0},{2,3},{3,2},{4,5},{5,4},{6,7},{7,6},{8,9},{9,8},{10,11... | collective-permute-start | bytes 221192 | tf_op jit(solution)/shard_map/ppermute | solution.py:309
  30.2 1.4 %collective-permute-start.14 = (bf16[32,2048]{1,0:T(8,128)(2,1)S(1)}, bf16[32,2048]{1,0:T(8,128)(2,1)S(1)}, u32[]{:S(2)}, u32[]{:S(2)}) collective-permute-start(bf16[32,2048]{1,0:T(8,128)(2,1)S(1)} %get-tuple-element.39), channel_id=1, source_target_pairs={{0,1},{1,0},{2,3},{3,2},{4,5},{5,4},{6,7},{7,6},{8,9},{9,8},{10,11... | collective-permute-start | bytes 393224 | tf_op jit(solution)/shard_map/ppermute | solution.py:309
  31.2 1.4 %collective-permute-start.16 = (bf16[32,2048]{1,0:T(8,128)(2,1)S(1)}, bf16[32,2048]{1,0:T(8,128)(2,1)S(1)}, u32[]{:S(2)}, u32[]{:S(2)}) collective-permute-start(bf16[32,2048]{1,0:T(8,128)(2,1)S(1)} %get-tuple-element.44), channel_id=1, source_target_pairs={{0,1},{1,0},{2,3},{3,2},{4,5},{5,4},{6,7},{7,6},{8,9},{9,8},{10,11... | collective-permute-start | bytes 393224 | tf_op jit(solution)/shard_map/ppermute | solution.py:309
  31.6 4.7 %collective-permute-start.15 = (bf16[16,2048]{1,0:T(8,128)(2,1)S(1)}, bf16[16,2048]{1,0:T(8,128)(2,1)S(1)}, u32[]{:S(2)}, u32[]{:S(2)}) collective-permute-start(bf16[16,2048]{1,0:T(8,128)(2,1)S(1)} %get-tuple-element.41), channel_id=1, source_target_pairs={{0,2},{1,3},{2,0},{3,1},{4,6},{5,7},{6,4},{7,5},{8,10},{9,11},{10,... | collective-permute-start | bytes 196616 | tf_op jit(solution)/shard_map/ppermute | solution.py:309
  32.7 4.7 %collective-permute-start.17 = (bf16[16,2048]{1,0:T(8,128)(2,1)S(1)}, bf16[16,2048]{1,0:T(8,128)(2,1)S(1)}, u32[]{:S(2)}, u32[]{:S(2)}) collective-permute-start(bf16[16,2048]{1,0:T(8,128)(2,1)S(1)} %get-tuple-element.46), channel_id=1, source_target_pairs={{0,2},{1,3},{2,0},{3,1},{4,6},{5,7},{6,4},{7,5},{8,10},{9,11},{10,... | collective-permute-start | bytes 196616 | tf_op jit(solution)/shard_map/ppermute | solution.py:309
  37.4 5.9 %collective-permute-start.18 = (bf16[4,4096]{1,0:T(4,128)(2,1)S(1)}, bf16[4,4096]{1,0:T(4,128)(2,1)S(1)}, u32[]{:S(2)}, u32[]{:S(2)}) collective-permute-start(bf16[4,4096]{1,0:T(4,128)(2,1)S(1)} %get-tuple-element.48), channel_id=1, source_target_pairs={{0,12},{4,8},{8,4},{12,0},{1,13},{5,9},{9,5},{13,1},{2,14},{6,10},... | collective-permute-start | bytes 98312 | tf_op jit(solution)/shard_map/ppermute | solution.py:309
  39.6 5.0 %collective-permute-start.19 = (bf16[4,4096]{1,0:T(4,128)(2,1)S(1)}, bf16[4,4096]{1,0:T(4,128)(2,1)S(1)}, u32[]{:S(2)}, u32[]{:S(2)}) collective-permute-start(bf16[4,4096]{1,0:T(4,128)(2,1)S(1)} %get-tuple-element.49), channel_id=1, source_target_pairs={{0,8},{4,12},{8,0},{12,4},{1,9},{5,13},{9,1},{13,5},{2,10},{6,14},... | collective-permute-start | bytes 98312 | tf_op jit(solution)/shard_map/ppermute | solution.py:309
  39.6 5.0 %collective-permute-start.20 = (bf16[4,4096]{1,0:T(4,128)(2,1)S(1)}, bf16[4,4096]{1,0:T(4,128)(2,1)S(1)}, u32[]{:S(2)}, u32[]{:S(2)}) collective-permute-start(bf16[4,4096]{1,0:T(4,128)(2,1)S(1)} %get-tuple-element.50), channel_id=1, source_target_pairs={{0,4},{4,0},{8,12},{12,8},{1,5},{5,1},{9,13},{13,9},{2,6},{6,2},{1... | collective-permute-start | bytes 98312 | tf_op jit(solution)/shard_map/ppermute | solution.py:309
  (8 other events, 78.9 us)

commit v6 on v5

--- a/solution.py
+++ b/solution.py
@@ -43,7 +43,7 @@
     return total
 
 
-def call(body, out_shape, operands, specs=None, room=2 << 20, scratch=()):
+def call(body, out_shape, operands, specs=None, room=2 << 20, scratch=(), in_place=False):
     specs = specs or [VM] * len(operands)
     held = [a for a, s in zip(operands, specs) if s is VM and size_of(a) < 1 << 20]
     limit = room + size_of(*held, *jax.tree.leaves(out_shape))
@@ -53,6 +53,7 @@
         in_specs=specs,
         out_specs=jax.tree.map(lambda _: VM, out_shape),
         scratch_shapes=scratch,
+        input_output_aliases={0: 0} if in_place else {},
         cost_estimate=pl.CostEstimate(flops=0, bytes_accessed=0, transcendentals=0),
         compiler_params=pltpu.CompilerParams(vmem_limit_bytes=limit),
     )(*operands)
@@ -99,7 +100,7 @@
 
 
 def relay(x, *refs):
-    refs[-1][...] = x[...]
+    pass
 
 
 def column(meta, lane, wanted):
@@ -164,7 +165,8 @@
 
 
 def down_kernel(each, n, flips, terms, opens, cut, *refs):
-    pairs, refs = refs[: 2 * len(terms)], refs[2 * len(terms) :]
+    count = sum(len(arrays) for _, _, arrays in terms)
+    pairs, refs = refs[:count], refs[count:]
     (info, down, shrink), refs = refs[:3], refs[3:]
     base = small = spreads = here_ref = None
     if not opens:
@@ -208,16 +210,19 @@
         one_hot = spreads[flips.index(m) * experts + e] if known else spread(e, m)
         return jnp.dot(one_hot, ref[i], preferred_element_type=F32).astype(BF)
 
-    for t, (m, picked) in enumerate(terms):
-        pair = (me ^ m) // 2
+    for m, picked, arrays in terms:
+        got, pairs = pairs[: len(arrays)], pairs[len(arrays) :]
         for i, e in enumerate(picked):
-            mine = ordered(pairs[2 * t], i, e, m)
-            other = ordered(pairs[2 * t + 1], i, e, m ^ 1)
-            x = [jnp.where(odd, other, mine), jnp.where(odd, mine, other)]
-            if part % LANES == 0:
-                x = [jnp.concatenate(x, axis=1)]
-            for j, piece in enumerate(x):
-                spot, size = pair * len(x) + j, piece.shape[1]
+            x = [ordered(r, i, e, m ^ o) for r, o in zip(got, arrays)]
+            spots = [me ^ m ^ o for o in arrays]
+            if len(x) == 2:
+                x = [jnp.where(odd, x[1], x[0]), jnp.where(odd, x[0], x[1])]
+                low = (me ^ m) // 2 * 2
+                spots = [low, low + 1]
+                if part % LANES == 0:
+                    x, spots = [jnp.concatenate(x, axis=1)], [low // 2]
+            for piece, spot in zip(x, spots):
+                size = piece.shape[1]
                 at = pl.ds(pl.multiple_of(spot * size, size), size)
                 term = jnp.dot(piece, down[e, at, across], preferred_element_type=F32)
                 base = term if base is None else base + term
@@ -372,7 +377,7 @@
         for m in pairs:
             x = got[m] if m else got["sent"]
             if behind:
-                x = call(relay, shape(x.shape), (x, *behind))
+                x = got[m] = call(relay, shape(x.shape), (x, *behind), in_place=True)
             got[m ^ 1] = over(x, "dp", 1)
 
     others = list(range(2, n_dp, 2))
@@ -386,13 +391,16 @@
     sums = [shape((all_rows, cols), F32), shape((all_rows, ranks), F32)]
     spreads = shape(((n_dp - 2) * experts, all_rows, packed_rows))
     flips = list(range(2, n_dp)) if size_of(spreads) < 1 << 20 else []
-    steps = [[(0, i) for i in range(len(lists))]]
-    steps += [[(m, i) for m in others] for i in range(len(lists))]
+    both, last = (0, 1), len(lists) - 1
+    steps = [[(0, i, both) for i in range(len(lists))]]
+    steps[0] += [(m, i, (0,)) for i in range(last) for m in others]
+    steps += [[(m, i, (int(i < last),)) for i in range(len(lists)) for m in others]]
+    steps += [[(m, last, (1,)) for m in others]]
     carried, routing = [], []
 
     def add_terms(step, opens, cut, outs, after):
-        arrays = [a for m, i in step for a in (hidden[i][m], hidden[i][m ^ 1])]
-        terms = [(m, lists[i]) for m, i in step]
+        arrays = [hidden[i][m ^ o] for m, i, cores in step for o in cores]
+        terms = [(m, lists[i], cores) for m, i, cores in step]
         with jax.named_scope("down"):
             return call(
                 functools.partial(down_kernel, rows, n_dp, flips, terms, opens, cut),
@@ -410,8 +418,6 @@
         carried = add_terms(step, s == 0, None, outs, [])
         if s == 0:
             carried, routing = carried[:2], carried[2:]
-    if len(steps) == 2:
-        between_cores(hidden[-1], others, carried)
 
     some = width // PARTS
     arrived, after = [], [expand2]

time: 45.4 us -> 45.3 us (level)
  transfers between devices with their start and end apart: 21 -> 21, of which waited for: 15 -> 14; matrix products, arithmetic and copies ran while one was open for 0% -> 0% of each run, Pallas kernels for 13% -> 14%
where the time goes in v6:
time: 45.3 us; the launch traced here: 45.2 us
  starting transfers between devices  18 us (40%)
  waiting for transfers between devices  16.1 us (36%)
  Pallas kernels  10.8 us (24%)
    ppermute x21, starting transfers between devices, over(): lax.ppermute(x, axis, [(i, i ^ m) for i in range(lax.axis_size(axis))])  18 us
    ppermute x21, waiting for transfers between devices, over(): lax.ppermute(x, axis, [(i, i ^ m) for i in range(lax.axis_size(axis))])  16.1 us
    pallas_call x14, Pallas kernels, call(): pl.pallas_call(body, out_shape=out_shape, in_specs=specs, out_specs=jax.t...  10.8 us
  transfers between devices with their start and end apart: 21, of which 14 were waited for; matrix products, arithmetic and copies ran while one was open for 0% of the time, Pallas kernels for 14%

profile of v6, /device:TPU:0, one launch (start us, length us, event | category | flops | bytes accessed | tf_op | source)
XLA Modules:
  0.0 45.2 jit_solution(5240692190275824224)
XLA Ops:
  0.0 1.1 %prepare.1.refs_0_ = bf16[4,4224]{1,0:T(4,128)(2,1)S(1)} custom-call(s32[4]{0:T(128)} %refs_0_.1, bf16[4,4096]{1,0:T(4,128)(2,1)} %refs_1_.1, s32[4,8]{1,0:T(4,128)} %refs_2_.6, f32[4,8]{1,0:T(4,128)} %refs_3_.5, s32[8,16]{1,0:T(8,128)} %refs_4_.2, s32[8,16]{1,0:T(8,128)} %refs_5_.1, bf16[4,4096,384]{2,1,0:T(8,128)(2,1)} %refs_2_.9, ...), custom_call_target="tpu_custom_call" | custom-call | tf_op jit(solution)/shard_map/prepare/pallas_call | solution.py:50
  1.1 3.0 %collective-permute-start = (bf16[4,4224]{1,0:T(4,128)(2,1)S(1)}, bf16[4,4224]{1,0:T(4,128)(2,1)S(1)}, u32[]{:S(2)}, u32[]{:S(2)}) collective-permute-start(bf16[4,4224]{1,0:T(4,128)(2,1)S(1)} %prepare.1.refs_0_), channel_id=1, source_target_pairs={{0,2},{1,3},{2,0},{3,1},{4,6},{5,7},{6,4},{7,5},{8,10},{9,11},{10,... | collective-permute-start | bytes 101384 | tf_op jit(solution)/shard_map/ppermute | solution.py:314
  4.1 1.9 %collective-permute-done.refs_1_ = bf16[4,4224]{1,0:T(4,128)(2,1)S(1)} collective-permute-done((bf16[4,4224]{1,0:T(4,128)(2,1)S(1)}, bf16[4,4224]{1,0:T(4,128)(2,1)S(1)}, u32[]{:S(2)}, u32[]{:S(2)}) %collective-permute-start) | collective-permute-done | bytes 33824 | tf_op jit(solution)/shard_map/ppermute | solution.py:314
  6.1 4.2 %collective-permute-start.1 = (bf16[8,4224]{1,0:T(8,128)(2,1)S(1)}, bf16[8,4224]{1,0:T(8,128)(2,1)S(1)}, u32[]{:S(2)}, u32[]{:S(2)}) collective-permute-start(bf16[8,4224]{1,0:T(8,128)(2,1)S(1)} %join.1.refs_0_), channel_id=1, source_target_pairs={{0,12},{4,8},{8,4},{12,0},{1,13},{5,9},{9,5},{13,1},{2,14},{6,10},... | collective-permute-start | bytes 202760 | tf_op jit(solution)/shard_map/ppermute | solution.py:314
  10.3 0.6 %collective-permute-start.3 = (bf16[8,4224]{1,0:T(8,128)(2,1)S(1)}, bf16[8,4224]{1,0:T(8,128)(2,1)S(1)}, u32[]{:S(2)}, u32[]{:S(2)}) collective-permute-start(bf16[8,4224]{1,0:T(8,128)(2,1)S(1)} %join.1.refs_0_), channel_id=1, source_target_pairs={{0,4},{4,0},{8,12},{12,8},{1,5},{5,1},{9,13},{13,9},{2,6},{6,2},{1... | collective-permute-start | bytes 202760 | tf_op jit(solution)/shard_map/ppermute | solution.py:314
  10.9 1.8 %collective-permute-done.1.refs_1_ = bf16[8,4224]{1,0:T(8,128)(2,1)S(1)} collective-permute-done((bf16[8,4224]{1,0:T(8,128)(2,1)S(1)}, bf16[8,4224]{1,0:T(8,128)(2,1)S(1)}, u32[]{:S(2)}, u32[]{:S(2)}) %collective-permute-start.1) | collective-permute-done | bytes 67616 | tf_op jit(solution)/shard_map/ppermute | solution.py:314
  12.7 2.8 %collective-permute-done.2.refs_2_ = bf16[8,4224]{1,0:T(8,128)(2,1)S(1)} collective-permute-done((bf16[8,4224]{1,0:T(8,128)(2,1)S(1)}, bf16[8,4224]{1,0:T(8,128)(2,1)S(1)}, u32[]{:S(2)}, u32[]{:S(2)}) %collective-permute-start.2) | collective-permute-done | bytes 67616 | tf_op jit(solution)/shard_map/ppermute | solution.py:314
  16.0 0.7 %collective-permute-done.6.refs_6_ = bf16[8,4224]{1,0:T(8,128)(2,1)S(1)} collective-permute-done((bf16[8,4224]{1,0:T(8,128)(2,1)S(1)}, bf16[8,4224]{1,0:T(8,128)(2,1)S(1)}, u32[]{:S(2)}, u32[]{:S(2)}) %collective-permute-start.6) | collective-permute-done | bytes 67616 | tf_op jit(solution)/shard_map/ppermute | solution.py:314
  17.1 2.0 %up.3.refs_0_ = bf16[2,64,384]{2,1,0:T(8,128)(2,1)S(1)} custom-call(bf16[64,4096]{1,0:T(8,128)(2,1)S(1)} %get-tuple-element.28.refs_0_, bf16[64,128]{1,0:T(8,128)(2,1)S(1)} %get-tuple-element.29.refs_1_.refs_5_.refs_2_, bf16[4,4096,384]{2,1,0:T(8,128)(2,1)S(1)} %bitcast.5, bf16[4,4096,384]{2,1,0:T(8,128)(2,1)S(1)} %bitcast.7), custom_call_target="tpu_custom_call" | custom-call | tf_op jit(solution)/shard_map/up/pallas_call | solution.py:50
  19.1 1.6 %collective-permute-start.11 = (bf16[2,64,384]{2,1,0:T(8,128)(2,1)S(1)}, bf16[2,64,384]{2,1,0:T(8,128)(2,1)S(1)}, u32[]{:S(2)}, u32[]{:S(2)}) collective-permute-start(bf16[2,64,384]{2,1,0:T(8,128)(2,1)S(1)} %up.3.refs_0_), channel_id=1, source_target_pairs={{0,2},{1,3},{2,0},{3,1},{4,6},{5,7},{6,4},{7,5},{8,10},{9,11},{10,... | collective-permute-start | bytes 294920 | tf_op jit(solution)/shard_map/ppermute | solution.py:314
  20.7 2.2 %up.2 = (bf16[2,64,384]{2,1,0:T(8,128)(2,1)S(1)}, bf16[2,48,384]{2,1,0:T(8,128)(2,1)S(1)}) custom-call(bf16[64,4096]{1,0:T(8,128)(2,1)S(1)} %get-tuple-element.28.refs_0_, bf16[64,128]{1,0:T(8,128)(2,1)S(1)} %get-tuple-element.29.refs_1_.refs_5_.refs_2_, bf16[4,4096,384]{2,1,0:T(8,128)(2,1)S(1)} %bitcast.5, bf16[4,4096,384]{2,1,0:T(8,128)(2,1)S(1)} %bitcast.7), custom_call_target="tpu_custom_call" | custom-call | tf_op jit(solution)/shard_map/up/pallas_call | solution.py:50
  24.4 2.2 %down.4 = (f32[64,1024]{1,0:T(8,128)S(1)}, f32[64,128]{1,0:T(8,128)S(1)}, f32[64,128]{1,0:T(8,128)S(1)}, bf16[8,64,48]{2,1,0:T(8,128)(2,1)S(1)}) custom-call(bf16[2,64,384]{2,1,0:T(8,128)(2,1)S(1)} %up.3.refs_0_, bf16[2,64,384]{2,1,0:T(8,128)(2,1)S(1)} %collective-permute-done.9.refs_1_, bf16[2,64,384]{2,1,0:T(8,128)(2,1)S(1)} %get-tuple-element.31.refs_2_, ...), custom_call_target="tpu_custom_call" | custom-call | tf_op jit(solution)/shard_map/down/pallas_call | solution.py:50
  26.6 1.2 %collective-permute-done.8.x = bf16[2,48,384]{2,1,0:T(8,128)(2,1)S(1)} collective-permute-done((bf16[2,48,384]{2,1,0:T(8,128)(2,1)S(1)}, bf16[2,48,384]{2,1,0:T(8,128)(2,1)S(1)}, u32[]{:S(2)}, u32[]{:S(2)}) %collective-permute-start.8) | collective-permute-done | bytes 73760 | tf_op jit(solution)/shard_map/ppermute | solution.py:314
  27.9 1.2 %down.5 = (f32[64,1024]{1,0:T(8,128)S(1)}, f32[64,128]{1,0:T(8,128)S(1)}) custom-call(bf16[2,64,384]{2,1,0:T(8,128)(2,1)S(1)} %collective-permute-done.13.refs_0_, bf16[2,48,384]{2,1,0:T(8,128)(2,1)S(1)} %shard_map.109.refs_1_, bf16[64,128]{1,0:T(8,128)(2,1)S(1)} %get-tuple-element.29.refs_1_.refs_5_.refs_2_, bf16[4,1536,1024]{2,1,0:T(8,128)(2,1)S(1)} %bitcast.3, ...), custom_call_target="tpu_custom_call" | custom-call | tf_op jit(solution)/shard_map/down/pallas_call | solution.py:50
  29.1 0.7 %down.6 = (f32[32,2048]{1,0:T(8,128)S(1)}, bf16[32,2048]{1,0:T(8,128)(2,1)S(1)}, bf16[64,128]{1,0:T(8,128)(2,1)S(1)}) custom-call(bf16[2,48,384]{2,1,0:T(8,128)(2,1)S(1)} %collective-permute-done.12.refs_0_, bf16[64,128]{1,0:T(8,128)(2,1)S(1)} %get-tuple-element.29.refs_1_.refs_5_.refs_2_, bf16[4,1536,1024]{2,1,0:T(8,128)(2,1)S(1)} %bitcast.3, ...), custom_call_target="tpu_custom_call" | custom-call | tf_op jit(solution)/shard_map/down/pallas_call | solution.py:50
  31.4 0.6 %collective-permute-start.15 = (bf16[16,2048]{1,0:T(8,128)(2,1)S(1)}, bf16[16,2048]{1,0:T(8,128)(2,1)S(1)}, u32[]{:S(2)}, u32[]{:S(2)}) collective-permute-start(bf16[16,2048]{1,0:T(8,128)(2,1)S(1)} %get-tuple-element.41), channel_id=1, source_target_pairs={{0,2},{1,3},{2,0},{3,1},{4,6},{5,7},{6,4},{7,5},{8,10},{9,11},{10,... | collective-permute-start | bytes 196616 | tf_op jit(solution)/shard_map/ppermute | solution.py:314
  32.4 1.2 %collective-permute-start.17 = (bf16[16,2048]{1,0:T(8,128)(2,1)S(1)}, bf16[16,2048]{1,0:T(8,128)(2,1)S(1)}, u32[]{:S(2)}, u32[]{:S(2)}) collective-permute-start(bf16[16,2048]{1,0:T(8,128)(2,1)S(1)} %get-tuple-element.46), channel_id=1, source_target_pairs={{0,2},{1,3},{2,0},{3,1},{4,6},{5,7},{6,4},{7,5},{8,10},{9,11},{10,... | collective-permute-start | bytes 196616 | tf_op jit(solution)/shard_map/ppermute | solution.py:314
  33.7 2.8 %collective-permute-done.15.refs_1_ = bf16[16,2048]{1,0:T(8,128)(2,1)S(1)} collective-permute-done((bf16[16,2048]{1,0:T(8,128)(2,1)S(1)}, bf16[16,2048]{1,0:T(8,128)(2,1)S(1)}, u32[]{:S(2)}, u32[]{:S(2)}) %collective-permute-start.15) | collective-permute-done | bytes 65568 | tf_op jit(solution)/shard_map/ppermute | solution.py:314
  36.4 0.8 %collective-permute-done.17.refs_3_ = bf16[16,2048]{1,0:T(8,128)(2,1)S(1)} collective-permute-done((bf16[16,2048]{1,0:T(8,128)(2,1)S(1)}, bf16[16,2048]{1,0:T(8,128)(2,1)S(1)}, u32[]{:S(2)}, u32[]{:S(2)}) %collective-permute-start.17) | collective-permute-done | bytes 65568 | tf_op jit(solution)/shard_map/ppermute | solution.py:314
  37.3 2.2 %collective-permute-start.18 = (bf16[4,4096]{1,0:T(4,128)(2,1)S(1)}, bf16[4,4096]{1,0:T(4,128)(2,1)S(1)}, u32[]{:S(2)}, u32[]{:S(2)}) collective-permute-start(bf16[4,4096]{1,0:T(4,128)(2,1)S(1)} %get-tuple-element.48), channel_id=1, source_target_pairs={{0,12},{4,8},{8,4},{12,0},{1,13},{5,9},{9,5},{13,1},{2,14},{6,10},... | collective-permute-start | bytes 98312 | tf_op jit(solution)/shard_map/ppermute | solution.py:314
  39.5 2.2 %collective-permute-start.20 = (bf16[4,4096]{1,0:T(4,128)(2,1)S(1)}, bf16[4,4096]{1,0:T(4,128)(2,1)S(1)}, u32[]{:S(2)}, u32[]{:S(2)}) collective-permute-start(bf16[4,4096]{1,0:T(4,128)(2,1)S(1)} %get-tuple-element.50), channel_id=1, source_target_pairs={{0,4},{4,0},{8,12},{12,8},{1,5},{5,1},{9,13},{13,9},{2,6},{6,2},{1... | collective-permute-start | bytes 98312 | tf_op jit(solution)/shard_map/ppermute | solution.py:314
  41.8 1.3 %collective-permute-done.18.refs_1_ = bf16[4,4096]{1,0:T(4,128)(2,1)S(1)} collective-permute-done((bf16[4,4096]{1,0:T(4,128)(2,1)S(1)}, bf16[4,4096]{1,0:T(4,128)(2,1)S(1)}, u32[]{:S(2)}, u32[]{:S(2)}) %collective-permute-start.18) | collective-permute-done | bytes 32800 | tf_op jit(solution)/shard_map/ppermute | solution.py:314
  43.1 1.4 %collective-permute-done.19.refs_2_ = bf16[4,4096]{1,0:T(4,128)(2,1)S(1)} collective-permute-done((bf16[4,4096]{1,0:T(4,128)(2,1)S(1)}, bf16[4,4096]{1,0:T(4,128)(2,1)S(1)}, u32[]{:S(2)}, u32[]{:S(2)}) %collective-permute-start.19) | collective-permute-done | bytes 32800 | tf_op jit(solution)/shard_map/ppermute | solution.py:314
  44.5 0.6 %finish.1 = bf16[4,4096]{1,0:T(4,128)(2,1)} custom-call(f32[4,4096]{1,0:T(4,128)S(1)} %get-tuple-element.47.refs_0_, bf16[4,4096]{1,0:T(4,128)(2,1)S(1)} %collective-permute-done.18.refs_1_, bf16[4,4096]{1,0:T(4,128)(2,1)S(1)} %collective-permute-done.19.refs_2_, bf16[4,4096]{1,0:T(4,128)(2,1)S(1)} %collective-permute-done.20.refs_3_), custom_call_target="tpu_custom_call" | custom-call | tf_op jit(solution)/shard_map/finish/pallas_call | solution.py:50
  (57 shorter events, 4.3 us)
Async XLA Ops:
  0.0 17.0 %slice-start.4 = ((s8[12582912]{0:T(1024)(128)(4,1)}), s8[4194304]{0:T(1024)(128)(4,1)S(1)}, s32[]{:S(2)}) async-start(s8[12582912]{0:T(1024)(128)(4,1)} %bitcast.4), calls=%async_computation.4 | async-start | bytes 8388608
  0.0 17.0 %slice-start.6 = ((s8[12582912]{0:T(1024)(128)(4,1)}), s8[4194304]{0:T(1024)(128)(4,1)S(1)}, s32[]{:S(2)}) async-start(s8[12582912]{0:T(1024)(128)(4,1)} %bitcast.6), calls=%async_computation.6 | async-start | bytes 8388608
  0.0 17.0 %slice-start.7 = ((s8[12582912]{0:T(1024)(128)(4,1)}), s8[4194304]{0:T(1024)(128)(4,1)S(1)}, s32[]{:S(2)}) async-start(s8[12582912]{0:T(1024)(128)(4,1)} %bitcast.6), calls=%async_computation.7 | async-start | bytes 8388608
  1.1 4.9 %collective-permute-start = (bf16[4,4224]{1,0:T(4,128)(2,1)S(1)}, bf16[4,4224]{1,0:T(4,128)(2,1)S(1)}, u32[]{:S(2)}, u32[]{:S(2)}) collective-permute-start(bf16[4,4224]{1,0:T(4,128)(2,1)S(1)} %prepare.1.refs_0_), channel_id=1, source_target_pairs={{0,2},{1,3},{2,0},{3,1},{4,6},{5,7},{6,4},{7,5},{8,10},{9,11},{10,... | collective-permute-start | bytes 101384 | tf_op jit(solution)/shard_map/ppermute | solution.py:314
  6.1 6.7 %collective-permute-start.1 = (bf16[8,4224]{1,0:T(8,128)(2,1)S(1)}, bf16[8,4224]{1,0:T(8,128)(2,1)S(1)}, u32[]{:S(2)}, u32[]{:S(2)}) collective-permute-start(bf16[8,4224]{1,0:T(8,128)(2,1)S(1)} %join.1.refs_0_), channel_id=1, source_target_pairs={{0,12},{4,8},{8,4},{12,0},{1,13},{5,9},{9,5},{13,1},{2,14},{6,10},... | collective-permute-start | bytes 202760 | tf_op jit(solution)/shard_map/ppermute | solution.py:314
  10.3 5.3 %collective-permute-start.2 = (bf16[8,4224]{1,0:T(8,128)(2,1)S(1)}, bf16[8,4224]{1,0:T(8,128)(2,1)S(1)}, u32[]{:S(2)}, u32[]{:S(2)}) collective-permute-start(bf16[8,4224]{1,0:T(8,128)(2,1)S(1)} %join.1.refs_0_), channel_id=1, source_target_pairs={{0,8},{4,12},{8,0},{12,4},{1,9},{5,13},{9,1},{13,5},{2,10},{6,14},... | collective-permute-start | bytes 202760 | tf_op jit(solution)/shard_map/ppermute | solution.py:314
  10.3 5.3 %collective-permute-start.3 = (bf16[8,4224]{1,0:T(8,128)(2,1)S(1)}, bf16[8,4224]{1,0:T(8,128)(2,1)S(1)}, u32[]{:S(2)}, u32[]{:S(2)}) collective-permute-start(bf16[8,4224]{1,0:T(8,128)(2,1)S(1)} %join.1.refs_0_), channel_id=1, source_target_pairs={{0,4},{4,0},{8,12},{12,8},{1,5},{5,1},{9,13},{13,9},{2,6},{6,2},{1... | collective-permute-start | bytes 202760 | tf_op jit(solution)/shard_map/ppermute | solution.py:314
  10.9 5.1 %collective-permute-start.4 = (bf16[8,4224]{1,0:T(8,128)(2,1)S(1)}, bf16[8,4224]{1,0:T(8,128)(2,1)S(1)}, u32[]{:S(2)}, u32[]{:S(2)}) collective-permute-start(bf16[8,4224]{1,0:T(8,128)(2,1)S(1)} %join.1.refs_0_), channel_id=1, source_target_pairs={{0,1},{1,0},{2,3},{3,2},{4,5},{5,4},{6,7},{7,6},{8,9},{9,8},{10,11... | collective-permute-start | bytes 202760 | tf_op jit(solution)/shard_map/ppermute | solution.py:314
  12.7 3.3 %collective-permute-start.5 = (bf16[8,4224]{1,0:T(8,128)(2,1)S(1)}, bf16[8,4224]{1,0:T(8,128)(2,1)S(1)}, u32[]{:S(2)}, u32[]{:S(2)}) collective-permute-start(bf16[8,4224]{1,0:T(8,128)(2,1)S(1)} %collective-permute-done.1.refs_1_), channel_id=1, source_target_pairs={{0,1},{1,0},{2,3},{3,2},{4,5},{5,4},{6,7},{7,6},{8,9},{9,8},{10,11... | collective-permute-start | bytes 202760 | tf_op jit(solution)/shard_map/ppermute | solution.py:314
  15.5 1.3 %collective-permute-start.6 = (bf16[8,4224]{1,0:T(8,128)(2,1)S(1)}, bf16[8,4224]{1,0:T(8,128)(2,1)S(1)}, u32[]{:S(2)}, u32[]{:S(2)}) collective-permute-start(bf16[8,4224]{1,0:T(8,128)(2,1)S(1)} %collective-permute-done.2.refs_2_), channel_id=1, source_target_pairs={{0,1},{1,0},{2,3},{3,2},{4,5},{5,4},{6,7},{7,6},{8,9},{9,8},{10,11... | collective-permute-start | bytes 202760 | tf_op jit(solution)/shard_map/ppermute | solution.py:314
  15.5 1.4 %collective-permute-start.7 = (bf16[8,4224]{1,0:T(8,128)(2,1)S(1)}, bf16[8,4224]{1,0:T(8,128)(2,1)S(1)}, u32[]{:S(2)}, u32[]{:S(2)}) collective-permute-start(bf16[8,4224]{1,0:T(8,128)(2,1)S(1)} %collective-permute-done.3.refs_3_), channel_id=1, source_target_pairs={{0,1},{1,0},{2,3},{3,2},{4,5},{5,4},{6,7},{7,6},{8,9},{9,8},{10,11... | collective-permute-start | bytes 202760 | tf_op jit(solution)/shard_map/ppermute | solution.py:314
  19.1 5.1 %collective-permute-start.11 = (bf16[2,64,384]{2,1,0:T(8,128)(2,1)S(1)}, bf16[2,64,384]{2,1,0:T(8,128)(2,1)S(1)}, u32[]{:S(2)}, u32[]{:S(2)}) collective-permute-start(bf16[2,64,384]{2,1,0:T(8,128)(2,1)S(1)} %up.3.refs_0_), channel_id=1, source_target_pairs={{0,2},{1,3},{2,0},{3,1},{4,6},{5,7},{6,4},{7,5},{8,10},{9,11},{10,... | collective-permute-start | bytes 294920 | tf_op jit(solution)/shard_map/ppermute | solution.py:314
  20.7 3.7 %collective-permute-start.9 = (bf16[2,64,384]{2,1,0:T(8,128)(2,1)S(1)}, bf16[2,64,384]{2,1,0:T(8,128)(2,1)S(1)}, u32[]{:S(2)}, u32[]{:S(2)}) collective-permute-start(bf16[2,64,384]{2,1,0:T(8,128)(2,1)S(1)} %up.3.refs_0_), channel_id=1, source_target_pairs={{0,1},{1,0},{2,3},{3,2},{4,5},{5,4},{6,7},{7,6},{8,9},{9,8},{10,11... | collective-permute-start | bytes 294920 | tf_op jit(solution)/shard_map/ppermute | solution.py:314
  23.0 1.4 %collective-permute-start.10 = (bf16[2,48,384]{2,1,0:T(8,128)(2,1)S(1)}, bf16[2,48,384]{2,1,0:T(8,128)(2,1)S(1)}, u32[]{:S(2)}, u32[]{:S(2)}) collective-permute-start(bf16[2,48,384]{2,1,0:T(8,128)(2,1)S(1)} %get-tuple-element.30), channel_id=1, source_target_pairs={{0,1},{1,0},{2,3},{3,2},{4,5},{5,4},{6,7},{7,6},{8,9},{9,8},{10,11... | collective-permute-start | bytes 221192 | tf_op jit(solution)/shard_map/ppermute | solution.py:314
  23.5 4.4 %collective-permute-start.8 = (bf16[2,48,384]{2,1,0:T(8,128)(2,1)S(1)}, bf16[2,48,384]{2,1,0:T(8,128)(2,1)S(1)}, u32[]{:S(2)}, u32[]{:S(2)}) collective-permute-start(bf16[2,48,384]{2,1,0:T(8,128)(2,1)S(1)} %get-tuple-element.30), channel_id=1, source_target_pairs={{0,2},{1,3},{2,0},{3,1},{4,6},{5,7},{6,4},{7,5},{8,10},{9,11},{10,... | collective-permute-start | bytes 221192 | tf_op jit(solution)/shard_map/ppermute | solution.py:314
  24.2 3.6 %collective-permute-start.13 = (bf16[2,64,384]{2,1,0:T(8,128)(2,1)S(1)}, bf16[2,64,384]{2,1,0:T(8,128)(2,1)S(1)}, u32[]{:S(2)}, u32[]{:S(2)}) collective-permute-start(bf16[2,64,384]{2,1,0:T(8,128)(2,1)S(1)} %collective-permute-done.11.refs_4_), channel_id=1, source_target_pairs={{0,1},{1,0},{2,3},{3,2},{4,5},{5,4},{6,7},{7,6},{8,9},{9,8},{10,11... | collective-permute-start | bytes 294920 | tf_op jit(solution)/shard_map/ppermute | solution.py:314
  27.8 1.3 %collective-permute-start.12 = (bf16[2,48,384]{2,1,0:T(8,128)(2,1)S(1)}, bf16[2,48,384]{2,1,0:T(8,128)(2,1)S(1)}, u32[]{:S(2)}, u32[]{:S(2)}) collective-permute-start(bf16[2,48,384]{2,1,0:T(8,128)(2,1)S(1)} %shard_map.109.refs_1_), channel_id=1, source_target_pairs={{0,1},{1,0},{2,3},{3,2},{4,5},{5,4},{6,7},{7,6},{8,9},{9,8},{10,11... | collective-permute-start | bytes 221192 | tf_op jit(solution)/shard_map/ppermute | solution.py:314
  29.8 1.6 %collective-permute-start.14 = (bf16[32,2048]{1,0:T(8,128)(2,1)S(1)}, bf16[32,2048]{1,0:T(8,128)(2,1)S(1)}, u32[]{:S(2)}, u32[]{:S(2)}) collective-permute-start(bf16[32,2048]{1,0:T(8,128)(2,1)S(1)} %get-tuple-element.39), channel_id=1, source_target_pairs={{0,1},{1,0},{2,3},{3,2},{4,5},{5,4},{6,7},{7,6},{8,9},{9,8},{10,11... | collective-permute-start | bytes 393224 | tf_op jit(solution)/shard_map/ppermute | solution.py:314
  30.9 1.4 %collective-permute-start.16 = (bf16[32,2048]{1,0:T(8,128)(2,1)S(1)}, bf16[32,2048]{1,0:T(8,128)(2,1)S(1)}, u32[]{:S(2)}, u32[]{:S(2)}) collective-permute-start(bf16[32,2048]{1,0:T(8,128)(2,1)S(1)} %get-tuple-element.44), channel_id=1, source_target_pairs={{0,1},{1,0},{2,3},{3,2},{4,5},{5,4},{6,7},{7,6},{8,9},{9,8},{10,11... | collective-permute-start | bytes 393224 | tf_op jit(solution)/shard_map/ppermute | solution.py:314
  31.4 5.0 %collective-permute-start.15 = (bf16[16,2048]{1,0:T(8,128)(2,1)S(1)}, bf16[16,2048]{1,0:T(8,128)(2,1)S(1)}, u32[]{:S(2)}, u32[]{:S(2)}) collective-permute-start(bf16[16,2048]{1,0:T(8,128)(2,1)S(1)} %get-tuple-element.41), channel_id=1, source_target_pairs={{0,2},{1,3},{2,0},{3,1},{4,6},{5,7},{6,4},{7,5},{8,10},{9,11},{10,... | collective-permute-start | bytes 196616 | tf_op jit(solution)/shard_map/ppermute | solution.py:314
  32.4 4.9 %collective-permute-start.17 = (bf16[16,2048]{1,0:T(8,128)(2,1)S(1)}, bf16[16,2048]{1,0:T(8,128)(2,1)S(1)}, u32[]{:S(2)}, u32[]{:S(2)}) collective-permute-start(bf16[16,2048]{1,0:T(8,128)(2,1)S(1)} %get-tuple-element.46), channel_id=1, source_target_pairs={{0,2},{1,3},{2,0},{3,1},{4,6},{5,7},{6,4},{7,5},{8,10},{9,11},{10,... | collective-permute-start | bytes 196616 | tf_op jit(solution)/shard_map/ppermute | solution.py:314
  37.3 5.8 %collective-permute-start.18 = (bf16[4,4096]{1,0:T(4,128)(2,1)S(1)}, bf16[4,4096]{1,0:T(4,128)(2,1)S(1)}, u32[]{:S(2)}, u32[]{:S(2)}) collective-permute-start(bf16[4,4096]{1,0:T(4,128)(2,1)S(1)} %get-tuple-element.48), channel_id=1, source_target_pairs={{0,12},{4,8},{8,4},{12,0},{1,13},{5,9},{9,5},{13,1},{2,14},{6,10},... | collective-permute-start | bytes 98312 | tf_op jit(solution)/shard_map/ppermute | solution.py:314
  39.5 5.0 %collective-permute-start.19 = (bf16[4,4096]{1,0:T(4,128)(2,1)S(1)}, bf16[4,4096]{1,0:T(4,128)(2,1)S(1)}, u32[]{:S(2)}, u32[]{:S(2)}) collective-permute-start(bf16[4,4096]{1,0:T(4,128)(2,1)S(1)} %get-tuple-element.49), channel_id=1, source_target_pairs={{0,8},{4,12},{8,0},{12,4},{1,9},{5,13},{9,1},{13,5},{2,10},{6,14},... | collective-permute-start | bytes 98312 | tf_op jit(solution)/shard_map/ppermute | solution.py:314
  39.5 5.0 %collective-permute-start.20 = (bf16[4,4096]{1,0:T(4,128)(2,1)S(1)}, bf16[4,4096]{1,0:T(4,128)(2,1)S(1)}, u32[]{:S(2)}, u32[]{:S(2)}) collective-permute-start(bf16[4,4096]{1,0:T(4,128)(2,1)S(1)} %get-tuple-element.50), channel_id=1, source_target_pairs={{0,4},{4,0},{8,12},{12,8},{1,5},{5,1},{9,13},{13,9},{2,6},{6,2},{1... | collective-permute-start | bytes 98312 | tf_op jit(solution)/shard_map/ppermute | solution.py:314
  (8 other events, 78.9 us)

commit v7 on v6

--- a/solution.py
+++ b/solution.py
@@ -100,7 +100,7 @@
 
 
 def relay(x, *refs):
-    pass
+    refs[-1][...] = x[...]
 
 
 def column(meta, lane, wanted):

time: 45.3 us -> 45.4 us (level)
  no operation moved by 1% of the time
where the time goes in v7:
time: 45.4 us; the launch traced here: 45.3 us
  starting transfers between devices  18.1 us (40%)
  waiting for transfers between devices  16.1 us (35%)
  Pallas kernels  10.8 us (24%)
    ppermute x21, starting transfers between devices, over(): lax.ppermute(x, axis, [(i, i ^ m) for i in range(lax.axis_size(axis))])  18.1 us
    ppermute x21, waiting for transfers between devices, over(): lax.ppermute(x, axis, [(i, i ^ m) for i in range(lax.axis_size(axis))])  16.1 us
    pallas_call x14, Pallas kernels, call(): pl.pallas_call(body, out_shape=out_shape, in_specs=specs, out_specs=jax.t...  10.8 us
  transfers between devices with their start and end apart: 21, of which 14 were waited for; matrix products, arithmetic and copies ran while one was open for 0% of the time, Pallas kernels for 14%

profile of v7, /device:TPU:0, one launch (start us, length us, event | category | flops | bytes accessed | tf_op | source)
XLA Modules:
  0.0 45.3 jit_solution(8271743336635364289)
XLA Ops:
  0.0 1.1 %prepare.1.refs_0_ = bf16[4,4224]{1,0:T(4,128)(2,1)S(1)} custom-call(s32[4]{0:T(128)} %refs_0_.1, bf16[4,4096]{1,0:T(4,128)(2,1)} %refs_1_.1, s32[4,8]{1,0:T(4,128)} %refs_2_.6, f32[4,8]{1,0:T(4,128)} %refs_3_.5, s32[8,16]{1,0:T(8,128)} %refs_4_.2, s32[8,16]{1,0:T(8,128)} %refs_5_.1, bf16[4,4096,384]{2,1,0:T(8,128)(2,1)} %refs_2_.9, ...), custom_call_target="tpu_custom_call" | custom-call | tf_op jit(solution)/shard_map/prepare/pallas_call | solution.py:50
  1.1 3.0 %collective-permute-start = (bf16[4,4224]{1,0:T(4,128)(2,1)S(1)}, bf16[4,4224]{1,0:T(4,128)(2,1)S(1)}, u32[]{:S(2)}, u32[]{:S(2)}) collective-permute-start(bf16[4,4224]{1,0:T(4,128)(2,1)S(1)} %prepare.1.refs_0_), channel_id=1, source_target_pairs={{0,2},{1,3},{2,0},{3,1},{4,6},{5,7},{6,4},{7,5},{8,10},{9,11},{10,... | collective-permute-start | bytes 101384 | tf_op jit(solution)/shard_map/ppermute | solution.py:314
  4.1 1.9 %collective-permute-done.refs_1_ = bf16[4,4224]{1,0:T(4,128)(2,1)S(1)} collective-permute-done((bf16[4,4224]{1,0:T(4,128)(2,1)S(1)}, bf16[4,4224]{1,0:T(4,128)(2,1)S(1)}, u32[]{:S(2)}, u32[]{:S(2)}) %collective-permute-start) | collective-permute-done | bytes 33824 | tf_op jit(solution)/shard_map/ppermute | solution.py:314
  6.1 4.2 %collective-permute-start.1 = (bf16[8,4224]{1,0:T(8,128)(2,1)S(1)}, bf16[8,4224]{1,0:T(8,128)(2,1)S(1)}, u32[]{:S(2)}, u32[]{:S(2)}) collective-permute-start(bf16[8,4224]{1,0:T(8,128)(2,1)S(1)} %join.1.refs_0_), channel_id=1, source_target_pairs={{0,12},{4,8},{8,4},{12,0},{1,13},{5,9},{9,5},{13,1},{2,14},{6,10},... | collective-permute-start | bytes 202760 | tf_op jit(solution)/shard_map/ppermute | solution.py:314
  10.3 0.6 %collective-permute-start.3 = (bf16[8,4224]{1,0:T(8,128)(2,1)S(1)}, bf16[8,4224]{1,0:T(8,128)(2,1)S(1)}, u32[]{:S(2)}, u32[]{:S(2)}) collective-permute-start(bf16[8,4224]{1,0:T(8,128)(2,1)S(1)} %join.1.refs_0_), channel_id=1, source_target_pairs={{0,4},{4,0},{8,12},{12,8},{1,5},{5,1},{9,13},{13,9},{2,6},{6,2},{1... | collective-permute-start | bytes 202760 | tf_op jit(solution)/shard_map/ppermute | solution.py:314
  10.9 1.8 %collective-permute-done.1.refs_1_ = bf16[8,4224]{1,0:T(8,128)(2,1)S(1)} collective-permute-done((bf16[8,4224]{1,0:T(8,128)(2,1)S(1)}, bf16[8,4224]{1,0:T(8,128)(2,1)S(1)}, u32[]{:S(2)}, u32[]{:S(2)}) %collective-permute-start.1) | collective-permute-done | bytes 67616 | tf_op jit(solution)/shard_map/ppermute | solution.py:314
  12.7 2.8 %collective-permute-done.2.refs_2_ = bf16[8,4224]{1,0:T(8,128)(2,1)S(1)} collective-permute-done((bf16[8,4224]{1,0:T(8,128)(2,1)S(1)}, bf16[8,4224]{1,0:T(8,128)(2,1)S(1)}, u32[]{:S(2)}, u32[]{:S(2)}) %collective-permute-start.2) | collective-permute-done | bytes 67616 | tf_op jit(solution)/shard_map/ppermute | solution.py:314
  16.0 0.7 %collective-permute-done.6.refs_6_ = bf16[8,4224]{1,0:T(8,128)(2,1)S(1)} collective-permute-done((bf16[8,4224]{1,0:T(8,128)(2,1)S(1)}, bf16[8,4224]{1,0:T(8,128)(2,1)S(1)}, u32[]{:S(2)}, u32[]{:S(2)}) %collective-permute-start.6) | collective-permute-done | bytes 67616 | tf_op jit(solution)/shard_map/ppermute | solution.py:314
  17.1 2.0 %up.3.refs_0_ = bf16[2,64,384]{2,1,0:T(8,128)(2,1)S(1)} custom-call(bf16[64,4096]{1,0:T(8,128)(2,1)S(1)} %get-tuple-element.28.refs_0_, bf16[64,128]{1,0:T(8,128)(2,1)S(1)} %get-tuple-element.29.refs_1_.refs_5_.refs_2_, bf16[4,4096,384]{2,1,0:T(8,128)(2,1)S(1)} %bitcast.5, bf16[4,4096,384]{2,1,0:T(8,128)(2,1)S(1)} %bitcast.7), custom_call_target="tpu_custom_call" | custom-call | tf_op jit(solution)/shard_map/up/pallas_call | solution.py:50
  19.1 1.6 %collective-permute-start.11 = (bf16[2,64,384]{2,1,0:T(8,128)(2,1)S(1)}, bf16[2,64,384]{2,1,0:T(8,128)(2,1)S(1)}, u32[]{:S(2)}, u32[]{:S(2)}) collective-permute-start(bf16[2,64,384]{2,1,0:T(8,128)(2,1)S(1)} %up.3.refs_0_), channel_id=1, source_target_pairs={{0,2},{1,3},{2,0},{3,1},{4,6},{5,7},{6,4},{7,5},{8,10},{9,11},{10,... | collective-permute-start | bytes 294920 | tf_op jit(solution)/shard_map/ppermute | solution.py:314
  20.7 2.2 %up.2 = (bf16[2,64,384]{2,1,0:T(8,128)(2,1)S(1)}, bf16[2,48,384]{2,1,0:T(8,128)(2,1)S(1)}) custom-call(bf16[64,4096]{1,0:T(8,128)(2,1)S(1)} %get-tuple-element.28.refs_0_, bf16[64,128]{1,0:T(8,128)(2,1)S(1)} %get-tuple-element.29.refs_1_.refs_5_.refs_2_, bf16[4,4096,384]{2,1,0:T(8,128)(2,1)S(1)} %bitcast.5, bf16[4,4096,384]{2,1,0:T(8,128)(2,1)S(1)} %bitcast.7), custom_call_target="tpu_custom_call" | custom-call | tf_op jit(solution)/shard_map/up/pallas_call | solution.py:50
  24.4 2.2 %down.4 = (f32[64,1024]{1,0:T(8,128)S(1)}, f32[64,128]{1,0:T(8,128)S(1)}, f32[64,128]{1,0:T(8,128)S(1)}, bf16[8,64,48]{2,1,0:T(8,128)(2,1)S(1)}) custom-call(bf16[2,64,384]{2,1,0:T(8,128)(2,1)S(1)} %up.3.refs_0_, bf16[2,64,384]{2,1,0:T(8,128)(2,1)S(1)} %collective-permute-done.9.refs_1_, bf16[2,64,384]{2,1,0:T(8,128)(2,1)S(1)} %get-tuple-element.31.refs_2_, ...), custom_call_target="tpu_custom_call" | custom-call | tf_op jit(solution)/shard_map/down/pallas_call | solution.py:50
  26.6 1.2 %collective-permute-done.8.x = bf16[2,48,384]{2,1,0:T(8,128)(2,1)S(1)} collective-permute-done((bf16[2,48,384]{2,1,0:T(8,128)(2,1)S(1)}, bf16[2,48,384]{2,1,0:T(8,128)(2,1)S(1)}, u32[]{:S(2)}, u32[]{:S(2)}) %collective-permute-start.8) | collective-permute-done | bytes 73760 | tf_op jit(solution)/shard_map/ppermute | solution.py:314
  28.0 1.2 %down.5 = (f32[64,1024]{1,0:T(8,128)S(1)}, f32[64,128]{1,0:T(8,128)S(1)}) custom-call(bf16[2,64,384]{2,1,0:T(8,128)(2,1)S(1)} %collective-permute-done.13.refs_0_, bf16[2,48,384]{2,1,0:T(8,128)(2,1)S(1)} %shard_map.109.refs_1_, bf16[64,128]{1,0:T(8,128)(2,1)S(1)} %get-tuple-element.29.refs_1_.refs_5_.refs_2_, bf16[4,1536,1024]{2,1,0:T(8,128)(2,1)S(1)} %bitcast.3, ...), custom_call_target="tpu_custom_call" | custom-call | tf_op jit(solution)/shard_map/down/pallas_call | solution.py:50
  29.2 0.7 %down.6 = (f32[32,2048]{1,0:T(8,128)S(1)}, bf16[32,2048]{1,0:T(8,128)(2,1)S(1)}, bf16[64,128]{1,0:T(8,128)(2,1)S(1)}) custom-call(bf16[2,48,384]{2,1,0:T(8,128)(2,1)S(1)} %collective-permute-done.12.refs_0_, bf16[64,128]{1,0:T(8,128)(2,1)S(1)} %get-tuple-element.29.refs_1_.refs_5_.refs_2_, bf16[4,1536,1024]{2,1,0:T(8,128)(2,1)S(1)} %bitcast.3, ...), custom_call_target="tpu_custom_call" | custom-call | tf_op jit(solution)/shard_map/down/pallas_call | solution.py:50
  31.5 0.6 %collective-permute-start.15 = (bf16[16,2048]{1,0:T(8,128)(2,1)S(1)}, bf16[16,2048]{1,0:T(8,128)(2,1)S(1)}, u32[]{:S(2)}, u32[]{:S(2)}) collective-permute-start(bf16[16,2048]{1,0:T(8,128)(2,1)S(1)} %get-tuple-element.41), channel_id=1, source_target_pairs={{0,2},{1,3},{2,0},{3,1},{4,6},{5,7},{6,4},{7,5},{8,10},{9,11},{10,... | collective-permute-start | bytes 196616 | tf_op jit(solution)/shard_map/ppermute | solution.py:314
  32.5 1.3 %collective-permute-start.17 = (bf16[16,2048]{1,0:T(8,128)(2,1)S(1)}, bf16[16,2048]{1,0:T(8,128)(2,1)S(1)}, u32[]{:S(2)}, u32[]{:S(2)}) collective-permute-start(bf16[16,2048]{1,0:T(8,128)(2,1)S(1)} %get-tuple-element.46), channel_id=1, source_target_pairs={{0,2},{1,3},{2,0},{3,1},{4,6},{5,7},{6,4},{7,5},{8,10},{9,11},{10,... | collective-permute-start | bytes 196616 | tf_op jit(solution)/shard_map/ppermute | solution.py:314
  33.7 2.8 %collective-permute-done.15.refs_1_ = bf16[16,2048]{1,0:T(8,128)(2,1)S(1)} collective-permute-done((bf16[16,2048]{1,0:T(8,128)(2,1)S(1)}, bf16[16,2048]{1,0:T(8,128)(2,1)S(1)}, u32[]{:S(2)}, u32[]{:S(2)}) %collective-permute-start.15) | collective-permute-done | bytes 65568 | tf_op jit(solution)/shard_map/ppermute | solution.py:314
  36.5 0.8 %collective-permute-done.17.refs_3_ = bf16[16,2048]{1,0:T(8,128)(2,1)S(1)} collective-permute-done((bf16[16,2048]{1,0:T(8,128)(2,1)S(1)}, bf16[16,2048]{1,0:T(8,128)(2,1)S(1)}, u32[]{:S(2)}, u32[]{:S(2)}) %collective-permute-start.17) | collective-permute-done | bytes 65568 | tf_op jit(solution)/shard_map/ppermute | solution.py:314
  37.4 2.2 %collective-permute-start.18 = (bf16[4,4096]{1,0:T(4,128)(2,1)S(1)}, bf16[4,4096]{1,0:T(4,128)(2,1)S(1)}, u32[]{:S(2)}, u32[]{:S(2)}) collective-permute-start(bf16[4,4096]{1,0:T(4,128)(2,1)S(1)} %get-tuple-element.48), channel_id=1, source_target_pairs={{0,12},{4,8},{8,4},{12,0},{1,13},{5,9},{9,5},{13,1},{2,14},{6,10},... | collective-permute-start | bytes 98312 | tf_op jit(solution)/shard_map/ppermute | solution.py:314
  39.6 2.2 %collective-permute-start.20 = (bf16[4,4096]{1,0:T(4,128)(2,1)S(1)}, bf16[4,4096]{1,0:T(4,128)(2,1)S(1)}, u32[]{:S(2)}, u32[]{:S(2)}) collective-permute-start(bf16[4,4096]{1,0:T(4,128)(2,1)S(1)} %get-tuple-element.50), channel_id=1, source_target_pairs={{0,4},{4,0},{8,12},{12,8},{1,5},{5,1},{9,13},{13,9},{2,6},{6,2},{1... | collective-permute-start | bytes 98312 | tf_op jit(solution)/shard_map/ppermute | solution.py:314
  41.8 1.3 %collective-permute-done.18.refs_1_ = bf16[4,4096]{1,0:T(4,128)(2,1)S(1)} collective-permute-done((bf16[4,4096]{1,0:T(4,128)(2,1)S(1)}, bf16[4,4096]{1,0:T(4,128)(2,1)S(1)}, u32[]{:S(2)}, u32[]{:S(2)}) %collective-permute-start.18) | collective-permute-done | bytes 32800 | tf_op jit(solution)/shard_map/ppermute | solution.py:314
  43.2 1.4 %collective-permute-done.19.refs_2_ = bf16[4,4096]{1,0:T(4,128)(2,1)S(1)} collective-permute-done((bf16[4,4096]{1,0:T(4,128)(2,1)S(1)}, bf16[4,4096]{1,0:T(4,128)(2,1)S(1)}, u32[]{:S(2)}, u32[]{:S(2)}) %collective-permute-start.19) | collective-permute-done | bytes 32800 | tf_op jit(solution)/shard_map/ppermute | solution.py:314
  44.6 0.6 %finish.1 = bf16[4,4096]{1,0:T(4,128)(2,1)} custom-call(f32[4,4096]{1,0:T(4,128)S(1)} %get-tuple-element.47.refs_0_, bf16[4,4096]{1,0:T(4,128)(2,1)S(1)} %collective-permute-done.18.refs_1_, bf16[4,4096]{1,0:T(4,128)(2,1)S(1)} %collective-permute-done.19.refs_2_, bf16[4,4096]{1,0:T(4,128)(2,1)S(1)} %collective-permute-done.20.refs_3_), custom_call_target="tpu_custom_call" | custom-call | tf_op jit(solution)/shard_map/finish/pallas_call | solution.py:50
  (57 shorter events, 4.4 us)
Async XLA Ops:
  0.0 17.0 %slice-start.4 = ((s8[12582912]{0:T(1024)(128)(4,1)}), s8[4194304]{0:T(1024)(128)(4,1)S(1)}, s32[]{:S(2)}) async-start(s8[12582912]{0:T(1024)(128)(4,1)} %bitcast.4), calls=%async_computation.4 | async-start | bytes 8388608
  0.0 17.0 %slice-start.6 = ((s8[12582912]{0:T(1024)(128)(4,1)}), s8[4194304]{0:T(1024)(128)(4,1)S(1)}, s32[]{:S(2)}) async-start(s8[12582912]{0:T(1024)(128)(4,1)} %bitcast.6), calls=%async_computation.6 | async-start | bytes 8388608
  0.0 17.0 %slice-start.7 = ((s8[12582912]{0:T(1024)(128)(4,1)}), s8[4194304]{0:T(1024)(128)(4,1)S(1)}, s32[]{:S(2)}) async-start(s8[12582912]{0:T(1024)(128)(4,1)} %bitcast.6), calls=%async_computation.7 | async-start | bytes 8388608
  1.1 4.9 %collective-permute-start = (bf16[4,4224]{1,0:T(4,128)(2,1)S(1)}, bf16[4,4224]{1,0:T(4,128)(2,1)S(1)}, u32[]{:S(2)}, u32[]{:S(2)}) collective-permute-start(bf16[4,4224]{1,0:T(4,128)(2,1)S(1)} %prepare.1.refs_0_), channel_id=1, source_target_pairs={{0,2},{1,3},{2,0},{3,1},{4,6},{5,7},{6,4},{7,5},{8,10},{9,11},{10,... | collective-permute-start | bytes 101384 | tf_op jit(solution)/shard_map/ppermute | solution.py:314
  6.1 6.7 %collective-permute-start.1 = (bf16[8,4224]{1,0:T(8,128)(2,1)S(1)}, bf16[8,4224]{1,0:T(8,128)(2,1)S(1)}, u32[]{:S(2)}, u32[]{:S(2)}) collective-permute-start(bf16[8,4224]{1,0:T(8,128)(2,1)S(1)} %join.1.refs_0_), channel_id=1, source_target_pairs={{0,12},{4,8},{8,4},{12,0},{1,13},{5,9},{9,5},{13,1},{2,14},{6,10},... | collective-permute-start | bytes 202760 | tf_op jit(solution)/shard_map/ppermute | solution.py:314
  10.3 5.3 %collective-permute-start.2 = (bf16[8,4224]{1,0:T(8,128)(2,1)S(1)}, bf16[8,4224]{1,0:T(8,128)(2,1)S(1)}, u32[]{:S(2)}, u32[]{:S(2)}) collective-permute-start(bf16[8,4224]{1,0:T(8,128)(2,1)S(1)} %join.1.refs_0_), channel_id=1, source_target_pairs={{0,8},{4,12},{8,0},{12,4},{1,9},{5,13},{9,1},{13,5},{2,10},{6,14},... | collective-permute-start | bytes 202760 | tf_op jit(solution)/shard_map/ppermute | solution.py:314
  10.3 5.3 %collective-permute-start.3 = (bf16[8,4224]{1,0:T(8,128)(2,1)S(1)}, bf16[8,4224]{1,0:T(8,128)(2,1)S(1)}, u32[]{:S(2)}, u32[]{:S(2)}) collective-permute-start(bf16[8,4224]{1,0:T(8,128)(2,1)S(1)} %join.1.refs_0_), channel_id=1, source_target_pairs={{0,4},{4,0},{8,12},{12,8},{1,5},{5,1},{9,13},{13,9},{2,6},{6,2},{1... | collective-permute-start | bytes 202760 | tf_op jit(solution)/shard_map/ppermute | solution.py:314
  10.9 5.1 %collective-permute-start.4 = (bf16[8,4224]{1,0:T(8,128)(2,1)S(1)}, bf16[8,4224]{1,0:T(8,128)(2,1)S(1)}, u32[]{:S(2)}, u32[]{:S(2)}) collective-permute-start(bf16[8,4224]{1,0:T(8,128)(2,1)S(1)} %join.1.refs_0_), channel_id=1, source_target_pairs={{0,1},{1,0},{2,3},{3,2},{4,5},{5,4},{6,7},{7,6},{8,9},{9,8},{10,11... | collective-permute-start | bytes 202760 | tf_op jit(solution)/shard_map/ppermute | solution.py:314
  12.7 3.3 %collective-permute-start.5 = (bf16[8,4224]{1,0:T(8,128)(2,1)S(1)}, bf16[8,4224]{1,0:T(8,128)(2,1)S(1)}, u32[]{:S(2)}, u32[]{:S(2)}) collective-permute-start(bf16[8,4224]{1,0:T(8,128)(2,1)S(1)} %collective-permute-done.1.refs_1_), channel_id=1, source_target_pairs={{0,1},{1,0},{2,3},{3,2},{4,5},{5,4},{6,7},{7,6},{8,9},{9,8},{10,11... | collective-permute-start | bytes 202760 | tf_op jit(solution)/shard_map/ppermute | solution.py:314
  15.5 1.3 %collective-permute-start.6 = (bf16[8,4224]{1,0:T(8,128)(2,1)S(1)}, bf16[8,4224]{1,0:T(8,128)(2,1)S(1)}, u32[]{:S(2)}, u32[]{:S(2)}) collective-permute-start(bf16[8,4224]{1,0:T(8,128)(2,1)S(1)} %collective-permute-done.2.refs_2_), channel_id=1, source_target_pairs={{0,1},{1,0},{2,3},{3,2},{4,5},{5,4},{6,7},{7,6},{8,9},{9,8},{10,11... | collective-permute-start | bytes 202760 | tf_op jit(solution)/shard_map/ppermute | solution.py:314
  15.5 1.4 %collective-permute-start.7 = (bf16[8,4224]{1,0:T(8,128)(2,1)S(1)}, bf16[8,4224]{1,0:T(8,128)(2,1)S(1)}, u32[]{:S(2)}, u32[]{:S(2)}) collective-permute-start(bf16[8,4224]{1,0:T(8,128)(2,1)S(1)} %collective-permute-done.3.refs_3_), channel_id=1, source_target_pairs={{0,1},{1,0},{2,3},{3,2},{4,5},{5,4},{6,7},{7,6},{8,9},{9,8},{10,11... | collective-permute-start | bytes 202760 | tf_op jit(solution)/shard_map/ppermute | solution.py:314
  19.1 5.1 %collective-permute-start.11 = (bf16[2,64,384]{2,1,0:T(8,128)(2,1)S(1)}, bf16[2,64,384]{2,1,0:T(8,128)(2,1)S(1)}, u32[]{:S(2)}, u32[]{:S(2)}) collective-permute-start(bf16[2,64,384]{2,1,0:T(8,128)(2,1)S(1)} %up.3.refs_0_), channel_id=1, source_target_pairs={{0,2},{1,3},{2,0},{3,1},{4,6},{5,7},{6,4},{7,5},{8,10},{9,11},{10,... | collective-permute-start | bytes 294920 | tf_op jit(solution)/shard_map/ppermute | solution.py:314
  20.7 3.7 %collective-permute-start.9 = (bf16[2,64,384]{2,1,0:T(8,128)(2,1)S(1)}, bf16[2,64,384]{2,1,0:T(8,128)(2,1)S(1)}, u32[]{:S(2)}, u32[]{:S(2)}) collective-permute-start(bf16[2,64,384]{2,1,0:T(8,128)(2,1)S(1)} %up.3.refs_0_), channel_id=1, source_target_pairs={{0,1},{1,0},{2,3},{3,2},{4,5},{5,4},{6,7},{7,6},{8,9},{9,8},{10,11... | collective-permute-start | bytes 294920 | tf_op jit(solution)/shard_map/ppermute | solution.py:314
  23.0 1.4 %collective-permute-start.10 = (bf16[2,48,384]{2,1,0:T(8,128)(2,1)S(1)}, bf16[2,48,384]{2,1,0:T(8,128)(2,1)S(1)}, u32[]{:S(2)}, u32[]{:S(2)}) collective-permute-start(bf16[2,48,384]{2,1,0:T(8,128)(2,1)S(1)} %get-tuple-element.30), channel_id=1, source_target_pairs={{0,1},{1,0},{2,3},{3,2},{4,5},{5,4},{6,7},{7,6},{8,9},{9,8},{10,11... | collective-permute-start | bytes 221192 | tf_op jit(solution)/shard_map/ppermute | solution.py:314
  23.5 4.4 %collective-permute-start.8 = (bf16[2,48,384]{2,1,0:T(8,128)(2,1)S(1)}, bf16[2,48,384]{2,1,0:T(8,128)(2,1)S(1)}, u32[]{:S(2)}, u32[]{:S(2)}) collective-permute-start(bf16[2,48,384]{2,1,0:T(8,128)(2,1)S(1)} %get-tuple-element.30), channel_id=1, source_target_pairs={{0,2},{1,3},{2,0},{3,1},{4,6},{5,7},{6,4},{7,5},{8,10},{9,11},{10,... | collective-permute-start | bytes 221192 | tf_op jit(solution)/shard_map/ppermute | solution.py:314
  24.2 3.7 %collective-permute-start.13 = (bf16[2,64,384]{2,1,0:T(8,128)(2,1)S(1)}, bf16[2,64,384]{2,1,0:T(8,128)(2,1)S(1)}, u32[]{:S(2)}, u32[]{:S(2)}) collective-permute-start(bf16[2,64,384]{2,1,0:T(8,128)(2,1)S(1)} %collective-permute-done.11.refs_4_), channel_id=1, source_target_pairs={{0,1},{1,0},{2,3},{3,2},{4,5},{5,4},{6,7},{7,6},{8,9},{9,8},{10,11... | collective-permute-start | bytes 294920 | tf_op jit(solution)/shard_map/ppermute | solution.py:314
  27.9 1.3 %collective-permute-start.12 = (bf16[2,48,384]{2,1,0:T(8,128)(2,1)S(1)}, bf16[2,48,384]{2,1,0:T(8,128)(2,1)S(1)}, u32[]{:S(2)}, u32[]{:S(2)}) collective-permute-start(bf16[2,48,384]{2,1,0:T(8,128)(2,1)S(1)} %shard_map.109.refs_1_), channel_id=1, source_target_pairs={{0,1},{1,0},{2,3},{3,2},{4,5},{5,4},{6,7},{7,6},{8,9},{9,8},{10,11... | collective-permute-start | bytes 221192 | tf_op jit(solution)/shard_map/ppermute | solution.py:314
  29.9 1.5 %collective-permute-start.14 = (bf16[32,2048]{1,0:T(8,128)(2,1)S(1)}, bf16[32,2048]{1,0:T(8,128)(2,1)S(1)}, u32[]{:S(2)}, u32[]{:S(2)}) collective-permute-start(bf16[32,2048]{1,0:T(8,128)(2,1)S(1)} %get-tuple-element.39), channel_id=1, source_target_pairs={{0,1},{1,0},{2,3},{3,2},{4,5},{5,4},{6,7},{7,6},{8,9},{9,8},{10,11... | collective-permute-start | bytes 393224 | tf_op jit(solution)/shard_map/ppermute | solution.py:314
  31.0 1.4 %collective-permute-start.16 = (bf16[32,2048]{1,0:T(8,128)(2,1)S(1)}, bf16[32,2048]{1,0:T(8,128)(2,1)S(1)}, u32[]{:S(2)}, u32[]{:S(2)}) collective-permute-start(bf16[32,2048]{1,0:T(8,128)(2,1)S(1)} %get-tuple-element.44), channel_id=1, source_target_pairs={{0,1},{1,0},{2,3},{3,2},{4,5},{5,4},{6,7},{7,6},{8,9},{9,8},{10,11... | collective-permute-start | bytes 393224 | tf_op jit(solution)/shard_map/ppermute | solution.py:314
  31.5 5.0 %collective-permute-start.15 = (bf16[16,2048]{1,0:T(8,128)(2,1)S(1)}, bf16[16,2048]{1,0:T(8,128)(2,1)S(1)}, u32[]{:S(2)}, u32[]{:S(2)}) collective-permute-start(bf16[16,2048]{1,0:T(8,128)(2,1)S(1)} %get-tuple-element.41), channel_id=1, source_target_pairs={{0,2},{1,3},{2,0},{3,1},{4,6},{5,7},{6,4},{7,5},{8,10},{9,11},{10,... | collective-permute-start | bytes 196616 | tf_op jit(solution)/shard_map/ppermute | solution.py:314
  32.5 4.9 %collective-permute-start.17 = (bf16[16,2048]{1,0:T(8,128)(2,1)S(1)}, bf16[16,2048]{1,0:T(8,128)(2,1)S(1)}, u32[]{:S(2)}, u32[]{:S(2)}) collective-permute-start(bf16[16,2048]{1,0:T(8,128)(2,1)S(1)} %get-tuple-element.46), channel_id=1, source_target_pairs={{0,2},{1,3},{2,0},{3,1},{4,6},{5,7},{6,4},{7,5},{8,10},{9,11},{10,... | collective-permute-start | bytes 196616 | tf_op jit(solution)/shard_map/ppermute | solution.py:314
  37.4 5.8 %collective-permute-start.18 = (bf16[4,4096]{1,0:T(4,128)(2,1)S(1)}, bf16[4,4096]{1,0:T(4,128)(2,1)S(1)}, u32[]{:S(2)}, u32[]{:S(2)}) collective-permute-start(bf16[4,4096]{1,0:T(4,128)(2,1)S(1)} %get-tuple-element.48), channel_id=1, source_target_pairs={{0,12},{4,8},{8,4},{12,0},{1,13},{5,9},{9,5},{13,1},{2,14},{6,10},... | collective-permute-start | bytes 98312 | tf_op jit(solution)/shard_map/ppermute | solution.py:314
  39.6 5.0 %collective-permute-start.19 = (bf16[4,4096]{1,0:T(4,128)(2,1)S(1)}, bf16[4,4096]{1,0:T(4,128)(2,1)S(1)}, u32[]{:S(2)}, u32[]{:S(2)}) collective-permute-start(bf16[4,4096]{1,0:T(4,128)(2,1)S(1)} %get-tuple-element.49), channel_id=1, source_target_pairs={{0,8},{4,12},{8,0},{12,4},{1,9},{5,13},{9,1},{13,5},{2,10},{6,14},... | collective-permute-start | bytes 98312 | tf_op jit(solution)/shard_map/ppermute | solution.py:314
  39.6 5.0 %collective-permute-start.20 = (bf16[4,4096]{1,0:T(4,128)(2,1)S(1)}, bf16[4,4096]{1,0:T(4,128)(2,1)S(1)}, u32[]{:S(2)}, u32[]{:S(2)}) collective-permute-start(bf16[4,4096]{1,0:T(4,128)(2,1)S(1)} %get-tuple-element.50), channel_id=1, source_target_pairs={{0,4},{4,0},{8,12},{12,8},{1,5},{5,1},{9,13},{13,9},{2,6},{6,2},{1... | collective-permute-start | bytes 98312 | tf_op jit(solution)/shard_map/ppermute | solution.py:314
  (8 other events, 79.0 us)

commit v8 on v7

--- a/solution.py
+++ b/solution.py
@@ -339,7 +339,7 @@
             room=(2 << 20) + 4 * block * wide,
         )
     along_z = {k: over(lead, "expert", k) if k else lead for k in range(n_z)}
-    places = [0, *range(n_z - 1, 0, -1)]
+    places = [0, *range(2, n_z), 1]
     places += [k + n_z for k in places]
     gathered = [along_z[k] for k in places[:n_z]]
     gathered += [over(a, "dp", 1) for a in gathered]
@@ -446,7 +446,7 @@
         arrived,
         room=(2 << 20) + 6 * size_of(arrived[0]),
     )
-    back = [over(kept[k], "expert", k) for k in range(n_z - 1, 0, -1)]
+    back = [over(kept[k], "expert", k) for k in [n_z - 1, *range(1, n_z - 1)]]
     with jax.named_scope("finish"):
         return call(
             functools.partial(finish, cols),

time: 45.4 us -> 45.4 us (level)
  transfers between devices with their start and end apart: 21 -> 21, of which waited for: 14 -> 16; matrix products, arithmetic and copies ran while one was open for 0% -> 0% of each run, Pallas kernels for 14% -> 14%
where the time goes in v8:
time: 45.4 us; the launch traced here: 45.2 us
  starting transfers between devices  17.8 us (39%)
  waiting for transfers between devices  16.3 us (36%)
  Pallas kernels  10.8 us (24%)
    ppermute x21, starting transfers between devices, over(): lax.ppermute(x, axis, [(i, i ^ m) for i in range(lax.axis_size(axis))])  17.8 us
    ppermute x21, waiting for transfers between devices, over(): lax.ppermute(x, axis, [(i, i ^ m) for i in range(lax.axis_size(axis))])  16.3 us
    pallas_call x14, Pallas kernels, call(): pl.pallas_call(body, out_shape=out_shape, in_specs=specs, out_specs=jax.t...  10.8 us
  transfers between devices with their start and end apart: 21, of which 16 were waited for; matrix products, arithmetic and copies ran while one was open for 0% of the time, Pallas kernels for 14%

profile of v8, /device:TPU:0, one launch (start us, length us, event | category | flops | bytes accessed | tf_op | source)
XLA Modules:
  0.0 45.2 jit_solution(8509010893813332365)
XLA Ops:
  0.0 1.1 %prepare.1.refs_0_ = bf16[4,4224]{1,0:T(4,128)(2,1)S(1)} custom-call(s32[4]{0:T(128)} %refs_0_.1, bf16[4,4096]{1,0:T(4,128)(2,1)} %refs_1_.1, s32[4,8]{1,0:T(4,128)} %refs_2_.6, f32[4,8]{1,0:T(4,128)} %refs_3_.5, s32[8,16]{1,0:T(8,128)} %refs_4_.2, s32[8,16]{1,0:T(8,128)} %refs_5_.1, bf16[4,4096,384]{2,1,0:T(8,128)(2,1)} %refs_2_.9, ...), custom_call_target="tpu_custom_call" | custom-call | tf_op jit(solution)/shard_map/prepare/pallas_call | solution.py:50
  1.1 3.0 %collective-permute-start = (bf16[4,4224]{1,0:T(4,128)(2,1)S(1)}, bf16[4,4224]{1,0:T(4,128)(2,1)S(1)}, u32[]{:S(2)}, u32[]{:S(2)}) collective-permute-start(bf16[4,4224]{1,0:T(4,128)(2,1)S(1)} %prepare.1.refs_0_), channel_id=1, source_target_pairs={{0,2},{1,3},{2,0},{3,1},{4,6},{5,7},{6,4},{7,5},{8,10},{9,11},{10,... | collective-permute-start | bytes 101384 | tf_op jit(solution)/shard_map/ppermute | solution.py:314
  4.1 1.9 %collective-permute-done.refs_1_ = bf16[4,4224]{1,0:T(4,128)(2,1)S(1)} collective-permute-done((bf16[4,4224]{1,0:T(4,128)(2,1)S(1)}, bf16[4,4224]{1,0:T(4,128)(2,1)S(1)}, u32[]{:S(2)}, u32[]{:S(2)}) %collective-permute-start) | collective-permute-done | bytes 33824 | tf_op jit(solution)/shard_map/ppermute | solution.py:314
  6.1 3.2 %collective-permute-start.1 = (bf16[8,4224]{1,0:T(8,128)(2,1)S(1)}, bf16[8,4224]{1,0:T(8,128)(2,1)S(1)}, u32[]{:S(2)}, u32[]{:S(2)}) collective-permute-start(bf16[8,4224]{1,0:T(8,128)(2,1)S(1)} %join.1.refs_0_), channel_id=1, source_target_pairs={{0,8},{4,12},{8,0},{12,4},{1,9},{5,13},{9,1},{13,5},{2,10},{6,14},... | collective-permute-start | bytes 202760 | tf_op jit(solution)/shard_map/ppermute | solution.py:314
  9.2 1.3 %collective-permute-start.2 = (bf16[8,4224]{1,0:T(8,128)(2,1)S(1)}, bf16[8,4224]{1,0:T(8,128)(2,1)S(1)}, u32[]{:S(2)}, u32[]{:S(2)}) collective-permute-start(bf16[8,4224]{1,0:T(8,128)(2,1)S(1)} %join.1.refs_0_), channel_id=1, source_target_pairs={{0,12},{4,8},{8,4},{12,0},{1,13},{5,9},{9,5},{13,1},{2,14},{6,10},... | collective-permute-start | bytes 202760 | tf_op jit(solution)/shard_map/ppermute | solution.py:314
  10.8 1.0 %collective-permute-done.1.refs_1_ = bf16[8,4224]{1,0:T(8,128)(2,1)S(1)} collective-permute-done((bf16[8,4224]{1,0:T(8,128)(2,1)S(1)}, bf16[8,4224]{1,0:T(8,128)(2,1)S(1)}, u32[]{:S(2)}, u32[]{:S(2)}) %collective-permute-start.1) | collective-permute-done | bytes 67616 | tf_op jit(solution)/shard_map/ppermute | solution.py:314
  11.9 3.6 %collective-permute-done.2.refs_2_ = bf16[8,4224]{1,0:T(8,128)(2,1)S(1)} collective-permute-done((bf16[8,4224]{1,0:T(8,128)(2,1)S(1)}, bf16[8,4224]{1,0:T(8,128)(2,1)S(1)}, u32[]{:S(2)}, u32[]{:S(2)}) %collective-permute-start.2) | collective-permute-done | bytes 67616 | tf_op jit(solution)/shard_map/ppermute | solution.py:314
  16.0 0.7 %collective-permute-done.6.refs_6_ = bf16[8,4224]{1,0:T(8,128)(2,1)S(1)} collective-permute-done((bf16[8,4224]{1,0:T(8,128)(2,1)S(1)}, bf16[8,4224]{1,0:T(8,128)(2,1)S(1)}, u32[]{:S(2)}, u32[]{:S(2)}) %collective-permute-start.6) | collective-permute-done | bytes 67616 | tf_op jit(solution)/shard_map/ppermute | solution.py:314
  17.0 2.0 %up.3.refs_0_ = bf16[2,64,384]{2,1,0:T(8,128)(2,1)S(1)} custom-call(bf16[64,4096]{1,0:T(8,128)(2,1)S(1)} %get-tuple-element.28.refs_0_, bf16[64,128]{1,0:T(8,128)(2,1)S(1)} %get-tuple-element.29.refs_1_.refs_5_.refs_2_, bf16[4,4096,384]{2,1,0:T(8,128)(2,1)S(1)} %bitcast.5, bf16[4,4096,384]{2,1,0:T(8,128)(2,1)S(1)} %bitcast.7), custom_call_target="tpu_custom_call" | custom-call | tf_op jit(solution)/shard_map/up/pallas_call | solution.py:50
  19.0 1.6 %collective-permute-start.11 = (bf16[2,64,384]{2,1,0:T(8,128)(2,1)S(1)}, bf16[2,64,384]{2,1,0:T(8,128)(2,1)S(1)}, u32[]{:S(2)}, u32[]{:S(2)}) collective-permute-start(bf16[2,64,384]{2,1,0:T(8,128)(2,1)S(1)} %up.3.refs_0_), channel_id=1, source_target_pairs={{0,2},{1,3},{2,0},{3,1},{4,6},{5,7},{6,4},{7,5},{8,10},{9,11},{10,... | collective-permute-start | bytes 294920 | tf_op jit(solution)/shard_map/ppermute | solution.py:314
  20.7 2.2 %up.2 = (bf16[2,64,384]{2,1,0:T(8,128)(2,1)S(1)}, bf16[2,48,384]{2,1,0:T(8,128)(2,1)S(1)}) custom-call(bf16[64,4096]{1,0:T(8,128)(2,1)S(1)} %get-tuple-element.28.refs_0_, bf16[64,128]{1,0:T(8,128)(2,1)S(1)} %get-tuple-element.29.refs_1_.refs_5_.refs_2_, bf16[4,4096,384]{2,1,0:T(8,128)(2,1)S(1)} %bitcast.5, bf16[4,4096,384]{2,1,0:T(8,128)(2,1)S(1)} %bitcast.7), custom_call_target="tpu_custom_call" | custom-call | tf_op jit(solution)/shard_map/up/pallas_call | solution.py:50
  24.4 2.2 %down.4 = (f32[64,1024]{1,0:T(8,128)S(1)}, f32[64,128]{1,0:T(8,128)S(1)}, f32[64,128]{1,0:T(8,128)S(1)}, bf16[8,64,48]{2,1,0:T(8,128)(2,1)S(1)}) custom-call(bf16[2,64,384]{2,1,0:T(8,128)(2,1)S(1)} %up.3.refs_0_, bf16[2,64,384]{2,1,0:T(8,128)(2,1)S(1)} %collective-permute-done.9.refs_1_, bf16[2,64,384]{2,1,0:T(8,128)(2,1)S(1)} %get-tuple-element.31.refs_2_, ...), custom_call_target="tpu_custom_call" | custom-call | tf_op jit(solution)/shard_map/down/pallas_call | solution.py:50
  26.6 1.2 %collective-permute-done.8.x = bf16[2,48,384]{2,1,0:T(8,128)(2,1)S(1)} collective-permute-done((bf16[2,48,384]{2,1,0:T(8,128)(2,1)S(1)}, bf16[2,48,384]{2,1,0:T(8,128)(2,1)S(1)}, u32[]{:S(2)}, u32[]{:S(2)}) %collective-permute-start.8) | collective-permute-done | bytes 73760 | tf_op jit(solution)/shard_map/ppermute | solution.py:314
  27.9 1.2 %down.5 = (f32[64,1024]{1,0:T(8,128)S(1)}, f32[64,128]{1,0:T(8,128)S(1)}) custom-call(bf16[2,64,384]{2,1,0:T(8,128)(2,1)S(1)} %collective-permute-done.13.refs_0_, bf16[2,48,384]{2,1,0:T(8,128)(2,1)S(1)} %shard_map.109.refs_1_, bf16[64,128]{1,0:T(8,128)(2,1)S(1)} %get-tuple-element.29.refs_1_.refs_5_.refs_2_, bf16[4,1536,1024]{2,1,0:T(8,128)(2,1)S(1)} %bitcast.3, ...), custom_call_target="tpu_custom_call" | custom-call | tf_op jit(solution)/shard_map/down/pallas_call | solution.py:50
  29.2 0.7 %down.6 = (f32[32,2048]{1,0:T(8,128)S(1)}, bf16[32,2048]{1,0:T(8,128)(2,1)S(1)}, bf16[64,128]{1,0:T(8,128)(2,1)S(1)}) custom-call(bf16[2,48,384]{2,1,0:T(8,128)(2,1)S(1)} %collective-permute-done.12.refs_0_, bf16[64,128]{1,0:T(8,128)(2,1)S(1)} %get-tuple-element.29.refs_1_.refs_5_.refs_2_, bf16[4,1536,1024]{2,1,0:T(8,128)(2,1)S(1)} %bitcast.3, ...), custom_call_target="tpu_custom_call" | custom-call | tf_op jit(solution)/shard_map/down/pallas_call | solution.py:50
  31.5 0.6 %collective-permute-start.15 = (bf16[16,2048]{1,0:T(8,128)(2,1)S(1)}, bf16[16,2048]{1,0:T(8,128)(2,1)S(1)}, u32[]{:S(2)}, u32[]{:S(2)}) collective-permute-start(bf16[16,2048]{1,0:T(8,128)(2,1)S(1)} %get-tuple-element.41), channel_id=1, source_target_pairs={{0,2},{1,3},{2,0},{3,1},{4,6},{5,7},{6,4},{7,5},{8,10},{9,11},{10,... | collective-permute-start | bytes 196616 | tf_op jit(solution)/shard_map/ppermute | solution.py:314
  32.5 1.2 %collective-permute-start.17 = (bf16[16,2048]{1,0:T(8,128)(2,1)S(1)}, bf16[16,2048]{1,0:T(8,128)(2,1)S(1)}, u32[]{:S(2)}, u32[]{:S(2)}) collective-permute-start(bf16[16,2048]{1,0:T(8,128)(2,1)S(1)} %get-tuple-element.46), channel_id=1, source_target_pairs={{0,2},{1,3},{2,0},{3,1},{4,6},{5,7},{6,4},{7,5},{8,10},{9,11},{10,... | collective-permute-start | bytes 196616 | tf_op jit(solution)/shard_map/ppermute | solution.py:314
  33.7 2.8 %collective-permute-done.15.refs_1_ = bf16[16,2048]{1,0:T(8,128)(2,1)S(1)} collective-permute-done((bf16[16,2048]{1,0:T(8,128)(2,1)S(1)}, bf16[16,2048]{1,0:T(8,128)(2,1)S(1)}, u32[]{:S(2)}, u32[]{:S(2)}) %collective-permute-start.15) | collective-permute-done | bytes 65568 | tf_op jit(solution)/shard_map/ppermute | solution.py:314
  36.5 0.8 %collective-permute-done.17.refs_3_ = bf16[16,2048]{1,0:T(8,128)(2,1)S(1)} collective-permute-done((bf16[16,2048]{1,0:T(8,128)(2,1)S(1)}, bf16[16,2048]{1,0:T(8,128)(2,1)S(1)}, u32[]{:S(2)}, u32[]{:S(2)}) %collective-permute-start.17) | collective-permute-done | bytes 65568 | tf_op jit(solution)/shard_map/ppermute | solution.py:314
  37.4 2.4 %collective-permute-start.18 = (bf16[4,4096]{1,0:T(4,128)(2,1)S(1)}, bf16[4,4096]{1,0:T(4,128)(2,1)S(1)}, u32[]{:S(2)}, u32[]{:S(2)}) collective-permute-start(bf16[4,4096]{1,0:T(4,128)(2,1)S(1)} %get-tuple-element.48), channel_id=1, source_target_pairs={{0,12},{4,8},{8,4},{12,0},{1,13},{5,9},{9,5},{13,1},{2,14},{6,10},... | collective-permute-start | bytes 98312 | tf_op jit(solution)/shard_map/ppermute | solution.py:314
  39.7 2.1 %collective-permute-start.20 = (bf16[4,4096]{1,0:T(4,128)(2,1)S(1)}, bf16[4,4096]{1,0:T(4,128)(2,1)S(1)}, u32[]{:S(2)}, u32[]{:S(2)}) collective-permute-start(bf16[4,4096]{1,0:T(4,128)(2,1)S(1)} %get-tuple-element.50), channel_id=1, source_target_pairs={{0,8},{4,12},{8,0},{12,4},{1,9},{5,13},{9,1},{13,5},{2,10},{6,14},... | collective-permute-start | bytes 98312 | tf_op jit(solution)/shard_map/ppermute | solution.py:314
  41.8 1.4 %collective-permute-done.18.refs_1_ = bf16[4,4096]{1,0:T(4,128)(2,1)S(1)} collective-permute-done((bf16[4,4096]{1,0:T(4,128)(2,1)S(1)}, bf16[4,4096]{1,0:T(4,128)(2,1)S(1)}, u32[]{:S(2)}, u32[]{:S(2)}) %collective-permute-start.18) | collective-permute-done | bytes 32800 | tf_op jit(solution)/shard_map/ppermute | solution.py:314
  43.6 0.9 %collective-permute-done.20.refs_3_ = bf16[4,4096]{1,0:T(4,128)(2,1)S(1)} collective-permute-done((bf16[4,4096]{1,0:T(4,128)(2,1)S(1)}, bf16[4,4096]{1,0:T(4,128)(2,1)S(1)}, u32[]{:S(2)}, u32[]{:S(2)}) %collective-permute-start.20) | collective-permute-done | bytes 32800 | tf_op jit(solution)/shard_map/ppermute | solution.py:314
  44.5 0.6 %finish.1 = bf16[4,4096]{1,0:T(4,128)(2,1)} custom-call(f32[4,4096]{1,0:T(4,128)S(1)} %get-tuple-element.47.refs_0_, bf16[4,4096]{1,0:T(4,128)(2,1)S(1)} %collective-permute-done.18.refs_1_, bf16[4,4096]{1,0:T(4,128)(2,1)S(1)} %collective-permute-done.19.refs_2_, bf16[4,4096]{1,0:T(4,128)(2,1)S(1)} %collective-permute-done.20.refs_3_), custom_call_target="tpu_custom_call" | custom-call | tf_op jit(solution)/shard_map/finish/pallas_call | solution.py:50
  (57 shorter events, 5.1 us)
Async XLA Ops:
  0.0 16.9 %slice-start.4 = ((s8[12582912]{0:T(1024)(128)(4,1)}), s8[4194304]{0:T(1024)(128)(4,1)S(1)}, s32[]{:S(2)}) async-start(s8[12582912]{0:T(1024)(128)(4,1)} %bitcast.4), calls=%async_computation.4 | async-start | bytes 8388608
  0.0 16.9 %slice-start.6 = ((s8[12582912]{0:T(1024)(128)(4,1)}), s8[4194304]{0:T(1024)(128)(4,1)S(1)}, s32[]{:S(2)}) async-start(s8[12582912]{0:T(1024)(128)(4,1)} %bitcast.6), calls=%async_computation.6 | async-start | bytes 8388608
  0.0 16.9 %slice-start.7 = ((s8[12582912]{0:T(1024)(128)(4,1)}), s8[4194304]{0:T(1024)(128)(4,1)S(1)}, s32[]{:S(2)}) async-start(s8[12582912]{0:T(1024)(128)(4,1)} %bitcast.6), calls=%async_computation.7 | async-start | bytes 8388608
  1.1 4.9 %collective-permute-start = (bf16[4,4224]{1,0:T(4,128)(2,1)S(1)}, bf16[4,4224]{1,0:T(4,128)(2,1)S(1)}, u32[]{:S(2)}, u32[]{:S(2)}) collective-permute-start(bf16[4,4224]{1,0:T(4,128)(2,1)S(1)} %prepare.1.refs_0_), channel_id=1, source_target_pairs={{0,2},{1,3},{2,0},{3,1},{4,6},{5,7},{6,4},{7,5},{8,10},{9,11},{10,... | collective-permute-start | bytes 101384 | tf_op jit(solution)/shard_map/ppermute | solution.py:314
  6.1 5.8 %collective-permute-start.1 = (bf16[8,4224]{1,0:T(8,128)(2,1)S(1)}, bf16[8,4224]{1,0:T(8,128)(2,1)S(1)}, u32[]{:S(2)}, u32[]{:S(2)}) collective-permute-start(bf16[8,4224]{1,0:T(8,128)(2,1)S(1)} %join.1.refs_0_), channel_id=1, source_target_pairs={{0,8},{4,12},{8,0},{12,4},{1,9},{5,13},{9,1},{13,5},{2,10},{6,14},... | collective-permute-start | bytes 202760 | tf_op jit(solution)/shard_map/ppermute | solution.py:314
  9.2 6.2 %collective-permute-start.2 = (bf16[8,4224]{1,0:T(8,128)(2,1)S(1)}, bf16[8,4224]{1,0:T(8,128)(2,1)S(1)}, u32[]{:S(2)}, u32[]{:S(2)}) collective-permute-start(bf16[8,4224]{1,0:T(8,128)(2,1)S(1)} %join.1.refs_0_), channel_id=1, source_target_pairs={{0,12},{4,8},{8,4},{12,0},{1,13},{5,9},{9,5},{13,1},{2,14},{6,10},... | collective-permute-start | bytes 202760 | tf_op jit(solution)/shard_map/ppermute | solution.py:314
  10.6 5.0 %collective-permute-start.3 = (bf16[8,4224]{1,0:T(8,128)(2,1)S(1)}, bf16[8,4224]{1,0:T(8,128)(2,1)S(1)}, u32[]{:S(2)}, u32[]{:S(2)}) collective-permute-start(bf16[8,4224]{1,0:T(8,128)(2,1)S(1)} %join.1.refs_0_), channel_id=1, source_target_pairs={{0,4},{4,0},{8,12},{12,8},{1,5},{5,1},{9,13},{13,9},{2,6},{6,2},{1... | collective-permute-start | bytes 202760 | tf_op jit(solution)/shard_map/ppermute | solution.py:314
  10.8 5.1 %collective-permute-start.4 = (bf16[8,4224]{1,0:T(8,128)(2,1)S(1)}, bf16[8,4224]{1,0:T(8,128)(2,1)S(1)}, u32[]{:S(2)}, u32[]{:S(2)}) collective-permute-start(bf16[8,4224]{1,0:T(8,128)(2,1)S(1)} %join.1.refs_0_), channel_id=1, source_target_pairs={{0,1},{1,0},{2,3},{3,2},{4,5},{5,4},{6,7},{7,6},{8,9},{9,8},{10,11... | collective-permute-start | bytes 202760 | tf_op jit(solution)/shard_map/ppermute | solution.py:314
  11.8 4.1 %collective-permute-start.5 = (bf16[8,4224]{1,0:T(8,128)(2,1)S(1)}, bf16[8,4224]{1,0:T(8,128)(2,1)S(1)}, u32[]{:S(2)}, u32[]{:S(2)}) collective-permute-start(bf16[8,4224]{1,0:T(8,128)(2,1)S(1)} %collective-permute-done.1.refs_1_), channel_id=1, source_target_pairs={{0,1},{1,0},{2,3},{3,2},{4,5},{5,4},{6,7},{7,6},{8,9},{9,8},{10,11... | collective-permute-start | bytes 202760 | tf_op jit(solution)/shard_map/ppermute | solution.py:314
  15.4 1.3 %collective-permute-start.6 = (bf16[8,4224]{1,0:T(8,128)(2,1)S(1)}, bf16[8,4224]{1,0:T(8,128)(2,1)S(1)}, u32[]{:S(2)}, u32[]{:S(2)}) collective-permute-start(bf16[8,4224]{1,0:T(8,128)(2,1)S(1)} %collective-permute-done.2.refs_2_), channel_id=1, source_target_pairs={{0,1},{1,0},{2,3},{3,2},{4,5},{5,4},{6,7},{7,6},{8,9},{9,8},{10,11... | collective-permute-start | bytes 202760 | tf_op jit(solution)/shard_map/ppermute | solution.py:314
  15.6 1.3 %collective-permute-start.7 = (bf16[8,4224]{1,0:T(8,128)(2,1)S(1)}, bf16[8,4224]{1,0:T(8,128)(2,1)S(1)}, u32[]{:S(2)}, u32[]{:S(2)}) collective-permute-start(bf16[8,4224]{1,0:T(8,128)(2,1)S(1)} %collective-permute-done.3.refs_3_), channel_id=1, source_target_pairs={{0,1},{1,0},{2,3},{3,2},{4,5},{5,4},{6,7},{7,6},{8,9},{9,8},{10,11... | collective-permute-start | bytes 202760 | tf_op jit(solution)/shard_map/ppermute | solution.py:314
  19.0 5.1 %collective-permute-start.11 = (bf16[2,64,384]{2,1,0:T(8,128)(2,1)S(1)}, bf16[2,64,384]{2,1,0:T(8,128)(2,1)S(1)}, u32[]{:S(2)}, u32[]{:S(2)}) collective-permute-start(bf16[2,64,384]{2,1,0:T(8,128)(2,1)S(1)} %up.3.refs_0_), channel_id=1, source_target_pairs={{0,2},{1,3},{2,0},{3,1},{4,6},{5,7},{6,4},{7,5},{8,10},{9,11},{10,... | collective-permute-start | bytes 294920 | tf_op jit(solution)/shard_map/ppermute | solution.py:314
  20.6 3.7 %collective-permute-start.9 = (bf16[2,64,384]{2,1,0:T(8,128)(2,1)S(1)}, bf16[2,64,384]{2,1,0:T(8,128)(2,1)S(1)}, u32[]{:S(2)}, u32[]{:S(2)}) collective-permute-start(bf16[2,64,384]{2,1,0:T(8,128)(2,1)S(1)} %up.3.refs_0_), channel_id=1, source_target_pairs={{0,1},{1,0},{2,3},{3,2},{4,5},{5,4},{6,7},{7,6},{8,9},{9,8},{10,11... | collective-permute-start | bytes 294920 | tf_op jit(solution)/shard_map/ppermute | solution.py:314
  23.0 1.4 %collective-permute-start.10 = (bf16[2,48,384]{2,1,0:T(8,128)(2,1)S(1)}, bf16[2,48,384]{2,1,0:T(8,128)(2,1)S(1)}, u32[]{:S(2)}, u32[]{:S(2)}) collective-permute-start(bf16[2,48,384]{2,1,0:T(8,128)(2,1)S(1)} %get-tuple-element.30), channel_id=1, source_target_pairs={{0,1},{1,0},{2,3},{3,2},{4,5},{5,4},{6,7},{7,6},{8,9},{9,8},{10,11... | collective-permute-start | bytes 221192 | tf_op jit(solution)/shard_map/ppermute | solution.py:314
  23.5 4.4 %collective-permute-start.8 = (bf16[2,48,384]{2,1,0:T(8,128)(2,1)S(1)}, bf16[2,48,384]{2,1,0:T(8,128)(2,1)S(1)}, u32[]{:S(2)}, u32[]{:S(2)}) collective-permute-start(bf16[2,48,384]{2,1,0:T(8,128)(2,1)S(1)} %get-tuple-element.30), channel_id=1, source_target_pairs={{0,2},{1,3},{2,0},{3,1},{4,6},{5,7},{6,4},{7,5},{8,10},{9,11},{10,... | collective-permute-start | bytes 221192 | tf_op jit(solution)/shard_map/ppermute | solution.py:314
  24.2 3.8 %collective-permute-start.13 = (bf16[2,64,384]{2,1,0:T(8,128)(2,1)S(1)}, bf16[2,64,384]{2,1,0:T(8,128)(2,1)S(1)}, u32[]{:S(2)}, u32[]{:S(2)}) collective-permute-start(bf16[2,64,384]{2,1,0:T(8,128)(2,1)S(1)} %collective-permute-done.11.refs_4_), channel_id=1, source_target_pairs={{0,1},{1,0},{2,3},{3,2},{4,5},{5,4},{6,7},{7,6},{8,9},{9,8},{10,11... | collective-permute-start | bytes 294920 | tf_op jit(solution)/shard_map/ppermute | solution.py:314
  27.8 1.3 %collective-permute-start.12 = (bf16[2,48,384]{2,1,0:T(8,128)(2,1)S(1)}, bf16[2,48,384]{2,1,0:T(8,128)(2,1)S(1)}, u32[]{:S(2)}, u32[]{:S(2)}) collective-permute-start(bf16[2,48,384]{2,1,0:T(8,128)(2,1)S(1)} %shard_map.109.refs_1_), channel_id=1, source_target_pairs={{0,1},{1,0},{2,3},{3,2},{4,5},{5,4},{6,7},{7,6},{8,9},{9,8},{10,11... | collective-permute-start | bytes 221192 | tf_op jit(solution)/shard_map/ppermute | solution.py:314
  29.9 1.5 %collective-permute-start.14 = (bf16[32,2048]{1,0:T(8,128)(2,1)S(1)}, bf16[32,2048]{1,0:T(8,128)(2,1)S(1)}, u32[]{:S(2)}, u32[]{:S(2)}) collective-permute-start(bf16[32,2048]{1,0:T(8,128)(2,1)S(1)} %get-tuple-element.39), channel_id=1, source_target_pairs={{0,1},{1,0},{2,3},{3,2},{4,5},{5,4},{6,7},{7,6},{8,9},{9,8},{10,11... | collective-permute-start | bytes 393224 | tf_op jit(solution)/shard_map/ppermute | solution.py:314
  31.0 1.4 %collective-permute-start.16 = (bf16[32,2048]{1,0:T(8,128)(2,1)S(1)}, bf16[32,2048]{1,0:T(8,128)(2,1)S(1)}, u32[]{:S(2)}, u32[]{:S(2)}) collective-permute-start(bf16[32,2048]{1,0:T(8,128)(2,1)S(1)} %get-tuple-element.44), channel_id=1, source_target_pairs={{0,1},{1,0},{2,3},{3,2},{4,5},{5,4},{6,7},{7,6},{8,9},{9,8},{10,11... | collective-permute-start | bytes 393224 | tf_op jit(solution)/shard_map/ppermute | solution.py:314
  31.5 5.0 %collective-permute-start.15 = (bf16[16,2048]{1,0:T(8,128)(2,1)S(1)}, bf16[16,2048]{1,0:T(8,128)(2,1)S(1)}, u32[]{:S(2)}, u32[]{:S(2)}) collective-permute-start(bf16[16,2048]{1,0:T(8,128)(2,1)S(1)} %get-tuple-element.41), channel_id=1, source_target_pairs={{0,2},{1,3},{2,0},{3,1},{4,6},{5,7},{6,4},{7,5},{8,10},{9,11},{10,... | collective-permute-start | bytes 196616 | tf_op jit(solution)/shard_map/ppermute | solution.py:314
  32.5 4.9 %collective-permute-start.17 = (bf16[16,2048]{1,0:T(8,128)(2,1)S(1)}, bf16[16,2048]{1,0:T(8,128)(2,1)S(1)}, u32[]{:S(2)}, u32[]{:S(2)}) collective-permute-start(bf16[16,2048]{1,0:T(8,128)(2,1)S(1)} %get-tuple-element.46), channel_id=1, source_target_pairs={{0,2},{1,3},{2,0},{3,1},{4,6},{5,7},{6,4},{7,5},{8,10},{9,11},{10,... | collective-permute-start | bytes 196616 | tf_op jit(solution)/shard_map/ppermute | solution.py:314
  37.4 5.8 %collective-permute-start.18 = (bf16[4,4096]{1,0:T(4,128)(2,1)S(1)}, bf16[4,4096]{1,0:T(4,128)(2,1)S(1)}, u32[]{:S(2)}, u32[]{:S(2)}) collective-permute-start(bf16[4,4096]{1,0:T(4,128)(2,1)S(1)} %get-tuple-element.48), channel_id=1, source_target_pairs={{0,12},{4,8},{8,4},{12,0},{1,13},{5,9},{9,5},{13,1},{2,14},{6,10},... | collective-permute-start | bytes 98312 | tf_op jit(solution)/shard_map/ppermute | solution.py:314
  39.7 3.9 %collective-permute-start.19 = (bf16[4,4096]{1,0:T(4,128)(2,1)S(1)}, bf16[4,4096]{1,0:T(4,128)(2,1)S(1)}, u32[]{:S(2)}, u32[]{:S(2)}) collective-permute-start(bf16[4,4096]{1,0:T(4,128)(2,1)S(1)} %get-tuple-element.49), channel_id=1, source_target_pairs={{0,4},{4,0},{8,12},{12,8},{1,5},{5,1},{9,13},{13,9},{2,6},{6,2},{1... | collective-permute-start | bytes 98312 | tf_op jit(solution)/shard_map/ppermute | solution.py:314
  39.7 4.8 %collective-permute-start.20 = (bf16[4,4096]{1,0:T(4,128)(2,1)S(1)}, bf16[4,4096]{1,0:T(4,128)(2,1)S(1)}, u32[]{:S(2)}, u32[]{:S(2)}) collective-permute-start(bf16[4,4096]{1,0:T(4,128)(2,1)S(1)} %get-tuple-element.50), channel_id=1, source_target_pairs={{0,8},{4,12},{8,0},{12,4},{1,9},{5,13},{9,1},{13,5},{2,10},{6,14},... | collective-permute-start | bytes 98312 | tf_op jit(solution)/shard_map/ppermute | solution.py:314
  (8 other events, 78.9 us)
